TPU v7x, 256 devices: a whole 4x4x8 slice. The times are simulated.
256 devices in a mesh: ctx: 32 (over z, y_hi, core), tp: 8 (over y_lo, x).
Axes of the slice: x: 4, y: 4 (y_hi: 2, y_lo: 2; y = y_hi * 2 + y_lo), z: 8, core: 2. Of those that a mesh axis runs over, the one named last changes fastest.
Arguments:
- queries: bfloat16 [8192, 4096], P('ctx', 'tp'), may hold values from -44 to 44
- keys: bfloat16 [8192, 1024], P('ctx', 'tp'), may hold values from -24 to 24
- values: bfloat16 [8192, 1024], P('ctx', 'tp'), may hold values from -6 to 6
- grad_out: bfloat16 [8192, 4096], P('ctx', 'tp'), may hold values from -6 to 6
- doc_lengths: int32 [17], replicated, may hold values from 1 to 4352, as said below
Outputs:
- grad_queries: bfloat16 [8192, 4096], P(('ctx', 'tp'))
- grad_keys: bfloat16 [8192, 1024], P(('ctx', 'tp'))
- grad_values: bfloat16 [8192, 1024], P(('ctx', 'tp'))
Inputs may be any that keep to these rules, and one draw needn't show every extreme that they name: `doc_lengths`: 17 documents fill the 8192 positions; the longest has exactly 4352 tokens.
All inputs are finite; a program needn't handle non-finite values.
Results may differ from a plain program's by a relative error of at most 0.008.
Values may be sent and summed in bfloat16 or wider, within the bound.
No kernel may reach another device: no remote copies, remote signals or barrier semaphores. Data moves between devices by JAX's collectives and lax.ppermute only.
A program may use at most 64 MiB of HBM per device.

v0:
```python
import math

import jax
import jax.numpy as jnp
from jax import lax
from jax.experimental import pallas as pl
from jax.experimental.pallas import tpu as pltpu
from jax.sharding import Mesh, PartitionSpec as P

HD = 128
GROUP = 4
ROWS = 256
SLAB = 4
REACH = 5
HALF = 3
HERE = (0, 2)
THERE = (2, 4)
DOC_COUNT = 17
SCALE = HD ** -0.5
SCALE2 = SCALE * math.log2(math.e)
MASKED = -1e30
EMPTY = -1e29
VMEM_LIMIT = 16 * 1024 * 1024
NT = (((1,), (1,)), ((), ()))
NN = (((1,), (0,)), ((), ()))
F32 = jnp.float32
BF16 = jnp.bfloat16


def dot_nt(a, b):
    return lax.dot_general(a, b, NT, preferred_element_type=F32)


def dot_nn(a, b):
    return lax.dot_general(a, b, NN, preferred_element_type=F32)


def start_of(doc_ref, positions):
    end = jnp.int32(0)
    starts = jnp.zeros_like(positions)
    for doc in range(DOC_COUNT):
        length = doc_ref[doc]
        end = end + length
        starts = starts + jnp.where(end <= positions, length, 0)
    return starts


def step_ranges(place_ref, doc_ref, steps_ref):
    z, j = place_ref[0], place_ref[1]
    for rel in range(SLAB):
        qb = j ^ rel
        first = start_of(doc_ref, (SLAB * z + qb) * ROWS) // ROWS
        steps_ref[2 * rel] = jnp.where(j <= qb, 0, 1)
        steps_ref[2 * rel + 1] = z - jnp.maximum((first - j + SLAB - 1) >> 2, 0)


def pack_kernel(q_ref, g_ref, k_ref, v_ref, qg_ref, kv_ref, sems):
    wide, thin = GROUP * HD, HD
    copies = [
        pltpu.make_async_copy(k_ref, kv_ref.at[:, :thin], sems.at[0]),
        pltpu.make_async_copy(v_ref, kv_ref.at[:, thin:], sems.at[1]),
        pltpu.make_async_copy(q_ref, qg_ref.at[:, :wide], sems.at[2]),
        pltpu.make_async_copy(g_ref, qg_ref.at[:, wide:], sems.at[3]),
    ]
    for copy in copies:
        copy.start()
    for copy in copies:
        copy.wait()


def stats_steps(place_ref, doc_ref, rels, steps, fresh, qg, kv, tops, weights, out_ref, ranges):
    z, j = place_ref[0], place_ref[1]
    step_ranges(place_ref, doc_ref, ranges)

    def per_block(rel, _):
        qb = j ^ rel
        positions = (SLAB * z + qb) * ROWS + lax.broadcasted_iota(jnp.int32, (1, ROWS), 1)
        starts = start_of(doc_ref, positions)

        def per_step(k, carry):
            key_pos = lax.broadcasted_iota(jnp.int32, (ROWS, ROWS), 0)
            offset = (SLAB * (z - k) + j) * ROWS
            mask = (key_pos >= starts - offset) & (key_pos <= positions - offset)
            keys = kv[k, :, :HD]
            values = kv[k, :, HD:]

            def products(h):
                q = qg[rel, :, h * HD : (h + 1) * HD]
                g = qg[rel, :, (GROUP + h) * HD : (GROUP + h + 1) * HD]
                return dot_nt(keys, q), dot_nt(values, g)

            new = []
            ahead = products(0)
            for h in range(GROUP):
                s, dp = ahead
                if h + 1 < GROUP:
                    ahead = products(h + 1)
                top, total, dot = carry[3 * h : 3 * h + 3]
                s = jnp.where(mask, s * SCALE2, MASKED)
                new_top = jnp.maximum(top, jnp.max(s, axis=0, keepdims=True))
                p = jnp.exp2(s - new_top)
                weights[rel * (REACH + 1) + k, h] = p.astype(BF16)
                tops[k, pl.ds(rel * GROUP + h, 1), :] = new_top
                factor = jnp.exp2(top - new_top)
                new += [
                    new_top,
                    total * factor + jnp.sum(p, axis=0, keepdims=True),
                    dot * factor + jnp.sum(p * dp, axis=0, keepdims=True),
                ]
            return tuple(new)

        if fresh:
            zero = jnp.zeros((1, ROWS), F32)
            init = (jnp.full((1, ROWS), EMPTY, F32), zero, zero) * GROUP
        else:
            init = tuple(
                out_ref[part, pl.ds(qb * GROUP + h, 1), :]
                for h in range(GROUP)
                for part in range(3)
            )
        first = jnp.maximum(ranges[2 * rel], steps[0])
        end = jnp.minimum(ranges[2 * rel + 1] + 1, steps[1])
        done = lax.fori_loop(first, end, per_step, init)
        for h in range(GROUP):
            for part in range(3):
                out_ref[part, pl.ds(qb * GROUP + h, 1), :] = done[3 * h + part]
        return 0

    lax.fori_loop(rels[0], rels[1], per_block, 0)


def first_stats_kernel(
    place_ref, doc_ref, qg0, qg1, kv0, out_ref, tops, weights, qg_all, kv_all, ranges
):
    qg_all[0] = qg0[...]
    qg_all[1] = qg1[...]
    kv_all[0] = kv0[...]
    stats_steps(
        place_ref, doc_ref, HERE, (0, 1), True, qg_all, kv_all, tops, weights, out_ref, ranges
    )


def here_stats_kernel(
    place_ref, doc_ref, in0, in1, in2, in3, qg_all, kv1, kv2, out_ref, tops, weights, kv_all, ranges
):
    del in0, in1, in2, in3
    kv_all[1] = kv1[...]
    kv_all[2] = kv2[...]
    stats_steps(
        place_ref, doc_ref, HERE, (1, HALF), False, qg_all, kv_all, tops, weights, out_ref, ranges
    )


def there_stats_kernel(
    place_ref, doc_ref, in0, in1, in2, in3, kv_all, qg2, qg3, out_ref, tops, weights, qg_all, ranges
):
    del in0, in1, in2, in3
    qg_all[2] = qg2[...]
    qg_all[3] = qg3[...]
    stats_steps(
        place_ref, doc_ref, THERE, (0, HALF), True, qg_all, kv_all, tops, weights, out_ref, ranges
    )


def far_stats_kernel(
    place_ref, doc_ref, in0, in1, in2, in3, qg_all, kv3, kv4, kv5,
    out_ref, tops, weights, kv_all, ranges,
):
    del in0, in1, in2, in3
    for slot, ref in enumerate((kv3, kv4, kv5)):
        kv_all[HALF + slot] = ref[...]
    stats_steps(
        place_ref, doc_ref, (0, SLAB), (HALF, REACH + 1), False,
        qg_all, kv_all, tops, weights, out_ref, ranges,
    )


def combine_stats(st_refs, lse_buf, delta_buf):
    stats = [ref[...] for ref in st_refs]
    top = jnp.maximum(
        jnp.maximum(stats[0][0], stats[1][0]), jnp.maximum(stats[2][0], stats[3][0])
    )
    total = jnp.zeros_like(top)
    dot = jnp.zeros_like(top)
    for st in stats:
        factor = jnp.exp2(st[0] - top)
        total = total + st[1] * factor
        dot = dot + st[2] * factor
    lse_buf[...] = top + jnp.log2(total)
    delta_buf[...] = dot / total


def visit_step(j, k, rels, ranges, data, dqt, acc):
    lse_buf, delta_buf, tops, weights, qg_all, kv_all = data
    keys_t = kv_all[k, :, :HD].astype(F32).T.astype(BF16)

    def per_block(rel, _):
        qb = j ^ rel

        @pl.when((k >= ranges[2 * rel]) & (k <= ranges[2 * rel + 1]))
        def _():
            values = kv_all[k, :, HD:]

            def grad_of(h):
                return qg_all[rel, :, (GROUP + h) * HD : (GROUP + h + 1) * HD]

            dk = dv = None
            ahead = dot_nt(values, grad_of(0))
            for h in range(GROUP):
                dp = ahead
                if h + 1 < GROUP:
                    ahead = dot_nt(values, grad_of(h + 1))
                q = qg_all[rel, :, h * HD : (h + 1) * HD]
                lse = lse_buf[pl.ds(qb * GROUP + h, 1), :]
                delta = delta_buf[pl.ds(qb * GROUP + h, 1), :]
                factor = jnp.exp2(tops[k, pl.ds(rel * GROUP + h, 1), :] - lse)
                p = weights[rel * (REACH + 1) + k, h].astype(F32) * factor
                ds = p * (dp - delta)
                pb = p.astype(BF16)
                dsb = ds.astype(BF16)
                dv_add, dk_add = dot_nn(pb, grad_of(h)), dot_nn(dsb, q)
                dv = dv_add if dv is None else dv + dv_add
                dk = dk_add if dk is None else dk + dk_add
                dqt[rel * GROUP + h] += dot_nn(keys_t, dsb)
            acc[:, :HD] += dk
            acc[:, HD:] += dv

        return 0

    lax.fori_loop(rels[0], rels[1], per_block, 0)


def write_dq(dqt, slot, out_ref):
    for h in range(GROUP):
        dq = dqt[slot * GROUP + h].T * SCALE
        out_ref[:, h * HD : (h + 1) * HD] = dq.astype(BF16)


def write_dkv(out_ref, acc):
    out_ref[:, :HD] = (acc[:, :HD] * SCALE).astype(out_ref.dtype)
    out_ref[:, HD:] = acc[:, HD:].astype(out_ref.dtype)


def far_kernel(
    place_ref, doc_ref, st0, st1, st2, st3, tops, weights, qg_all, kv_all,
    dqt, dkv34, dkv5, acc0_ref, lse_ref, delta_ref, acc, ranges,
):
    step_ranges(place_ref, doc_ref, ranges)
    combine_stats((st0, st1, st2, st3), lse_ref, delta_ref)
    dqt[...] = jnp.zeros_like(dqt)

    def per_step(step, _):
        k = jnp.where(step == 0, 0, REACH + 1 - step)
        acc[...] = jnp.zeros_like(acc)
        visit_step(
            place_ref[1], k, (jnp.where(step == 0, THERE[0], 0), SLAB), ranges,
            (lse_ref, delta_ref, tops, weights, qg_all, kv_all), dqt, acc,
        )

        @pl.when(step == 0)
        def _():
            acc0_ref[...] = acc[...]

        for slot, ref in enumerate((dkv5, dkv34.at[1], dkv34.at[0])):

            @pl.when(step == slot + 1)
            def _():
                write_dkv(ref, acc)

        return 0

    lax.fori_loop(0, HALF + 1, per_step, 0)


def near_kernel(
    place_ref, doc_ref, dqt_in, lse_ref, delta_ref, tops, weights, qg_all, kv_all,
    dqt, across_ref, both_ref, dkv1, dkv2, acc, ranges,
):
    del dqt_in
    step_ranges(place_ref, doc_ref, ranges)

    def per_step(step, _):
        k = 2 - step
        acc[...] = jnp.zeros_like(acc)
        visit_step(
            place_ref[1], k, (0, SLAB), ranges,
            (lse_ref, delta_ref, tops, weights, qg_all, kv_all), dqt, acc,
        )

        @pl.when(k == 2)
        def _():
            write_dkv(dkv2, acc)

        @pl.when(k == 1)
        def _():
            write_dkv(dkv1, acc)

        return 0

    lax.fori_loop(0, 2, per_step, 0)
    write_dq(dqt, 2, across_ref)
    write_dq(dqt, 3, both_ref)


def own_kernel(
    place_ref, doc_ref, dqt_in, lse_ref, delta_ref, tops, weights, qg_all, kv_all, acc0,
    dqt, keep_ref, send_ref, dkv_ref, acc, ranges,
):
    del dqt_in
    step_ranges(place_ref, doc_ref, ranges)
    acc[...] = acc0[...]
    visit_step(
        place_ref[1], jnp.int32(0), HERE, ranges,
        (lse_ref, delta_ref, tops, weights, qg_all, kv_all), dqt, acc,
    )
    write_dkv(dkv_ref, acc)
    write_dq(dqt, 0, keep_ref)
    write_dq(dqt, 1, send_ref)


def merge_kernel(keep, beside, across, both, dkv0, got1, got2, got5, out_ref):
    parts, part = out_ref.shape[:2]
    width = GROUP * HD
    dq = keep[...].astype(F32) + beside[...].astype(F32)
    dq = dq + across[...].astype(F32) + both[...].astype(F32)
    dkv = dkv0[...] + got1[...].astype(F32) + got2[...].astype(F32) + got5[...].astype(F32)
    out_ref[:, :, :width] = dq.astype(BF16).reshape(parts, part, width)
    out_ref[:, :, width:] = dkv.astype(BF16).reshape(parts, part, 2 * HD)


def finish_kernel(got, q_ref, k_ref, v_ref):
    width = GROUP * HD
    for t in range(got.shape[0]):
        q_ref[:, t * width : (t + 1) * width] = got[t, :, :width]
        k_ref[:, t * HD : (t + 1) * HD] = got[t, :, width : width + HD]
        v_ref[:, t * HD : (t + 1) * HD] = got[t, :, width + HD :]


SMEM_SPEC = pl.BlockSpec(memory_space=pltpu.SMEM)
VMEM_SPEC = pl.BlockSpec(memory_space=pltpu.VMEM)


def call(kernel, name, outs, scratch, *args, scalars=2, aliases=None, ranges=True):
    return pl.pallas_call(
        kernel,
        out_shape=tuple(jax.ShapeDtypeStruct(shape, dtype) for shape, dtype in outs),
        in_specs=[SMEM_SPEC] * scalars + [VMEM_SPEC] * (len(args) - scalars),
        out_specs=(VMEM_SPEC,) * len(outs),
        scratch_shapes=[pltpu.VMEM(shape, dtype) for shape, dtype in scratch]
        + [pltpu.SMEM((2 * SLAB,), jnp.int32)] * ranges,
        input_output_aliases=aliases or {},
        compiler_params=pltpu.CompilerParams(vmem_limit_bytes=VMEM_LIMIT),
        cost_estimate=pl.CostEstimate(flops=1, bytes_accessed=1, transcendentals=0),
        name=name,
    )(*args)


QG_ALL = ((SLAB, ROWS, 2 * GROUP * HD), BF16)
KV_ALL = ((REACH + 1, ROWS, 2 * HD), BF16)
STATS = ((3, SLAB * GROUP, ROWS), F32)
TOPS = ((REACH + 1, SLAB * GROUP, ROWS), F32)
WEIGHTS = ((SLAB * (REACH + 1), GROUP, ROWS, ROWS), BF16)
ROW_STATS = ((SLAB * GROUP, ROWS), F32)
DQT = ((SLAB * GROUP, HD, ROWS), F32)
ACC = ((ROWS, 2 * HD), F32)
DKV = ((ROWS, 2 * HD), BF16)
DQ = ((ROWS, GROUP * HD), BF16)


def flip(x, axis):
    return lax.ppermute(x, axis, [(0, 1), (1, 0)])


def shift(x, by, slabs):
    pairs = [(i, i + by) for i in range(slabs) if 0 <= i + by < slabs]
    return lax.ppermute(x, "z", pairs)


def wrapped(x, by, sources, slabs):
    return lax.ppermute(x, "z", [(i, (i + by) % slabs) for i in sources])


def shift_last(x, by, slabs):
    last = SLAB - 1
    pairs = [
        (i * SLAB + last, (i + by) * SLAB + last) for i in range(slabs) if 0 <= i + by < slabs
    ]
    return lax.ppermute(x, ("z", "y", "core"), pairs)


def local(queries, keys, values, grad_out, doc_lengths):
    z = lax.axis_index("z")
    j = lax.axis_index(("y", "core"))
    slabs = lax.axis_size("z")
    place = jnp.stack((z, j)).astype(jnp.int32)

    qg, kv = pl.pallas_call(
        pack_kernel,
        out_shape=(
            jax.ShapeDtypeStruct((ROWS, 2 * GROUP * HD), BF16),
            jax.ShapeDtypeStruct((ROWS, 2 * HD), BF16),
        ),
        in_specs=[pl.BlockSpec(memory_space=pltpu.HBM)] * 4,
        out_specs=(VMEM_SPEC,) * 2,
        scratch_shapes=[pltpu.SemaphoreType.DMA((4,))],
        compiler_params=pltpu.CompilerParams(vmem_limit_bytes=56 * 1024 * 1024),
        cost_estimate=pl.CostEstimate(flops=1, bytes_accessed=1, transcendentals=0),
        name="pack",
    )(queries, grad_out, keys, values)
    across = flip(qg, "y")
    kv1 = shift(kv, 1, slabs)
    kv2 = shift(kv, 2, slabs)
    beside = flip(qg, "core")
    kv5 = shift_last(kv, 5, slabs)
    ahead = [i for i in range(slabs) if i + 4 < slabs]
    kv_by = wrapped(kv, -2, ahead, slabs)

    stats, tops, weights, qg_all, kv_all = call(
        first_stats_kernel, "first_statistics", [STATS, TOPS, WEIGHTS, QG_ALL, KV_ALL], [],
        place, doc_lengths, qg, beside, kv,
    )
    across, kv1, kv2, kv5, kv_by, stats = lax.optimization_barrier(
        (across, kv1, kv2, kv5, kv_by, stats)
    )
    kv3 = shift(kv2, 1, slabs)
    kv4 = wrapped(kv_by, -2, [(i - 2) % slabs for i in ahead], slabs)
    both = flip(across, "core")
    stats, tops, weights, kv_all = call(
        here_stats_kernel, "here_statistics", [STATS, TOPS, WEIGHTS, KV_ALL], [],
        place, doc_lengths, stats, tops, weights, kv_all, qg_all, kv1, kv2,
        aliases={2: 0, 3: 1, 4: 2, 5: 3},
    )
    stats, tops, weights, qg_all = call(
        there_stats_kernel, "there_statistics", [STATS, TOPS, WEIGHTS, QG_ALL], [],
        place, doc_lengths, stats, tops, weights, qg_all, kv_all, across, both,
        aliases={2: 0, 3: 1, 4: 2, 5: 3},
    )
    stats, tops, weights, kv_all = call(
        far_stats_kernel, "far_statistics", [STATS, TOPS, WEIGHTS, KV_ALL], [],
        place, doc_lengths, stats, tops, weights, kv_all, qg_all, kv3, kv4, kv5,
        aliases={2: 0, 3: 1, 4: 2, 5: 3},
    )
    stats_y = flip(stats, "y")
    stats_c = flip(stats, "core")
    stats_yc = flip(stats_y, "core")

    data = (tops, weights, qg_all, kv_all)
    dqt, dkv34, dkv5, acc0, lse, delta = call(
        far_kernel, "far_gradients",
        [DQT, ((2,) + DKV[0], BF16), DKV, ACC, ROW_STATS, ROW_STATS], [ACC],
        place, doc_lengths, stats, stats_c, stats_y, stats_yc, *data,
    )
    got_far = shift(dkv34, -2, slabs)
    got5 = shift_last(dkv5, -5, slabs)
    dqt, dq_across, dq_both, dkv1, dkv2 = call(
        near_kernel, "near_gradients", [DQT, DQ, DQ, ACC, ACC], [ACC],
        place, doc_lengths, dqt, lse, delta, *data, aliases={2: 0},
    )
    dq_across = flip(dq_across, "y")
    dq_both = lax.ppermute(dq_both, ("y", "core"), [(i, i ^ 3) for i in range(SLAB)])
    dkv1 = (dkv1 + got_far[0].astype(F32)).astype(BF16)
    dkv2 = (dkv2 + got_far[1].astype(F32)).astype(BF16)
    got2 = shift(dkv2, -2, slabs)
    got1 = shift(dkv1, -1, slabs)
    _, dq_keep, dq_send, dkv0 = call(
        own_kernel, "own_gradients", [DQT, DQ, DQ, ACC], [ACC],
        place, doc_lengths, dqt, lse, delta, *data, acc0, aliases={2: 0},
    )
    dq_beside = flip(dq_send, "core")
    got1, got2, got5, dq_across, dq_both, dq_beside = lax.optimization_barrier(
        (got1, got2, got5, dq_across, dq_both, dq_beside)
    )

    tp = lax.axis_size("tp")
    part = ROWS // tp
    width = GROUP * HD
    whole, = call(
        merge_kernel, "merge", [((tp, part, width + 2 * HD), BF16)], [],
        dq_keep, dq_beside, dq_across, dq_both, dkv0, got1, got2, got5, scalars=0, ranges=False,
    )
    got = lax.all_to_all(whole, "tp", split_axis=0, concat_axis=0, tiled=True)
    return call(
        finish_kernel, "finish",
        [((part, tp * width), BF16), ((part, tp * HD), BF16), ((part, tp * HD), BF16)], [],
        got, scalars=0, ranges=False,
    )


def solution(mesh):
    tp = mesh.shape["tp"]
    inner = Mesh(mesh.devices.reshape(-1, 2, 2, tp), ("z", "y", "core", "tp"))
    tokens = ("z", "y", "core")
    in_specs = (P(tokens, "tp"),) * 4 + (P(),)
    out_specs = (P(tokens + ("tp",), None),) * 3
    return jax.shard_map(local, mesh=inner, in_specs=in_specs, out_specs=out_specs, check_vma=False)
```

profile of v0, /device:TPU:96, one launch (start us, length us, event | category | flops | bytes accessed | tf_op | source)
XLA Modules:
  0.0 92.8 jit_solution(15779085724132230757)
XLA Ops:
  0.6 2.0 %pack.1 = (bf16[256,1024]{1,0:T(8,128)(2,1)}, bf16[256,256]{1,0:T(8,128)(2,1)}) custom-call(bf16[256,512]{1,0:T(8,128)(2,1)} %q_ref.1, bf16[256,512]{1,0:T(8,128)(2,1)} %g_ref.1, bf16[256,128]{1,0:T(8,128)(2,1)} %k_ref.1, bf16[256,128]{1,0:T(8,128)(2,1)} %v_ref.1), custom_call_target="tpu_custom_call" | custom-call | flops 1 | bytes 1 | tf_op jit(solution)/shard_map/pack/pallas_call | solution.py:397
  2.6 0.1 collective-permute-start.5
  2.7 3.3 %collective-permute-start = (bf16[256,1024]{1,0:T(8,128)(2,1)}, bf16[256,1024]{1,0:T(8,128)(2,1)S(1)}, u32[]{:S(2)}, u32[]{:S(2)}) collective-permute-start(bf16[256,1024]{1,0:T(8,128)(2,1)} %get-tuple-element.48.qg0), channel_id=1, source_target_pairs={{0,16},{16,0},{1,17},{17,1},{2,18},{18,2},{3,19},{19,3},{4,20},{20... | collective-permute-start | bytes 1572872 | tf_op jit(solution)/shard_map/ppermute | solution.py:371
  6.0 1.6 %collective-permute-start.4 = (bf16[256,256]{1,0:T(8,128)(2,1)}, bf16[256,256]{1,0:T(8,128)(2,1)S(1)}, u32[]{:S(2)}, u32[]{:S(2)}) collective-permute-start(bf16[256,256]{1,0:T(8,128)(2,1)} %get-tuple-element.49.kv0), channel_id=1, source_target_pairs={{0,192},{32,224},{64,0},{96,32},{1,193},{33,225},{65,1},{97,33},{2... | collective-permute-start | bytes 393224 | tf_op jit(solution)/shard_map/ppermute | solution.py:380
  7.5 0.7 collective-permute-start.3
  8.2 4.6 %collective-permute-start.2 = (bf16[256,256]{1,0:T(8,128)(2,1)}, bf16[256,256]{1,0:T(8,128)(2,1)S(1)}, u32[]{:S(2)}, u32[]{:S(2)}) collective-permute-start(bf16[256,256]{1,0:T(8,128)(2,1)} %get-tuple-element.49.kv0), channel_id=1, source_target_pairs={{0,64},{32,96},{64,128},{96,160},{128,192},{160,224},{1,65},{33,97... | collective-permute-start | bytes 393224 | tf_op jit(solution)/shard_map/ppermute | solution.py:376
  12.8 0.0 collective-permute-done.5.qg1
  12.8 3.5 %collective-permute-start.1 = (bf16[256,256]{1,0:T(8,128)(2,1)}, bf16[256,256]{1,0:T(8,128)(2,1)S(1)}, u32[]{:S(2)}, u32[]{:S(2)}) collective-permute-start(bf16[256,256]{1,0:T(8,128)(2,1)} %get-tuple-element.49.kv0), channel_id=1, source_target_pairs={{0,32},{32,64},{64,96},{96,128},{128,160},{160,192},{192,224},{1,3... | collective-permute-start | bytes 393224 | tf_op jit(solution)/shard_map/ppermute | solution.py:376
  16.4 0.1 pad_add_fusion.place_ref
  16.5 0.0 copy-start
  16.5 1.0 %copy-done = bf16[256,1024]{1,0:T(8,128)(2,1)S(1)} copy-done((bf16[256,1024]{1,0:T(8,128)(2,1)S(1)}, bf16[256,1024]{1,0:T(8,128)(2,1)}, u32[]{:S(2)}) %copy-start) | copy-done | bytes 524312
  17.5 0.0 copy-start.1
  17.5 0.9 copy-done.1
  18.4 0.0 copy-start.2
  18.4 0.7 copy-done.2
  19.1 2.0 %first_statistics.1 = (f32[3,16,256]{2,1,0:T(8,128)S(1)}, f32[6,16,256]{2,1,0:T(8,128)S(1)}, bf16[24,4,256,256]{3,2,1,0:T(8,128)(2,1)S(1)}, bf16[4,256,1024]{2,1,0:T(8,128)(2,1)S(1)}, bf16[6,256,256]{2,1,0:T(8,128)(2,1)S(1)}) custom-call(s32[2]{0:T(128)S(1)} %pad_add_fusion.place_ref, s32[17]{0:T(128)S(1)} %copy-done.2, bf16[256,1024]{1,0:T(8,128)(2,1)S(1)} %copy-done, ...), custom_call_target="tpu_custom_call" | custom-call | flops 1 | bytes 1 | tf_op jit(solution)/shard_map/first_statistics/pallas_call | solution.py:344
  21.1 0.0 collective-permute-done.4
  21.1 0.0 collective-permute-done.3.kv5
  21.1 0.9 collective-permute-done.2.kv2
  22.0 1.2 %collective-permute-done.1.kv1 = bf16[256,256]{1,0:T(8,128)(2,1)S(1)} collective-permute-done((bf16[256,256]{1,0:T(8,128)(2,1)}, bf16[256,256]{1,0:T(8,128)(2,1)S(1)}, u32[]{:S(2)}, u32[]{:S(2)}) %collective-permute-start.1) | collective-permute-done | bytes 131104 | tf_op jit(solution)/shard_map/ppermute | solution.py:376
  23.2 0.0 collective-permute-done.qg2
  23.2 0.0 collective-permute-start.6
  23.2 0.7 collective-permute-start.8
  23.9 4.7 %collective-permute-start.7 = (bf16[256,256]{1,0:T(8,128)(2,1)S(1)}, bf16[256,256]{1,0:T(8,128)(2,1)S(1)}, u32[]{:S(2)}, u32[]{:S(2)}) collective-permute-start(bf16[256,256]{1,0:T(8,128)(2,1)S(1)} %collective-permute-done.2.kv2), channel_id=1, source_target_pairs={{0,32},{32,64},{64,96},{96,128},{128,160},{160,192},{192,224},{1,3... | collective-permute-start | bytes 393224 | tf_op jit(solution)/shard_map/ppermute | solution.py:376
  28.6 2.0 %here_statistics.1 = (f32[3,16,256]{2,1,0:T(8,128)S(1)}, f32[6,16,256]{2,1,0:T(8,128)S(1)}, bf16[24,4,256,256]{3,2,1,0:T(8,128)(2,1)S(1)}, bf16[6,256,256]{2,1,0:T(8,128)(2,1)S(1)}) custom-call(s32[2]{0:T(128)S(1)} %pad_add_fusion.place_ref, s32[17]{0:T(128)S(1)} %copy-done.2, ...), custom_call_target="tpu_custom_call", output_to_operand_aliasing={{0}: (2, {}), {1}: (3, {}), {2}: (4, {}), {3}: (5, {})} | custom-call | flops 1 | bytes 1 | tf_op jit(solution)/shard_map/here_statistics/pallas_call | solution.py:344
  30.6 0.0 collective-permute-done.6.qg3
  30.6 3.3 %there_statistics.1 = (f32[3,16,256]{2,1,0:T(8,128)S(1)}, f32[6,16,256]{2,1,0:T(8,128)S(1)}, bf16[24,4,256,256]{3,2,1,0:T(8,128)(2,1)S(1)}, bf16[4,256,1024]{2,1,0:T(8,128)(2,1)S(1)}) custom-call(s32[2]{0:T(128)S(1)} %pad_add_fusion.place_ref, s32[17]{0:T(128)S(1)} %copy-done.2, ...), custom_call_target="tpu_custom_call", output_to_operand_aliasing={{0}: (2, {}), {1}: (3, {}), {2}: (4, {}), {3}: (5, {})} | custom-call | flops 1 | bytes 1 | tf_op jit(solution)/shard_map/there_statistics/pallas_call | solution.py:344
  33.9 0.0 collective-permute-done.8.kv4
  33.9 0.0 collective-permute-done.7.kv3
  33.9 0.8 far_statistics.1
  34.7 0.1 collective-permute-start.10
  34.8 2.1 %collective-permute-start.9 = (f32[3,16,256]{2,1,0:T(8,128)S(1)}, f32[3,16,256]{2,1,0:T(8,128)S(1)}, u32[]{:S(2)}, u32[]{:S(2)}) collective-permute-start(f32[3,16,256]{2,1,0:T(8,128)S(1)} %get-tuple-element.69.st0), channel_id=1, source_target_pairs={{0,8},{8,0},{1,9},{9,1},{2,10},{10,2},{3,11},{11,3},{4,12},{12,4},... | collective-permute-start | bytes 147464 | tf_op jit(solution)/shard_map/ppermute | solution.py:371
  37.0 3.5 %collective-permute-done.10.st2 = f32[3,16,256]{2,1,0:T(8,128)S(1)} collective-permute-done((f32[3,16,256]{2,1,0:T(8,128)S(1)}, f32[3,16,256]{2,1,0:T(8,128)S(1)}, u32[]{:S(2)}, u32[]{:S(2)}) %collective-permute-start.10) | collective-permute-done | bytes 49184 | tf_op jit(solution)/shard_map/ppermute | solution.py:371
  40.4 0.0 collective-permute-start.11
  40.4 0.0 collective-permute-done.9.st1
  40.4 1.2 %collective-permute-done.11.st3 = f32[3,16,256]{2,1,0:T(8,128)S(1)} collective-permute-done((f32[3,16,256]{2,1,0:T(8,128)S(1)}, f32[3,16,256]{2,1,0:T(8,128)S(1)}, u32[]{:S(2)}, u32[]{:S(2)}) %collective-permute-start.11) | collective-permute-done | bytes 49184 | tf_op jit(solution)/shard_map/ppermute | solution.py:371
  41.6 0.0 copy-start.3
  41.7 3.2 %far_gradients.1 = (f32[16,128,256]{2,1,0:T(8,128)S(1)}, bf16[2,256,256]{2,1,0:T(8,128)(2,1)S(1)}, bf16[256,256]{1,0:T(8,128)(2,1)S(1)}, f32[256,256]{1,0:T(8,12...) custom-call(s32[2]{0:T(128)S(1)} %pad_add_fusion.place_ref, s32[17]{0:T(128)S(1)} %copy-done.2, ...), custom_call_target="tpu_custom_call" | custom-call | flops 1 | bytes 1 | tf_op jit(solution)/shard_map/far_gradients/pallas_call | solution.py:344
  44.8 2.8 %collective-permute-start.12 = (bf16[2,256,256]{2,1,0:T(8,128)(2,1)S(1)}, bf16[2,256,256]{2,1,0:T(8,128)(2,1)S(1)}, u32[]{:S(2)}, u32[]{:S(2)}) collective-permute-start(bf16[2,256,256]{2,1,0:T(8,128)(2,1)S(1)} %get-tuple-element.80), channel_id=1, source_target_pairs={{64,0},{96,32},{128,64},{160,96},{192,128},{224,160},{65,1},{97,33... | collective-permute-start | bytes 786440 | tf_op jit(solution)/shard_map/ppermute | solution.py:376
  47.7 0.7 collective-permute-start.15
  48.3 0.0 copy-done.3
  48.3 4.6 %near_gradients.1 = (f32[16,128,256]{2,1,0:T(8,128)S(1)}, bf16[256,512]{1,0:T(8,128)(2,1)S(1)}, bf16[256,512]{1,0:T(8,128)(2,1)S(1)}, f32[256,256]{1,0:T(8,128)S(1)}, f32[256,256]{1,0:T(8,128)S(1)}) custom-call(s32[2]{0:T(128)S(1)} %pad_add_fusion.place_ref, s32[17]{0:T(128)S(1)} %copy-done.3, ...), custom_call_target="tpu_custom_call", output_to_operand_aliasing={{0}: (2, {})} | custom-call | flops 1 | bytes 1 | tf_op jit(solution)/shard_map/near_gradients/pallas_call | solution.py:344
  52.9 2.7 %own_gradients.1 = (f32[16,128,256]{2,1,0:T(8,128)S(1)}, bf16[256,512]{1,0:T(8,128)(2,1)S(1)}, bf16[256,512]{1,0:T(8,128)(2,1)S(1)}, f32[256,256]{1,0:T(8,128)S(1)}) custom-call(s32[2]{0:T(128)S(1)} %pad_add_fusion.place_ref, s32[17]{0:T(128)S(1)} %copy-done.3, f32[16,128,256]{2,1,0:T(8,128)S(1)} %get-tuple-element.76.dqt_in, ...), custom_call_target="tpu_custom_call", output_to_operand_aliasing={{0}: (2, {})} | custom-call | flops 1 | bytes 1 | tf_op jit(solution)/shard_map/own_gradients/pallas_call | solution.py:344
  55.6 0.1 collective-permute-start.18
  55.7 2.3 %collective-permute-start.16 = (bf16[256,512]{1,0:T(8,128)(2,1)S(1)}, bf16[256,512]{1,0:T(8,128)(2,1)S(1)}, u32[]{:S(2)}, u32[]{:S(2)}) collective-permute-start(bf16[256,512]{1,0:T(8,128)(2,1)S(1)} %get-tuple-element.83), channel_id=1, source_target_pairs={{0,16},{16,0},{1,17},{17,1},{2,18},{18,2},{3,19},{19,3},{4,20},{20... | collective-permute-start | bytes 786440 | tf_op jit(solution)/shard_map/ppermute | solution.py:371
  58.0 1.1 %collective-permute-start.17 = (bf16[256,512]{1,0:T(8,128)(2,1)S(1)}, bf16[256,512]{1,0:T(8,128)(2,1)S(1)}, u32[]{:S(2)}, u32[]{:S(2)}) collective-permute-start(bf16[256,512]{1,0:T(8,128)(2,1)S(1)} %get-tuple-element.84), channel_id=1, source_target_pairs={{0,24},{8,16},{16,8},{24,0},{1,25},{9,17},{17,9},{25,1},{2,26},{10... | collective-permute-start | bytes 786440 | tf_op jit(solution)/shard_map/ppermute | solution.py:460
  59.1 5.9 %collective-permute-done.12 = bf16[2,256,256]{2,1,0:T(8,128)(2,1)S(1)} collective-permute-done((bf16[2,256,256]{2,1,0:T(8,128)(2,1)S(1)}, bf16[2,256,256]{2,1,0:T(8,128)(2,1)S(1)}, u32[]{:S(2)}, u32[]{:S(2)}) %collective-permute-start.12) | collective-permute-done | bytes 262176 | tf_op jit(solution)/shard_map/ppermute | solution.py:376
  65.0 0.1 fusion
  65.1 1.9 %collective-permute-start.14 = (bf16[256,256]{1,0:T(8,128)(2,1)S(1)}, bf16[256,256]{1,0:T(8,128)(2,1)S(1)}, u32[]{:S(2)}, u32[]{:S(2)}) collective-permute-start(bf16[256,256]{1,0:T(8,128)(2,1)S(1)} %get-tuple-element.93), channel_id=1, source_target_pairs={{64,0},{96,32},{128,64},{160,96},{192,128},{224,160},{65,1},{97,33... | collective-permute-start | bytes 393224 | tf_op jit(solution)/shard_map/ppermute | solution.py:376
  67.0 0.0 collective-permute-done.15.got5
  67.0 1.9 %collective-permute-start.13 = (bf16[256,256]{1,0:T(8,128)(2,1)S(1)}, bf16[256,256]{1,0:T(8,128)(2,1)S(1)}, u32[]{:S(2)}, u32[]{:S(2)}) collective-permute-start(bf16[256,256]{1,0:T(8,128)(2,1)S(1)} %get-tuple-element.94), channel_id=1, source_target_pairs={{32,0},{64,32},{96,64},{128,96},{160,128},{192,160},{224,192},{33,... | collective-permute-start | bytes 393224 | tf_op jit(solution)/shard_map/ppermute | solution.py:376
  68.9 0.0 collective-permute-done.18.beside
  68.9 0.0 collective-permute-done.16.across
  69.0 2.1 %collective-permute-done.17.both = bf16[256,512]{1,0:T(8,128)(2,1)S(1)} collective-permute-done((bf16[256,512]{1,0:T(8,128)(2,1)S(1)}, bf16[256,512]{1,0:T(8,128)(2,1)S(1)}, u32[]{:S(2)}, u32[]{:S(2)}) %collective-permute-start.17) | collective-permute-done | bytes 262176 | tf_op jit(solution)/shard_map/ppermute | solution.py:460
  71.1 8.2 %collective-permute-done.14.got2 = bf16[256,256]{1,0:T(8,128)(2,1)S(1)} collective-permute-done((bf16[256,256]{1,0:T(8,128)(2,1)S(1)}, bf16[256,256]{1,0:T(8,128)(2,1)S(1)}, u32[]{:S(2)}, u32[]{:S(2)}) %collective-permute-start.14) | collective-permute-done | bytes 131104 | tf_op jit(solution)/shard_map/ppermute | solution.py:376
  79.3 0.0 collective-permute-done.13.got1
  79.3 0.2 merge.1
  79.5 12.5 %all_to_all.5.got = bf16[8,32,768]{2,1,0:T(8,128)(2,1)S(1)} all-to-all(bf16[8,32,768]{2,1,0:T(8,128)(2,1)S(1)} %merge.1), channel_id=1, replica_groups=mesh['z'=8,'y'=2,'core'=2,'tp'=8] {'tp'}, dimensions={0} | all-to-all | bytes 786432 | tf_op jit(solution)/shard_map/all_to_all | solution.py:481
  92.0 0.8 finish.1
Async XLA Ops:
  2.6 10.2 %collective-permute-start.5 = (bf16[256,1024]{1,0:T(8,128)(2,1)}, bf16[256,1024]{1,0:T(8,128)(2,1)S(1)}, u32[]{:S(2)}, u32[]{:S(2)}) collective-permute-start(bf16[256,1024]{1,0:T(8,128)(2,1)} %get-tuple-element.48.qg0), channel_id=1, source_target_pairs={{0,8},{8,0},{1,9},{9,1},{2,10},{10,2},{3,11},{11,3},{4,12},{12,4},... | collective-permute-start | bytes 1572872 | tf_op jit(solution)/shard_map/ppermute | solution.py:371
  2.7 20.5 %collective-permute-start = (bf16[256,1024]{1,0:T(8,128)(2,1)}, bf16[256,1024]{1,0:T(8,128)(2,1)S(1)}, u32[]{:S(2)}, u32[]{:S(2)}) collective-permute-start(bf16[256,1024]{1,0:T(8,128)(2,1)} %get-tuple-element.48.qg0), channel_id=1, source_target_pairs={{0,16},{16,0},{1,17},{17,1},{2,18},{18,2},{3,19},{19,3},{4,20},{20... | collective-permute-start | bytes 1572872 | tf_op jit(solution)/shard_map/ppermute | solution.py:371
  6.0 15.1 %collective-permute-start.4 = (bf16[256,256]{1,0:T(8,128)(2,1)}, bf16[256,256]{1,0:T(8,128)(2,1)S(1)}, u32[]{:S(2)}, u32[]{:S(2)}) collective-permute-start(bf16[256,256]{1,0:T(8,128)(2,1)} %get-tuple-element.49.kv0), channel_id=1, source_target_pairs={{0,192},{32,224},{64,0},{96,32},{1,193},{33,225},{65,1},{97,33},{2... | collective-permute-start | bytes 393224 | tf_op jit(solution)/shard_map/ppermute | solution.py:380
  7.5 13.6 %collective-permute-start.3 = (bf16[256,256]{1,0:T(8,128)(2,1)}, bf16[256,256]{1,0:T(8,128)(2,1)S(1)}, u32[]{:S(2)}, u32[]{:S(2)}) collective-permute-start(bf16[256,256]{1,0:T(8,128)(2,1)} %get-tuple-element.49.kv0), channel_id=1, source_target_pairs={{24,184},{56,216},{88,248},{25,185},{57,217},{89,249},{26,186},{58... | collective-permute-start | bytes 393224 | tf_op jit(solution)/shard_map/ppermute | solution.py:388
  8.2 13.8 %collective-permute-start.2 = (bf16[256,256]{1,0:T(8,128)(2,1)}, bf16[256,256]{1,0:T(8,128)(2,1)S(1)}, u32[]{:S(2)}, u32[]{:S(2)}) collective-permute-start(bf16[256,256]{1,0:T(8,128)(2,1)} %get-tuple-element.49.kv0), channel_id=1, source_target_pairs={{0,64},{32,96},{64,128},{96,160},{128,192},{160,224},{1,65},{33,97... | collective-permute-start | bytes 393224 | tf_op jit(solution)/shard_map/ppermute | solution.py:376
  12.8 10.4 %collective-permute-start.1 = (bf16[256,256]{1,0:T(8,128)(2,1)}, bf16[256,256]{1,0:T(8,128)(2,1)S(1)}, u32[]{:S(2)}, u32[]{:S(2)}) collective-permute-start(bf16[256,256]{1,0:T(8,128)(2,1)} %get-tuple-element.49.kv0), channel_id=1, source_target_pairs={{0,32},{32,64},{64,96},{96,128},{128,160},{160,192},{192,224},{1,3... | collective-permute-start | bytes 393224 | tf_op jit(solution)/shard_map/ppermute | solution.py:376
  16.5 1.0 %copy-start = (bf16[256,1024]{1,0:T(8,128)(2,1)S(1)}, bf16[256,1024]{1,0:T(8,128)(2,1)}, u32[]{:S(2)}) copy-start(bf16[256,1024]{1,0:T(8,128)(2,1)} %get-tuple-element.48.qg0) | copy-start | bytes 1572868
  17.5 0.9 copy-start.1
  18.4 0.7 copy-start.2
  23.2 7.4 %collective-permute-start.6 = (bf16[256,1024]{1,0:T(8,128)(2,1)S(1)}, bf16[256,1024]{1,0:T(8,128)(2,1)S(1)}, u32[]{:S(2)}, u32[]{:S(2)}) collective-permute-start(bf16[256,1024]{1,0:T(8,128)(2,1)S(1)} %collective-permute-done.qg2), channel_id=1, source_target_pairs={{0,8},{8,0},{1,9},{9,1},{2,10},{10,2},{3,11},{11,3},{4,12},{12,4},... | collective-permute-start | bytes 1572872 | tf_op jit(solution)/shard_map/ppermute | solution.py:371
  23.2 10.7 %collective-permute-start.8 = (bf16[256,256]{1,0:T(8,128)(2,1)S(1)}, bf16[256,256]{1,0:T(8,128)(2,1)S(1)}, u32[]{:S(2)}, u32[]{:S(2)}) collective-permute-start(bf16[256,256]{1,0:T(8,128)(2,1)S(1)} %collective-permute-done.4), channel_id=1, source_target_pairs={{192,128},{224,160},{0,192},{32,224},{193,129},{225,161},{1,193},{... | collective-permute-start | bytes 393224 | tf_op jit(solution)/shard_map/ppermute | solution.py:380
  23.9 10.0 %collective-permute-start.7 = (bf16[256,256]{1,0:T(8,128)(2,1)S(1)}, bf16[256,256]{1,0:T(8,128)(2,1)S(1)}, u32[]{:S(2)}, u32[]{:S(2)}) collective-permute-start(bf16[256,256]{1,0:T(8,128)(2,1)S(1)} %collective-permute-done.2.kv2), channel_id=1, source_target_pairs={{0,32},{32,64},{64,96},{96,128},{128,160},{160,192},{192,224},{1,3... | collective-permute-start | bytes 393224 | tf_op jit(solution)/shard_map/ppermute | solution.py:376
  34.7 5.7 %collective-permute-start.10 = (f32[3,16,256]{2,1,0:T(8,128)S(1)}, f32[3,16,256]{2,1,0:T(8,128)S(1)}, u32[]{:S(2)}, u32[]{:S(2)}) collective-permute-start(f32[3,16,256]{2,1,0:T(8,128)S(1)} %get-tuple-element.69.st0), channel_id=1, source_target_pairs={{0,16},{16,0},{1,17},{17,1},{2,18},{18,2},{3,19},{19,3},{4,20},{20... | collective-permute-start | bytes 147464 | tf_op jit(solution)/shard_map/ppermute | solution.py:371
  34.8 5.6 %collective-permute-start.9 = (f32[3,16,256]{2,1,0:T(8,128)S(1)}, f32[3,16,256]{2,1,0:T(8,128)S(1)}, u32[]{:S(2)}, u32[]{:S(2)}) collective-permute-start(f32[3,16,256]{2,1,0:T(8,128)S(1)} %get-tuple-element.69.st0), channel_id=1, source_target_pairs={{0,8},{8,0},{1,9},{9,1},{2,10},{10,2},{3,11},{11,3},{4,12},{12,4},... | collective-permute-start | bytes 147464 | tf_op jit(solution)/shard_map/ppermute | solution.py:371
  40.4 1.2 %collective-permute-start.11 = (f32[3,16,256]{2,1,0:T(8,128)S(1)}, f32[3,16,256]{2,1,0:T(8,128)S(1)}, u32[]{:S(2)}, u32[]{:S(2)}) collective-permute-start(f32[3,16,256]{2,1,0:T(8,128)S(1)} %collective-permute-done.10.st2), channel_id=1, source_target_pairs={{0,8},{8,0},{1,9},{9,1},{2,10},{10,2},{3,11},{11,3},{4,12},{12,4},... | collective-permute-start | bytes 147464 | tf_op jit(solution)/shard_map/ppermute | solution.py:371
  41.6 6.7 %copy-start.3 = (s32[17]{0:T(128)S(1)}, s32[17]{0:T(128)}, u32[]{:S(2)}) copy-start(s32[17]{0:T(128)} %doc_ref.13) | copy-start | bytes 208
  44.8 20.2 %collective-permute-start.12 = (bf16[2,256,256]{2,1,0:T(8,128)(2,1)S(1)}, bf16[2,256,256]{2,1,0:T(8,128)(2,1)S(1)}, u32[]{:S(2)}, u32[]{:S(2)}) collective-permute-start(bf16[2,256,256]{2,1,0:T(8,128)(2,1)S(1)} %get-tuple-element.80), channel_id=1, source_target_pairs={{64,0},{96,32},{128,64},{160,96},{192,128},{224,160},{65,1},{97,33... | collective-permute-start | bytes 786440 | tf_op jit(solution)/shard_map/ppermute | solution.py:376
  47.7 19.3 %collective-permute-start.15 = (bf16[256,256]{1,0:T(8,128)(2,1)S(1)}, bf16[256,256]{1,0:T(8,128)(2,1)S(1)}, u32[]{:S(2)}, u32[]{:S(2)}) collective-permute-start(bf16[256,256]{1,0:T(8,128)(2,1)S(1)} %get-tuple-element.82), channel_id=1, source_target_pairs={{184,24},{216,56},{248,88},{185,25},{217,57},{249,89},{186,26},{21... | collective-permute-start | bytes 393224 | tf_op jit(solution)/shard_map/ppermute | solution.py:388
  55.6 13.3 %collective-permute-start.18 = (bf16[256,512]{1,0:T(8,128)(2,1)S(1)}, bf16[256,512]{1,0:T(8,128)(2,1)S(1)}, u32[]{:S(2)}, u32[]{:S(2)}) collective-permute-start(bf16[256,512]{1,0:T(8,128)(2,1)S(1)} %get-tuple-element.85), channel_id=1, source_target_pairs={{0,8},{8,0},{1,9},{9,1},{2,10},{10,2},{3,11},{11,3},{4,12},{12,4},... | collective-permute-start | bytes 786440 | tf_op jit(solution)/shard_map/ppermute | solution.py:371
  55.7 13.3 %collective-permute-start.16 = (bf16[256,512]{1,0:T(8,128)(2,1)S(1)}, bf16[256,512]{1,0:T(8,128)(2,1)S(1)}, u32[]{:S(2)}, u32[]{:S(2)}) collective-permute-start(bf16[256,512]{1,0:T(8,128)(2,1)S(1)} %get-tuple-element.83), channel_id=1, source_target_pairs={{0,16},{16,0},{1,17},{17,1},{2,18},{18,2},{3,19},{19,3},{4,20},{20... | collective-permute-start | bytes 786440 | tf_op jit(solution)/shard_map/ppermute | solution.py:371
  58.0 13.1 %collective-permute-start.17 = (bf16[256,512]{1,0:T(8,128)(2,1)S(1)}, bf16[256,512]{1,0:T(8,128)(2,1)S(1)}, u32[]{:S(2)}, u32[]{:S(2)}) collective-permute-start(bf16[256,512]{1,0:T(8,128)(2,1)S(1)} %get-tuple-element.84), channel_id=1, source_target_pairs={{0,24},{8,16},{16,8},{24,0},{1,25},{9,17},{17,9},{25,1},{2,26},{10... | collective-permute-start | bytes 786440 | tf_op jit(solution)/shard_map/ppermute | solution.py:460
  65.1 14.2 %collective-permute-start.14 = (bf16[256,256]{1,0:T(8,128)(2,1)S(1)}, bf16[256,256]{1,0:T(8,128)(2,1)S(1)}, u32[]{:S(2)}, u32[]{:S(2)}) collective-permute-start(bf16[256,256]{1,0:T(8,128)(2,1)S(1)} %get-tuple-element.93), channel_id=1, source_target_pairs={{64,0},{96,32},{128,64},{160,96},{192,128},{224,160},{65,1},{97,33... | collective-permute-start | bytes 393224 | tf_op jit(solution)/shard_map/ppermute | solution.py:376
  67.0 12.3 %collective-permute-start.13 = (bf16[256,256]{1,0:T(8,128)(2,1)S(1)}, bf16[256,256]{1,0:T(8,128)(2,1)S(1)}, u32[]{:S(2)}, u32[]{:S(2)}) collective-permute-start(bf16[256,256]{1,0:T(8,128)(2,1)S(1)} %get-tuple-element.94), channel_id=1, source_target_pairs={{32,0},{64,32},{96,64},{128,96},{160,128},{192,160},{224,192},{33,... | collective-permute-start | bytes 393224 | tf_op jit(solution)/shard_map/ppermute | solution.py:376
where the time goes:
time: 94.5 us; the launch traced here: 92.8 us
  starting transfers between devices  32.1 us (34%)
  waiting for transfers between devices  23.1 us (24%)
  Pallas kernels  21.4 us (23%)
  blocking collectives  12.5 us (13%)
  local copies, waits for them, and re-layouts  2.6 us (3%)
    ppermute x6, starting transfers between devices, shift(): return lax.ppermute(x, 'z', pairs)  19.5 us
    pallas_call x9, Pallas kernels, call(): pl.pallas_call(kernel, out_shape=tuple((jax.ShapeDtypeStruct(shape, dtype...  19.4 us
    ppermute x6, waiting for transfers between devices, shift(): return lax.ppermute(x, 'z', pairs)  16.2 us
    all_to_all x1, blocking collectives, local(): got = lax.all_to_all(whole, 'tp', split_axis=0, concat_axis=0, tiled=True)  12.5 us
    ppermute x8, starting transfers between devices, flip(): return lax.ppermute(x, axis, [(0, 1), (1, 0)])  7.96 us
    ppermute x8, waiting for transfers between devices, flip(): return lax.ppermute(x, axis, [(0, 1), (1, 0)])  4.7 us
    unnamed x8, local copies, waits for them, and re-layouts  2.6 us
    ppermute x2, starting transfers between devices, wrapped(): return lax.ppermute(x, 'z', [(i, (i + by) % slabs) for i in sources])  2.21 us
  transfers between devices with their start and end apart: 19, of which 7 were waited for; matrix products, arithmetic and copies ran while one was open for 0% of the time, Pallas kernels for 16%

commit v1 on v0

--- a/solution.py
+++ b/solution.py
@@ -272,9 +272,9 @@
     lax.fori_loop(0, HALF + 1, per_step, 0)
 
 
-def near_kernel(
+def there_kernel(
     place_ref, doc_ref, dqt_in, lse_ref, delta_ref, tops, weights, qg_all, kv_all,
-    dqt, across_ref, both_ref, dkv1, dkv2, acc, ranges,
+    dqt, keep_ref, send_ref, acc_ref, acc, ranges,
 ):
     del dqt_in
     step_ranges(place_ref, doc_ref, ranges)
@@ -283,7 +283,37 @@
         k = 2 - step
         acc[...] = jnp.zeros_like(acc)
         visit_step(
-            place_ref[1], k, (0, SLAB), ranges,
+            place_ref[1], k, THERE, ranges,
+            (lse_ref, delta_ref, tops, weights, qg_all, kv_all), dqt, acc,
+        )
+        acc_ref[k - 1] = acc[...]
+        return 0
+
+    lax.fori_loop(0, 2, per_step, 0)
+    write_dq(dqt, 2, keep_ref)
+    write_dq(dqt, 3, send_ref)
+
+
+def here_kernel(
+    place_ref, doc_ref, dqt_in, lse_ref, delta_ref, tops, weights, qg_all, kv_all, acc0, acc_near,
+    dqt, beside_ref, dkv1, dkv2, acc0_out, acc, ranges,
+):
+    del dqt_in
+    step_ranges(place_ref, doc_ref, ranges)
+
+    def per_step(step, _):
+        k = 2 - step
+
+        @pl.when(k > 0)
+        def _():
+            acc[...] = acc_near[jnp.maximum(k - 1, 0)]
+
+        @pl.when(k == 0)
+        def _():
+            acc[...] = acc0[...]
+
+        visit_step(
+            place_ref[1], k, (jnp.where(k == 0, 1, 0), HERE[1]), ranges,
             (lse_ref, delta_ref, tops, weights, qg_all, kv_all), dqt, acc,
         )
 
@@ -297,33 +327,35 @@
 
         return 0
 
-    lax.fori_loop(0, 2, per_step, 0)
-    write_dq(dqt, 2, across_ref)
-    write_dq(dqt, 3, both_ref)
+    lax.fori_loop(0, 3, per_step, 0)
+    acc0_out[...] = acc[...]
+    write_dq(dqt, 1, beside_ref)
 
 
 def own_kernel(
     place_ref, doc_ref, dqt_in, lse_ref, delta_ref, tops, weights, qg_all, kv_all, acc0,
-    dqt, keep_ref, send_ref, dkv_ref, acc, ranges,
+    dqt, dq_ref, dkv_ref, acc, ranges,
 ):
     del dqt_in
     step_ranges(place_ref, doc_ref, ranges)
     acc[...] = acc0[...]
     visit_step(
-        place_ref[1], jnp.int32(0), HERE, ranges,
+        place_ref[1], jnp.int32(0), (0, 1), ranges,
         (lse_ref, delta_ref, tops, weights, qg_all, kv_all), dqt, acc,
     )
     write_dkv(dkv_ref, acc)
-    write_dq(dqt, 0, keep_ref)
-    write_dq(dqt, 1, send_ref)
-
-
-def merge_kernel(keep, beside, across, both, dkv0, got1, got2, got5, out_ref):
+    write_dq(dqt, 0, dq_ref)
+
+
+def pair_kernel(keep, got, out_ref):
+    out_ref[...] = (keep[...].astype(F32) + got[...].astype(F32)).astype(BF16)
+
+
+def merge_kernel(keep, beside, across, dkv0, got1, got2, got5, out_ref):
     parts, part = out_ref.shape[:2]
     width = GROUP * HD
-    dq = keep[...].astype(F32) + beside[...].astype(F32)
-    dq = dq + across[...].astype(F32) + both[...].astype(F32)
     dkv = dkv0[...] + got1[...].astype(F32) + got2[...].astype(F32) + got5[...].astype(F32)
+    dq = keep[...].astype(F32) + beside[...].astype(F32) + across[...].astype(F32)
     out_ref[:, :, :width] = dq.astype(BF16).reshape(parts, part, width)
     out_ref[:, :, width:] = dkv.astype(BF16).reshape(parts, part, 2 * HD)
 
@@ -452,23 +484,28 @@
     )
     got_far = shift(dkv34, -2, slabs)
     got5 = shift_last(dkv5, -5, slabs)
-    dqt, dq_across, dq_both, dkv1, dkv2 = call(
-        near_kernel, "near_gradients", [DQT, DQ, DQ, ACC, ACC], [ACC],
+    dqt, there_keep, there_send, acc_near = call(
+        there_kernel, "there_gradients", [DQT, DQ, DQ, ((2,) + ACC[0], F32)], [ACC],
         place, doc_lengths, dqt, lse, delta, *data, aliases={2: 0},
     )
-    dq_across = flip(dq_across, "y")
-    dq_both = lax.ppermute(dq_both, ("y", "core"), [(i, i ^ 3) for i in range(SLAB)])
+    there_got = flip(there_send, "core")
+    dqt, dq_beside, dkv1, dkv2, acc0 = call(
+        here_kernel, "here_gradients", [DQT, DQ, ACC, ACC, ACC], [ACC],
+        place, doc_lengths, dqt, lse, delta, *data, acc0, acc_near, aliases={2: 0},
+    )
     dkv1 = (dkv1 + got_far[0].astype(F32)).astype(BF16)
     dkv2 = (dkv2 + got_far[1].astype(F32)).astype(BF16)
+    there_got, dkv1, dkv2 = lax.optimization_barrier((there_got, dkv1, dkv2))
+    dq_pair, = call(
+        pair_kernel, "pair", [DQ], [], there_keep, there_got, scalars=0, ranges=False
+    )
+    dq_across = flip(dq_pair, "y")
+    dq_beside = flip(dq_beside, "core")
     got2 = shift(dkv2, -2, slabs)
     got1 = shift(dkv1, -1, slabs)
-    _, dq_keep, dq_send, dkv0 = call(
-        own_kernel, "own_gradients", [DQT, DQ, DQ, ACC], [ACC],
+    _, dq_keep, dkv0 = call(
+        own_kernel, "own_gradients", [DQT, DQ, ACC], [ACC],
         place, doc_lengths, dqt, lse, delta, *data, acc0, aliases={2: 0},
-    )
-    dq_beside = flip(dq_send, "core")
-    got1, got2, got5, dq_across, dq_both, dq_beside = lax.optimization_barrier(
-        (got1, got2, got5, dq_across, dq_both, dq_beside)
     )
 
     tp = lax.axis_size("tp")
@@ -476,7 +513,7 @@
     width = GROUP * HD
     whole, = call(
         merge_kernel, "merge", [((tp, part, width + 2 * HD), BF16)], [],
-        dq_keep, dq_beside, dq_across, dq_both, dkv0, got1, got2, got5, scalars=0, ranges=False,
+        dq_keep, dq_beside, dq_across, dkv0, got1, got2, got5, scalars=0, ranges=False,
     )
     got = lax.all_to_all(whole, "tp", split_axis=0, concat_axis=0, tiled=True)
     return call(

time: 94.5 us -> 98.5 us (1.042)
  the two profiles are of different devices: /device:TPU:96 before, /device:TPU:80 now
where the time goes in v1:
time: 98.5 us; the launch traced here: 96.5 us
  starting transfers between devices  33.8 us (34%)
  waiting for transfers between devices  32.1 us (33%)
  Pallas kernels  14.1 us (14%)
  blocking collectives  12.9 us (13%)
  local copies, waits for them, and re-layouts  2.6 us (3%)
    ppermute x6, waiting for transfers between devices, shift(): return lax.ppermute(x, 'z', pairs)  26.9 us
    ppermute x6, starting transfers between devices, shift(): return lax.ppermute(x, 'z', pairs)  21.1 us
    all_to_all x1, blocking collectives, local(): got = lax.all_to_all(whole, 'tp', split_axis=0, concat_axis=0, tiled=True)  12.9 us
    pallas_call x11, Pallas kernels, call(): pl.pallas_call(kernel, out_shape=tuple((jax.ShapeDtypeStruct(shape, dtype...  12.1 us
    ppermute x9, starting transfers between devices, flip(): return lax.ppermute(x, axis, [(0, 1), (1, 0)])  7.44 us
    ppermute x9, waiting for transfers between devices, flip(): return lax.ppermute(x, axis, [(0, 1), (1, 0)])  5.24 us
    ppermute x2, starting transfers between devices, wrapped(): return lax.ppermute(x, 'z', [(i, (i + by) % slabs) for i in sources])  3.95 us
    unnamed x8, local copies, waits for them, and re-layouts  2.6 us
  transfers between devices with their start and end apart: 19, of which 7 were waited for; matrix products, arithmetic and copies ran while one was open for 0% of the time, Pallas kernels for 9%

profile of v1, /device:TPU:80, one launch (start us, length us, event | category | flops | bytes accessed | tf_op | source)
XLA Modules:
  0.0 96.5 jit_solution(10358438649570165256)
XLA Ops:
  0.6 2.0 %pack.1 = (bf16[256,1024]{1,0:T(8,128)(2,1)}, bf16[256,256]{1,0:T(8,128)(2,1)}) custom-call(bf16[256,512]{1,0:T(8,128)(2,1)} %q_ref.1, bf16[256,512]{1,0:T(8,128)(2,1)} %g_ref.1, bf16[256,128]{1,0:T(8,128)(2,1)} %k_ref.1, bf16[256,128]{1,0:T(8,128)(2,1)} %v_ref.1), custom_call_target="tpu_custom_call" | custom-call | flops 1 | bytes 1 | tf_op jit(solution)/shard_map/pack/pallas_call | solution.py:429
  2.6 0.1 collective-permute-start.5
  2.7 0.4 collective-permute-start
  3.1 3.3 %collective-permute-start.4 = (bf16[256,256]{1,0:T(8,128)(2,1)}, bf16[256,256]{1,0:T(8,128)(2,1)S(1)}, u32[]{:S(2)}, u32[]{:S(2)}) collective-permute-start(bf16[256,256]{1,0:T(8,128)(2,1)} %get-tuple-element.49.kv0), channel_id=1, source_target_pairs={{0,192},{32,224},{64,0},{96,32},{1,193},{33,225},{65,1},{97,33},{2... | collective-permute-start | bytes 393224 | tf_op jit(solution)/shard_map/ppermute | solution.py:412
  6.4 0.7 collective-permute-start.3
  7.1 3.8 %collective-permute-start.2 = (bf16[256,256]{1,0:T(8,128)(2,1)}, bf16[256,256]{1,0:T(8,128)(2,1)S(1)}, u32[]{:S(2)}, u32[]{:S(2)}) collective-permute-start(bf16[256,256]{1,0:T(8,128)(2,1)} %get-tuple-element.49.kv0), channel_id=1, source_target_pairs={{0,64},{32,96},{64,128},{96,160},{128,192},{160,224},{1,65},{33,97... | collective-permute-start | bytes 393224 | tf_op jit(solution)/shard_map/ppermute | solution.py:408
  10.9 0.0 collective-permute-done.5.qg1
  10.9 2.9 %collective-permute-start.1 = (bf16[256,256]{1,0:T(8,128)(2,1)}, bf16[256,256]{1,0:T(8,128)(2,1)S(1)}, u32[]{:S(2)}, u32[]{:S(2)}) collective-permute-start(bf16[256,256]{1,0:T(8,128)(2,1)} %get-tuple-element.49.kv0), channel_id=1, source_target_pairs={{0,32},{32,64},{64,96},{96,128},{128,160},{160,192},{192,224},{1,3... | collective-permute-start | bytes 393224 | tf_op jit(solution)/shard_map/ppermute | solution.py:408
  13.8 0.1 pad_add_fusion.place_ref
  13.9 0.0 copy-start
  13.9 1.0 %copy-done = bf16[256,1024]{1,0:T(8,128)(2,1)S(1)} copy-done((bf16[256,1024]{1,0:T(8,128)(2,1)S(1)}, bf16[256,1024]{1,0:T(8,128)(2,1)}, u32[]{:S(2)}) %copy-start) | copy-done | bytes 524312
  14.9 0.0 copy-start.1
  14.9 0.9 copy-done.1
  15.8 0.0 copy-start.2
  15.8 0.7 copy-done.2
  16.5 2.0 %first_statistics.1 = (f32[3,16,256]{2,1,0:T(8,128)S(1)}, f32[6,16,256]{2,1,0:T(8,128)S(1)}, bf16[24,4,256,256]{3,2,1,0:T(8,128)(2,1)S(1)}, bf16[4,256,1024]{2,1,0:T(8,128)(2,1)S(1)}, bf16[6,256,256]{2,1,0:T(8,128)(2,1)S(1)}) custom-call(s32[2]{0:T(128)S(1)} %pad_add_fusion.place_ref, s32[17]{0:T(128)S(1)} %copy-done.2, bf16[256,1024]{1,0:T(8,128)(2,1)S(1)} %copy-done, ...), custom_call_target="tpu_custom_call" | custom-call | flops 1 | bytes 1 | tf_op jit(solution)/shard_map/first_statistics/pallas_call | solution.py:376
  18.5 0.0 collective-permute-done.4
  18.5 0.0 collective-permute-done.3.kv5
  18.5 0.0 collective-permute-done.2.kv2
  18.5 3.9 %collective-permute-done.1.kv1 = bf16[256,256]{1,0:T(8,128)(2,1)S(1)} collective-permute-done((bf16[256,256]{1,0:T(8,128)(2,1)}, bf16[256,256]{1,0:T(8,128)(2,1)S(1)}, u32[]{:S(2)}, u32[]{:S(2)}) %collective-permute-start.1) | collective-permute-done | bytes 131104 | tf_op jit(solution)/shard_map/ppermute | solution.py:408
  22.4 0.0 collective-permute-done.qg2
  22.4 0.1 collective-permute-start.6
  22.6 0.7 collective-permute-start.8
  23.2 2.3 %collective-permute-start.7 = (bf16[256,256]{1,0:T(8,128)(2,1)S(1)}, bf16[256,256]{1,0:T(8,128)(2,1)S(1)}, u32[]{:S(2)}, u32[]{:S(2)}) collective-permute-start(bf16[256,256]{1,0:T(8,128)(2,1)S(1)} %collective-permute-done.2.kv2), channel_id=1, source_target_pairs={{0,32},{32,64},{64,96},{96,128},{128,160},{160,192},{192,224},{1,3... | collective-permute-start | bytes 393224 | tf_op jit(solution)/shard_map/ppermute | solution.py:408
  25.5 0.8 here_statistics.1
  26.3 0.0 collective-permute-done.6.qg3
  26.3 0.8 there_statistics.1
  27.1 0.0 collective-permute-done.8.kv4
  27.1 4.9 %collective-permute-done.7.kv3 = bf16[256,256]{1,0:T(8,128)(2,1)S(1)} collective-permute-done((bf16[256,256]{1,0:T(8,128)(2,1)S(1)}, bf16[256,256]{1,0:T(8,128)(2,1)S(1)}, u32[]{:S(2)}, u32[]{:S(2)}) %collective-permute-start.7) | collective-permute-done | bytes 131104 | tf_op jit(solution)/shard_map/ppermute | solution.py:408
  32.0 0.0 copy-start.3
  32.0 0.8 far_statistics.1
  32.8 1.7 %collective-permute-start.10 = (f32[3,16,256]{2,1,0:T(8,128)S(1)}, f32[3,16,256]{2,1,0:T(8,128)S(1)}, u32[]{:S(2)}, u32[]{:S(2)}) collective-permute-start(f32[3,16,256]{2,1,0:T(8,128)S(1)} %get-tuple-element.69.st0), channel_id=1, source_target_pairs={{0,16},{16,0},{1,17},{17,1},{2,18},{18,2},{3,19},{19,3},{4,20},{20... | collective-permute-start | bytes 147464 | tf_op jit(solution)/shard_map/ppermute | solution.py:403
  34.5 0.0 collective-permute-start.9
  34.5 4.0 %collective-permute-done.10.st2 = f32[3,16,256]{2,1,0:T(8,128)S(1)} collective-permute-done((f32[3,16,256]{2,1,0:T(8,128)S(1)}, f32[3,16,256]{2,1,0:T(8,128)S(1)}, u32[]{:S(2)}, u32[]{:S(2)}) %collective-permute-start.10) | collective-permute-done | bytes 49184 | tf_op jit(solution)/shard_map/ppermute | solution.py:403
  38.5 0.0 collective-permute-start.11
  38.5 0.0 collective-permute-done.9.st1
  38.5 1.2 %collective-permute-done.11.st3 = f32[3,16,256]{2,1,0:T(8,128)S(1)} collective-permute-done((f32[3,16,256]{2,1,0:T(8,128)S(1)}, f32[3,16,256]{2,1,0:T(8,128)S(1)}, u32[]{:S(2)}, u32[]{:S(2)}) %collective-permute-start.11) | collective-permute-done | bytes 49184 | tf_op jit(solution)/shard_map/ppermute | solution.py:403
  39.7 0.0 copy-done.3
  39.7 1.6 %far_gradients.1 = (f32[16,128,256]{2,1,0:T(8,128)S(1)}, bf16[2,256,256]{2,1,0:T(8,128)(2,1)S(1)}, bf16[256,256]{1,0:T(8,128)(2,1)S(1)}, f32[256,256]{1,0:T(8,12...) custom-call(s32[2]{0:T(128)S(1)} %pad_add_fusion.place_ref, s32[17]{0:T(128)S(1)} %copy-done.3, ...), custom_call_target="tpu_custom_call" | custom-call | flops 1 | bytes 1 | tf_op jit(solution)/shard_map/far_gradients/pallas_call | solution.py:376
  41.3 3.3 %collective-permute-start.14 = (bf16[2,256,256]{2,1,0:T(8,128)(2,1)S(1)}, bf16[2,256,256]{2,1,0:T(8,128)(2,1)S(1)}, u32[]{:S(2)}, u32[]{:S(2)}) collective-permute-start(bf16[2,256,256]{2,1,0:T(8,128)(2,1)S(1)} %get-tuple-element.86), channel_id=1, source_target_pairs={{64,0},{96,32},{128,64},{160,96},{192,128},{224,160},{65,1},{97,33... | collective-permute-start | bytes 786440 | tf_op jit(solution)/shard_map/ppermute | solution.py:408
  44.6 1.3 %there_gradients.1 = (f32[16,128,256]{2,1,0:T(8,128)S(1)}, bf16[256,512]{1,0:T(8,128)(2,1)S(1)}, bf16[256,512]{1,0:T(8,128)(2,1)S(1)}, f32[2,256,256]{2,1,0:T(8,128)S(1)}) custom-call(s32[2]{0:T(128)S(1)} %pad_add_fusion.place_ref, s32[17]{0:T(128)S(1)} %copy-done.3, f32[16,128,256]{2,1,0:T(8,128)S(1)} %get-tuple-element.73.dqt_in, ...), custom_call_target="tpu_custom_call", output_to_operand_aliasing={{0}: (2, {})} | custom-call | flops 1 | bytes 1 | tf_op jit(solution)/shard_map/there_gradients/pallas_call | solution.py:376
  45.9 0.8 collective-permute-start.13
  46.7 2.2 %here_gradients.1 = (f32[16,128,256]{2,1,0:T(8,128)S(1)}, bf16[256,512]{1,0:T(8,128)(2,1)S(1)}, f32[256,256]{1,0:T(8,128)S(1)}, f32[256,256]{1,0:T(8,128)S(1)}, f32[256,256]{1,0:T(8,128)S(1)}) custom-call(s32[2]{0:T(128)S(1)} %pad_add_fusion.place_ref, s32[17]{0:T(128)S(1)} %copy-done.3, ...), custom_call_target="tpu_custom_call", output_to_operand_aliasing={{0}: (2, {})} | custom-call | flops 1 | bytes 1 | tf_op jit(solution)/shard_map/here_gradients/pallas_call | solution.py:376
  48.9 0.1 collective-permute-start.12
  49.0 5.0 %collective-permute-done.14 = bf16[2,256,256]{2,1,0:T(8,128)(2,1)S(1)} collective-permute-done((bf16[2,256,256]{2,1,0:T(8,128)(2,1)S(1)}, bf16[2,256,256]{2,1,0:T(8,128)(2,1)S(1)}, u32[]{:S(2)}, u32[]{:S(2)}) %collective-permute-start.14) | collective-permute-done | bytes 262176 | tf_op jit(solution)/shard_map/ppermute | solution.py:408
  54.0 0.1 fusion
  54.0 0.0 collective-permute-done.13.got
  54.1 0.1 pair.1
  54.1 4.3 %collective-permute-start.15 = (bf16[256,512]{1,0:T(8,128)(2,1)S(1)}, bf16[256,512]{1,0:T(8,128)(2,1)S(1)}, u32[]{:S(2)}, u32[]{:S(2)}) collective-permute-start(bf16[256,512]{1,0:T(8,128)(2,1)S(1)} %pair.1), channel_id=1, source_target_pairs={{0,16},{16,0},{1,17},{17,1},{2,18},{18,2},{3,19},{19,3},{4,20},{20... | collective-permute-start | bytes 786440 | tf_op jit(solution)/shard_map/ppermute | solution.py:403
  58.4 0.7 collective-permute-start.18
  59.1 7.0 %collective-permute-start.16 = (bf16[256,256]{1,0:T(8,128)(2,1)S(1)}, bf16[256,256]{1,0:T(8,128)(2,1)S(1)}, u32[]{:S(2)}, u32[]{:S(2)}) collective-permute-start(bf16[256,256]{1,0:T(8,128)(2,1)S(1)} %get-tuple-element.90), channel_id=1, source_target_pairs={{32,0},{64,32},{96,64},{128,96},{160,128},{192,160},{224,192},{33,... | collective-permute-start | bytes 393224 | tf_op jit(solution)/shard_map/ppermute | solution.py:408
  66.0 1.9 %collective-permute-start.17 = (bf16[256,256]{1,0:T(8,128)(2,1)S(1)}, bf16[256,256]{1,0:T(8,128)(2,1)S(1)}, u32[]{:S(2)}, u32[]{:S(2)}) collective-permute-start(bf16[256,256]{1,0:T(8,128)(2,1)S(1)} %get-tuple-element.91), channel_id=1, source_target_pairs={{64,0},{96,32},{128,64},{160,96},{192,128},{224,160},{65,1},{97,33... | collective-permute-start | bytes 393224 | tf_op jit(solution)/shard_map/ppermute | solution.py:408
  68.0 1.7 %own_gradients.1 = (f32[16,128,256]{2,1,0:T(8,128)S(1)}, bf16[256,512]{1,0:T(8,128)(2,1)S(1)}, f32[256,256]{1,0:T(8,128)S(1)}) custom-call(s32[2]{0:T(128)S(1)} %pad_add_fusion.place_ref, s32[17]{0:T(128)S(1)} %copy-done.3, f32[16,128,256]{2,1,0:T(8,128)S(1)} %get-tuple-element.79.dqt_in, ...), custom_call_target="tpu_custom_call", output_to_operand_aliasing={{0}: (2, {})} | custom-call | flops 1 | bytes 1 | tf_op jit(solution)/shard_map/own_gradients/pallas_call | solution.py:376
  69.6 0.0 collective-permute-done.18.got5
  69.6 0.0 collective-permute-done.12.beside
  69.6 5.9 %collective-permute-done.16.got1 = bf16[256,256]{1,0:T(8,128)(2,1)S(1)} collective-permute-done((bf16[256,256]{1,0:T(8,128)(2,1)S(1)}, bf16[256,256]{1,0:T(8,128)(2,1)S(1)}, u32[]{:S(2)}, u32[]{:S(2)}) %collective-permute-start.16) | collective-permute-done | bytes 131104 | tf_op jit(solution)/shard_map/ppermute | solution.py:408
  75.6 7.1 %collective-permute-done.17.got2 = bf16[256,256]{1,0:T(8,128)(2,1)S(1)} collective-permute-done((bf16[256,256]{1,0:T(8,128)(2,1)S(1)}, bf16[256,256]{1,0:T(8,128)(2,1)S(1)}, u32[]{:S(2)}, u32[]{:S(2)}) %collective-permute-start.17) | collective-permute-done | bytes 131104 | tf_op jit(solution)/shard_map/ppermute | solution.py:408
  82.7 0.0 collective-permute-done.15.across
  82.7 0.2 merge.1
  82.8 12.9 %all_to_all.5.got = bf16[8,32,768]{2,1,0:T(8,128)(2,1)S(1)} all-to-all(bf16[8,32,768]{2,1,0:T(8,128)(2,1)S(1)} %merge.1), channel_id=1, replica_groups=mesh['z'=8,'y'=2,'core'=2,'tp'=8] {'tp'}, dimensions={0} | all-to-all | bytes 786432 | tf_op jit(solution)/shard_map/all_to_all | solution.py:518
  95.7 0.8 finish.1
Async XLA Ops:
  2.6 8.3 %collective-permute-start.5 = (bf16[256,1024]{1,0:T(8,128)(2,1)}, bf16[256,1024]{1,0:T(8,128)(2,1)S(1)}, u32[]{:S(2)}, u32[]{:S(2)}) collective-permute-start(bf16[256,1024]{1,0:T(8,128)(2,1)} %get-tuple-element.48.qg0), channel_id=1, source_target_pairs={{0,8},{8,0},{1,9},{9,1},{2,10},{10,2},{3,11},{11,3},{4,12},{12,4},... | collective-permute-start | bytes 1572872 | tf_op jit(solution)/shard_map/ppermute | solution.py:403
  2.7 19.7 %collective-permute-start = (bf16[256,1024]{1,0:T(8,128)(2,1)}, bf16[256,1024]{1,0:T(8,128)(2,1)S(1)}, u32[]{:S(2)}, u32[]{:S(2)}) collective-permute-start(bf16[256,1024]{1,0:T(8,128)(2,1)} %get-tuple-element.48.qg0), channel_id=1, source_target_pairs={{0,16},{16,0},{1,17},{17,1},{2,18},{18,2},{3,19},{19,3},{4,20},{20... | collective-permute-start | bytes 1572872 | tf_op jit(solution)/shard_map/ppermute | solution.py:403
  3.1 15.4 %collective-permute-start.4 = (bf16[256,256]{1,0:T(8,128)(2,1)}, bf16[256,256]{1,0:T(8,128)(2,1)S(1)}, u32[]{:S(2)}, u32[]{:S(2)}) collective-permute-start(bf16[256,256]{1,0:T(8,128)(2,1)} %get-tuple-element.49.kv0), channel_id=1, source_target_pairs={{0,192},{32,224},{64,0},{96,32},{1,193},{33,225},{65,1},{97,33},{2... | collective-permute-start | bytes 393224 | tf_op jit(solution)/shard_map/ppermute | solution.py:412
  6.4 12.1 %collective-permute-start.3 = (bf16[256,256]{1,0:T(8,128)(2,1)}, bf16[256,256]{1,0:T(8,128)(2,1)S(1)}, u32[]{:S(2)}, u32[]{:S(2)}) collective-permute-start(bf16[256,256]{1,0:T(8,128)(2,1)} %get-tuple-element.49.kv0), channel_id=1, source_target_pairs={{24,184},{56,216},{88,248},{25,185},{57,217},{89,249},{26,186},{58... | collective-permute-start | bytes 393224 | tf_op jit(solution)/shard_map/ppermute | solution.py:420
  7.1 11.4 %collective-permute-start.2 = (bf16[256,256]{1,0:T(8,128)(2,1)}, bf16[256,256]{1,0:T(8,128)(2,1)S(1)}, u32[]{:S(2)}, u32[]{:S(2)}) collective-permute-start(bf16[256,256]{1,0:T(8,128)(2,1)} %get-tuple-element.49.kv0), channel_id=1, source_target_pairs={{0,64},{32,96},{64,128},{96,160},{128,192},{160,224},{1,65},{33,97... | collective-permute-start | bytes 393224 | tf_op jit(solution)/shard_map/ppermute | solution.py:408
  10.9 11.6 %collective-permute-start.1 = (bf16[256,256]{1,0:T(8,128)(2,1)}, bf16[256,256]{1,0:T(8,128)(2,1)S(1)}, u32[]{:S(2)}, u32[]{:S(2)}) collective-permute-start(bf16[256,256]{1,0:T(8,128)(2,1)} %get-tuple-element.49.kv0), channel_id=1, source_target_pairs={{0,32},{32,64},{64,96},{96,128},{128,160},{160,192},{192,224},{1,3... | collective-permute-start | bytes 393224 | tf_op jit(solution)/shard_map/ppermute | solution.py:408
  13.9 1.0 %copy-start = (bf16[256,1024]{1,0:T(8,128)(2,1)S(1)}, bf16[256,1024]{1,0:T(8,128)(2,1)}, u32[]{:S(2)}) copy-start(bf16[256,1024]{1,0:T(8,128)(2,1)} %get-tuple-element.48.qg0) | copy-start | bytes 1572868
  14.9 0.9 copy-start.1
  15.8 0.7 copy-start.2
  22.4 3.8 %collective-permute-start.6 = (bf16[256,1024]{1,0:T(8,128)(2,1)S(1)}, bf16[256,1024]{1,0:T(8,128)(2,1)S(1)}, u32[]{:S(2)}, u32[]{:S(2)}) collective-permute-start(bf16[256,1024]{1,0:T(8,128)(2,1)S(1)} %collective-permute-done.qg2), channel_id=1, source_target_pairs={{0,8},{8,0},{1,9},{9,1},{2,10},{10,2},{3,11},{11,3},{4,12},{12,4},... | collective-permute-start | bytes 1572872 | tf_op jit(solution)/shard_map/ppermute | solution.py:403
  22.6 4.5 %collective-permute-start.8 = (bf16[256,256]{1,0:T(8,128)(2,1)S(1)}, bf16[256,256]{1,0:T(8,128)(2,1)S(1)}, u32[]{:S(2)}, u32[]{:S(2)}) collective-permute-start(bf16[256,256]{1,0:T(8,128)(2,1)S(1)} %collective-permute-done.4), channel_id=1, source_target_pairs={{192,128},{224,160},{0,192},{32,224},{193,129},{225,161},{1,193},{... | collective-permute-start | bytes 393224 | tf_op jit(solution)/shard_map/ppermute | solution.py:412
  23.2 8.8 %collective-permute-start.7 = (bf16[256,256]{1,0:T(8,128)(2,1)S(1)}, bf16[256,256]{1,0:T(8,128)(2,1)S(1)}, u32[]{:S(2)}, u32[]{:S(2)}) collective-permute-start(bf16[256,256]{1,0:T(8,128)(2,1)S(1)} %collective-permute-done.2.kv2), channel_id=1, source_target_pairs={{0,32},{32,64},{64,96},{96,128},{128,160},{160,192},{192,224},{1,3... | collective-permute-start | bytes 393224 | tf_op jit(solution)/shard_map/ppermute | solution.py:408
  32.0 7.7 %copy-start.3 = (s32[17]{0:T(128)S(1)}, s32[17]{0:T(128)}, u32[]{:S(2)}) copy-start(s32[17]{0:T(128)} %doc_ref.15) | copy-start | bytes 208
  32.8 5.7 %collective-permute-start.10 = (f32[3,16,256]{2,1,0:T(8,128)S(1)}, f32[3,16,256]{2,1,0:T(8,128)S(1)}, u32[]{:S(2)}, u32[]{:S(2)}) collective-permute-start(f32[3,16,256]{2,1,0:T(8,128)S(1)} %get-tuple-element.69.st0), channel_id=1, source_target_pairs={{0,16},{16,0},{1,17},{17,1},{2,18},{18,2},{3,19},{19,3},{4,20},{20... | collective-permute-start | bytes 147464 | tf_op jit(solution)/shard_map/ppermute | solution.py:403
  34.5 4.0 %collective-permute-start.9 = (f32[3,16,256]{2,1,0:T(8,128)S(1)}, f32[3,16,256]{2,1,0:T(8,128)S(1)}, u32[]{:S(2)}, u32[]{:S(2)}) collective-permute-start(f32[3,16,256]{2,1,0:T(8,128)S(1)} %get-tuple-element.69.st0), channel_id=1, source_target_pairs={{0,8},{8,0},{1,9},{9,1},{2,10},{10,2},{3,11},{11,3},{4,12},{12,4},... | collective-permute-start | bytes 147464 | tf_op jit(solution)/shard_map/ppermute | solution.py:403
  38.5 1.2 %collective-permute-start.11 = (f32[3,16,256]{2,1,0:T(8,128)S(1)}, f32[3,16,256]{2,1,0:T(8,128)S(1)}, u32[]{:S(2)}, u32[]{:S(2)}) collective-permute-start(f32[3,16,256]{2,1,0:T(8,128)S(1)} %collective-permute-done.10.st2), channel_id=1, source_target_pairs={{0,8},{8,0},{1,9},{9,1},{2,10},{10,2},{3,11},{11,3},{4,12},{12,4},... | collective-permute-start | bytes 147464 | tf_op jit(solution)/shard_map/ppermute | solution.py:403
  41.3 12.7 %collective-permute-start.14 = (bf16[2,256,256]{2,1,0:T(8,128)(2,1)S(1)}, bf16[2,256,256]{2,1,0:T(8,128)(2,1)S(1)}, u32[]{:S(2)}, u32[]{:S(2)}) collective-permute-start(bf16[2,256,256]{2,1,0:T(8,128)(2,1)S(1)} %get-tuple-element.86), channel_id=1, source_target_pairs={{64,0},{96,32},{128,64},{160,96},{192,128},{224,160},{65,1},{97,33... | collective-permute-start | bytes 786440 | tf_op jit(solution)/shard_map/ppermute | solution.py:408
  45.9 8.2 %collective-permute-start.13 = (bf16[256,512]{1,0:T(8,128)(2,1)S(1)}, bf16[256,512]{1,0:T(8,128)(2,1)S(1)}, u32[]{:S(2)}, u32[]{:S(2)}) collective-permute-start(bf16[256,512]{1,0:T(8,128)(2,1)S(1)} %get-tuple-element.84), channel_id=1, source_target_pairs={{0,8},{8,0},{1,9},{9,1},{2,10},{10,2},{3,11},{11,3},{4,12},{12,4},... | collective-permute-start | bytes 786440 | tf_op jit(solution)/shard_map/ppermute | solution.py:403
  48.9 20.8 %collective-permute-start.12 = (bf16[256,512]{1,0:T(8,128)(2,1)S(1)}, bf16[256,512]{1,0:T(8,128)(2,1)S(1)}, u32[]{:S(2)}, u32[]{:S(2)}) collective-permute-start(bf16[256,512]{1,0:T(8,128)(2,1)S(1)} %get-tuple-element.82), channel_id=1, source_target_pairs={{0,8},{8,0},{1,9},{9,1},{2,10},{10,2},{3,11},{11,3},{4,12},{12,4},... | collective-permute-start | bytes 786440 | tf_op jit(solution)/shard_map/ppermute | solution.py:403
  54.1 28.6 %collective-permute-start.15 = (bf16[256,512]{1,0:T(8,128)(2,1)S(1)}, bf16[256,512]{1,0:T(8,128)(2,1)S(1)}, u32[]{:S(2)}, u32[]{:S(2)}) collective-permute-start(bf16[256,512]{1,0:T(8,128)(2,1)S(1)} %pair.1), channel_id=1, source_target_pairs={{0,16},{16,0},{1,17},{17,1},{2,18},{18,2},{3,19},{19,3},{4,20},{20... | collective-permute-start | bytes 786440 | tf_op jit(solution)/shard_map/ppermute | solution.py:403
  58.4 11.2 %collective-permute-start.18 = (bf16[256,256]{1,0:T(8,128)(2,1)S(1)}, bf16[256,256]{1,0:T(8,128)(2,1)S(1)}, u32[]{:S(2)}, u32[]{:S(2)}) collective-permute-start(bf16[256,256]{1,0:T(8,128)(2,1)S(1)} %get-tuple-element.92), channel_id=1, source_target_pairs={{184,24},{216,56},{248,88},{185,25},{217,57},{249,89},{186,26},{21... | collective-permute-start | bytes 393224 | tf_op jit(solution)/shard_map/ppermute | solution.py:420
  59.1 16.5 %collective-permute-start.16 = (bf16[256,256]{1,0:T(8,128)(2,1)S(1)}, bf16[256,256]{1,0:T(8,128)(2,1)S(1)}, u32[]{:S(2)}, u32[]{:S(2)}) collective-permute-start(bf16[256,256]{1,0:T(8,128)(2,1)S(1)} %get-tuple-element.90), channel_id=1, source_target_pairs={{32,0},{64,32},{96,64},{128,96},{160,128},{192,160},{224,192},{33,... | collective-permute-start | bytes 393224 | tf_op jit(solution)/shard_map/ppermute | solution.py:408
  66.0 16.7 %collective-permute-start.17 = (bf16[256,256]{1,0:T(8,128)(2,1)S(1)}, bf16[256,256]{1,0:T(8,128)(2,1)S(1)}, u32[]{:S(2)}, u32[]{:S(2)}) collective-permute-start(bf16[256,256]{1,0:T(8,128)(2,1)S(1)} %get-tuple-element.91), channel_id=1, source_target_pairs={{64,0},{96,32},{128,64},{160,96},{192,128},{224,160},{65,1},{97,33... | collective-permute-start | bytes 393224 | tf_op jit(solution)/shard_map/ppermute | solution.py:408

commit v2 on v1

--- a/solution.py
+++ b/solution.py
@@ -45,13 +45,18 @@
     return starts
 
 
-def step_ranges(place_ref, doc_ref, steps_ref):
+def find_starts(place_ref, doc_ref, starts_ref, ranges_ref):
     z, j = place_ref[0], place_ref[1]
     for rel in range(SLAB):
         qb = j ^ rel
         first = start_of(doc_ref, (SLAB * z + qb) * ROWS) // ROWS
-        steps_ref[2 * rel] = jnp.where(j <= qb, 0, 1)
-        steps_ref[2 * rel + 1] = z - jnp.maximum((first - j + SLAB - 1) >> 2, 0)
+        ranges_ref[2 * rel] = jnp.where(j <= qb, 0, 1)
+        ranges_ref[2 * rel + 1] = z - jnp.maximum((first - j + SLAB - 1) >> 2, 0)
+        starts_ref[rel : rel + 1, :] = start_of(doc_ref, query_positions(z, qb))
+
+
+def query_positions(z, qb):
+    return (SLAB * z + qb) * ROWS + lax.broadcasted_iota(jnp.int32, (1, ROWS), 1)
 
 
 def pack_kernel(q_ref, g_ref, k_ref, v_ref, qg_ref, kv_ref, sems):
@@ -68,14 +73,14 @@
         copy.wait()
 
 
-def stats_steps(place_ref, doc_ref, rels, steps, fresh, qg, kv, tops, weights, out_ref, ranges):
+def stats_steps(place_ref, where, rels, steps, fresh, qg, kv, tops, weights, out_ref):
     z, j = place_ref[0], place_ref[1]
-    step_ranges(place_ref, doc_ref, ranges)
+    ranges, starts_ref = where
 
     def per_block(rel, _):
         qb = j ^ rel
-        positions = (SLAB * z + qb) * ROWS + lax.broadcasted_iota(jnp.int32, (1, ROWS), 1)
-        starts = start_of(doc_ref, positions)
+        positions = query_positions(z, qb)
+        starts = starts_ref[pl.ds(rel, 1), :]
 
         def per_step(k, carry):
             key_pos = lax.broadcasted_iota(jnp.int32, (ROWS, ROWS), 0)
@@ -130,48 +135,51 @@
 
 
 def first_stats_kernel(
-    place_ref, doc_ref, qg0, qg1, kv0, out_ref, tops, weights, qg_all, kv_all, ranges
-):
+    place_ref, doc_ref, qg0, qg1, kv0, ranges, starts, out_ref, tops, weights, qg_all, kv_all
+):
+    find_starts(place_ref, doc_ref, starts, ranges)
     qg_all[0] = qg0[...]
     qg_all[1] = qg1[...]
     kv_all[0] = kv0[...]
     stats_steps(
-        place_ref, doc_ref, HERE, (0, 1), True, qg_all, kv_all, tops, weights, out_ref, ranges
+        place_ref, (ranges, starts), HERE, (0, 1), True, qg_all, kv_all, tops, weights, out_ref
     )
 
 
 def here_stats_kernel(
-    place_ref, doc_ref, in0, in1, in2, in3, qg_all, kv1, kv2, out_ref, tops, weights, kv_all, ranges
+    place_ref, ranges, in0, in1, in2, in3, starts, qg_all, kv1, kv2, out_ref, tops, weights, kv_all
 ):
     del in0, in1, in2, in3
     kv_all[1] = kv1[...]
     kv_all[2] = kv2[...]
     stats_steps(
-        place_ref, doc_ref, HERE, (1, HALF), False, qg_all, kv_all, tops, weights, out_ref, ranges
+        place_ref, (ranges, starts), HERE, (1, HALF), False,
+        qg_all, kv_all, tops, weights, out_ref,
     )
 
 
 def there_stats_kernel(
-    place_ref, doc_ref, in0, in1, in2, in3, kv_all, qg2, qg3, out_ref, tops, weights, qg_all, ranges
+    place_ref, ranges, in0, in1, in2, in3, starts, kv_all, qg2, qg3, out_ref, tops, weights, qg_all
 ):
     del in0, in1, in2, in3
     qg_all[2] = qg2[...]
     qg_all[3] = qg3[...]
     stats_steps(
-        place_ref, doc_ref, THERE, (0, HALF), True, qg_all, kv_all, tops, weights, out_ref, ranges
+        place_ref, (ranges, starts), THERE, (0, HALF), True,
+        qg_all, kv_all, tops, weights, out_ref,
     )
 
 
 def far_stats_kernel(
-    place_ref, doc_ref, in0, in1, in2, in3, qg_all, kv3, kv4, kv5,
-    out_ref, tops, weights, kv_all, ranges,
+    place_ref, ranges, in0, in1, in2, in3, starts, qg_all, kv3, kv4, kv5,
+    out_ref, tops, weights, kv_all,
 ):
     del in0, in1, in2, in3
     for slot, ref in enumerate((kv3, kv4, kv5)):
         kv_all[HALF + slot] = ref[...]
     stats_steps(
-        place_ref, doc_ref, (0, SLAB), (HALF, REACH + 1), False,
-        qg_all, kv_all, tops, weights, out_ref, ranges,
+        place_ref, (ranges, starts), (0, SLAB), (HALF, REACH + 1), False,
+        qg_all, kv_all, tops, weights, out_ref,
     )
 
 
@@ -192,7 +200,7 @@
 
 def visit_step(j, k, rels, ranges, data, dqt, acc):
     lse_buf, delta_buf, tops, weights, qg_all, kv_all = data
-    keys_t = kv_all[k, :, :HD].astype(F32).T.astype(BF16)
+    keys_t = kv_all[k, :, :HD].T
 
     def per_block(rel, _):
         qb = j ^ rel
@@ -232,8 +240,8 @@
 
 def write_dq(dqt, slot, out_ref):
     for h in range(GROUP):
-        dq = dqt[slot * GROUP + h].T * SCALE
-        out_ref[:, h * HD : (h + 1) * HD] = dq.astype(BF16)
+        dq = (dqt[slot * GROUP + h] * SCALE).astype(BF16)
+        out_ref[:, h * HD : (h + 1) * HD] = dq.T
 
 
 def write_dkv(out_ref, acc):
@@ -242,10 +250,9 @@
 
 
 def far_kernel(
-    place_ref, doc_ref, st0, st1, st2, st3, tops, weights, qg_all, kv_all,
-    dqt, dkv34, dkv5, acc0_ref, lse_ref, delta_ref, acc, ranges,
-):
-    step_ranges(place_ref, doc_ref, ranges)
+    place_ref, ranges, st0, st1, st2, st3, tops, weights, qg_all, kv_all,
+    dqt, dkv3, dkv4, dkv5, acc0_ref, lse_ref, delta_ref, acc,
+):
     combine_stats((st0, st1, st2, st3), lse_ref, delta_ref)
     dqt[...] = jnp.zeros_like(dqt)
 
@@ -261,7 +268,7 @@
         def _():
             acc0_ref[...] = acc[...]
 
-        for slot, ref in enumerate((dkv5, dkv34.at[1], dkv34.at[0])):
+        for slot, ref in enumerate((dkv5, dkv4, dkv3)):
 
             @pl.when(step == slot + 1)
             def _():
@@ -273,11 +280,10 @@
 
 
 def there_kernel(
-    place_ref, doc_ref, dqt_in, lse_ref, delta_ref, tops, weights, qg_all, kv_all,
-    dqt, keep_ref, send_ref, acc_ref, acc, ranges,
+    place_ref, ranges, dqt_in, lse_ref, delta_ref, tops, weights, qg_all, kv_all,
+    dqt, keep_ref, send_ref, acc_ref, acc,
 ):
     del dqt_in
-    step_ranges(place_ref, doc_ref, ranges)
 
     def per_step(step, _):
         k = 2 - step
@@ -295,11 +301,10 @@
 
 
 def here_kernel(
-    place_ref, doc_ref, dqt_in, lse_ref, delta_ref, tops, weights, qg_all, kv_all, acc0, acc_near,
-    dqt, beside_ref, dkv1, dkv2, acc0_out, acc, ranges,
+    place_ref, ranges, dqt_in, lse_ref, delta_ref, tops, weights, qg_all, kv_all, acc0, acc_near,
+    dqt, beside_ref, dkv1, dkv2, acc0_out, acc,
 ):
     del dqt_in
-    step_ranges(place_ref, doc_ref, ranges)
 
     def per_step(step, _):
         k = 2 - step
@@ -333,11 +338,10 @@
 
 
 def own_kernel(
-    place_ref, doc_ref, dqt_in, lse_ref, delta_ref, tops, weights, qg_all, kv_all, acc0,
-    dqt, dq_ref, dkv_ref, acc, ranges,
+    place_ref, ranges, dqt_in, lse_ref, delta_ref, tops, weights, qg_all, kv_all, acc0,
+    dqt, dq_ref, dkv_ref, acc,
 ):
     del dqt_in
-    step_ranges(place_ref, doc_ref, ranges)
     acc[...] = acc0[...]
     visit_step(
         place_ref[1], jnp.int32(0), (0, 1), ranges,
@@ -351,10 +355,11 @@
     out_ref[...] = (keep[...].astype(F32) + got[...].astype(F32)).astype(BF16)
 
 
-def merge_kernel(keep, beside, across, dkv0, got1, got2, got5, out_ref):
+def merge_kernel(keep, beside, across, dkv0, got1, got2, got4, got5, out_ref):
     parts, part = out_ref.shape[:2]
     width = GROUP * HD
-    dkv = dkv0[...] + got1[...].astype(F32) + got2[...].astype(F32) + got5[...].astype(F32)
+    dkv = dkv0[...] + got1[...].astype(F32) + got2[...].astype(F32)
+    dkv = dkv + got4[...].astype(F32) + got5[...].astype(F32)
     dq = keep[...].astype(F32) + beside[...].astype(F32) + across[...].astype(F32)
     out_ref[:, :, :width] = dq.astype(BF16).reshape(parts, part, width)
     out_ref[:, :, width:] = dkv.astype(BF16).reshape(parts, part, 2 * HD)
@@ -372,14 +377,13 @@
 VMEM_SPEC = pl.BlockSpec(memory_space=pltpu.VMEM)
 
 
-def call(kernel, name, outs, scratch, *args, scalars=2, aliases=None, ranges=True):
+def call(kernel, name, outs, scratch, *args, scalars=2, aliases=None, smem_outs=0):
     return pl.pallas_call(
         kernel,
         out_shape=tuple(jax.ShapeDtypeStruct(shape, dtype) for shape, dtype in outs),
         in_specs=[SMEM_SPEC] * scalars + [VMEM_SPEC] * (len(args) - scalars),
-        out_specs=(VMEM_SPEC,) * len(outs),
-        scratch_shapes=[pltpu.VMEM(shape, dtype) for shape, dtype in scratch]
-        + [pltpu.SMEM((2 * SLAB,), jnp.int32)] * ranges,
+        out_specs=(SMEM_SPEC,) * smem_outs + (VMEM_SPEC,) * (len(outs) - smem_outs),
+        scratch_shapes=[pltpu.VMEM(shape, dtype) for shape, dtype in scratch],
         input_output_aliases=aliases or {},
         compiler_params=pltpu.CompilerParams(vmem_limit_bytes=VMEM_LIMIT),
         cost_estimate=pl.CostEstimate(flops=1, bytes_accessed=1, transcendentals=0),
@@ -392,6 +396,8 @@
 STATS = ((3, SLAB * GROUP, ROWS), F32)
 TOPS = ((REACH + 1, SLAB * GROUP, ROWS), F32)
 WEIGHTS = ((SLAB * (REACH + 1), GROUP, ROWS, ROWS), BF16)
+RANGES = ((2 * SLAB,), jnp.int32)
+STARTS = ((2 * SLAB, ROWS), jnp.int32)
 ROW_STATS = ((SLAB * GROUP, ROWS), F32)
 DQT = ((SLAB * GROUP, HD, ROWS), F32)
 ACC = ((ROWS, 2 * HD), F32)
@@ -410,6 +416,16 @@
 
 def wrapped(x, by, sources, slabs):
     return lax.ppermute(x, "z", [(i, (i + by) % slabs) for i in sources])
+
+
+def crossed(x, by, slabs):
+    pairs = [
+        (i * SLAB + at, (i + by) * SLAB + (at ^ 1))
+        for i in range(slabs)
+        if 0 <= i + by < slabs
+        for at in range(SLAB)
+    ]
+    return flip(lax.ppermute(x, ("z", "y", "core"), pairs), "core")
 
 
 def shift_last(x, by, slabs):
@@ -440,36 +456,37 @@
         name="pack",
     )(queries, grad_out, keys, values)
     across = flip(qg, "y")
+    ahead = [i for i in range(slabs) if i + 4 < slabs]
+    kv_by = wrapped(kv, -2, ahead, slabs)
+    kv5 = shift_last(kv, 5, slabs)
     kv1 = shift(kv, 1, slabs)
     kv2 = shift(kv, 2, slabs)
     beside = flip(qg, "core")
-    kv5 = shift_last(kv, 5, slabs)
-    ahead = [i for i in range(slabs) if i + 4 < slabs]
-    kv_by = wrapped(kv, -2, ahead, slabs)
-
-    stats, tops, weights, qg_all, kv_all = call(
-        first_stats_kernel, "first_statistics", [STATS, TOPS, WEIGHTS, QG_ALL, KV_ALL], [],
-        place, doc_lengths, qg, beside, kv,
-    )
-    across, kv1, kv2, kv5, kv_by, stats = lax.optimization_barrier(
-        (across, kv1, kv2, kv5, kv_by, stats)
+
+    ranges, starts, stats, tops, weights, qg_all, kv_all = call(
+        first_stats_kernel, "first_statistics",
+        [RANGES, STARTS, STATS, TOPS, WEIGHTS, QG_ALL, KV_ALL], [],
+        place, doc_lengths, qg, beside, kv, smem_outs=1,
+    )
+    across, kv_by, kv5, kv1, kv2, stats = lax.optimization_barrier(
+        (across, kv_by, kv5, kv1, kv2, stats)
     )
     kv3 = shift(kv2, 1, slabs)
     kv4 = wrapped(kv_by, -2, [(i - 2) % slabs for i in ahead], slabs)
     both = flip(across, "core")
     stats, tops, weights, kv_all = call(
         here_stats_kernel, "here_statistics", [STATS, TOPS, WEIGHTS, KV_ALL], [],
-        place, doc_lengths, stats, tops, weights, kv_all, qg_all, kv1, kv2,
+        place, ranges, stats, tops, weights, kv_all, starts, qg_all, kv1, kv2,
         aliases={2: 0, 3: 1, 4: 2, 5: 3},
     )
     stats, tops, weights, qg_all = call(
         there_stats_kernel, "there_statistics", [STATS, TOPS, WEIGHTS, QG_ALL], [],
-        place, doc_lengths, stats, tops, weights, qg_all, kv_all, across, both,
+        place, ranges, stats, tops, weights, qg_all, starts, kv_all, across, both,
         aliases={2: 0, 3: 1, 4: 2, 5: 3},
     )
     stats, tops, weights, kv_all = call(
         far_stats_kernel, "far_statistics", [STATS, TOPS, WEIGHTS, KV_ALL], [],
-        place, doc_lengths, stats, tops, weights, kv_all, qg_all, kv3, kv4, kv5,
+        place, ranges, stats, tops, weights, kv_all, starts, qg_all, kv3, kv4, kv5,
         aliases={2: 0, 3: 1, 4: 2, 5: 3},
     )
     stats_y = flip(stats, "y")
@@ -477,27 +494,26 @@
     stats_yc = flip(stats_y, "core")
 
     data = (tops, weights, qg_all, kv_all)
-    dqt, dkv34, dkv5, acc0, lse, delta = call(
-        far_kernel, "far_gradients",
-        [DQT, ((2,) + DKV[0], BF16), DKV, ACC, ROW_STATS, ROW_STATS], [ACC],
-        place, doc_lengths, stats, stats_c, stats_y, stats_yc, *data,
-    )
-    got_far = shift(dkv34, -2, slabs)
+    dqt, dkv3, dkv4, dkv5, acc0, lse, delta = call(
+        far_kernel, "far_gradients", [DQT, DKV, DKV, DKV, ACC, ROW_STATS, ROW_STATS], [ACC],
+        place, ranges, stats, stats_c, stats_y, stats_yc, *data,
+    )
+    got3 = shift(dkv3, -2, slabs)
+    got4 = crossed(dkv4, -4, slabs)
     got5 = shift_last(dkv5, -5, slabs)
     dqt, there_keep, there_send, acc_near = call(
         there_kernel, "there_gradients", [DQT, DQ, DQ, ((2,) + ACC[0], F32)], [ACC],
-        place, doc_lengths, dqt, lse, delta, *data, aliases={2: 0},
+        place, ranges, dqt, lse, delta, *data, aliases={2: 0},
     )
     there_got = flip(there_send, "core")
     dqt, dq_beside, dkv1, dkv2, acc0 = call(
-        here_kernel, "here_gradients", [DQT, DQ, ACC, ACC, ACC], [ACC],
-        place, doc_lengths, dqt, lse, delta, *data, acc0, acc_near, aliases={2: 0},
-    )
-    dkv1 = (dkv1 + got_far[0].astype(F32)).astype(BF16)
-    dkv2 = (dkv2 + got_far[1].astype(F32)).astype(BF16)
-    there_got, dkv1, dkv2 = lax.optimization_barrier((there_got, dkv1, dkv2))
+        here_kernel, "here_gradients", [DQT, DQ, ACC, DKV, ACC], [ACC],
+        place, ranges, dqt, lse, delta, *data, acc0, acc_near, aliases={2: 0},
+    )
+    dkv1 = (dkv1 + got3.astype(F32)).astype(BF16)
+    there_got, dkv1 = lax.optimization_barrier((there_got, dkv1))
     dq_pair, = call(
-        pair_kernel, "pair", [DQ], [], there_keep, there_got, scalars=0, ranges=False
+        pair_kernel, "pair", [DQ], [], there_keep, there_got, scalars=0
     )
     dq_across = flip(dq_pair, "y")
     dq_beside = flip(dq_beside, "core")
@@ -505,7 +521,7 @@
     got1 = shift(dkv1, -1, slabs)
     _, dq_keep, dkv0 = call(
         own_kernel, "own_gradients", [DQT, DQ, ACC], [ACC],
-        place, doc_lengths, dqt, lse, delta, *data, acc0, aliases={2: 0},
+        place, ranges, dqt, lse, delta, *data, acc0, aliases={2: 0},
     )
 
     tp = lax.axis_size("tp")
@@ -513,13 +529,13 @@
     width = GROUP * HD
     whole, = call(
         merge_kernel, "merge", [((tp, part, width + 2 * HD), BF16)], [],
-        dq_keep, dq_beside, dq_across, dkv0, got1, got2, got5, scalars=0, ranges=False,
+        dq_keep, dq_beside, dq_across, dkv0, got1, got2, got4, got5, scalars=0,
     )
     got = lax.all_to_all(whole, "tp", split_axis=0, concat_axis=0, tiled=True)
     return call(
         finish_kernel, "finish",
         [((part, tp * width), BF16), ((part, tp * HD), BF16), ((part, tp * HD), BF16)], [],
-        got, scalars=0, ranges=False,
+        got, scalars=0,
     )
 
 

time: 98.5 us -> 93.1 us (0.945)
  the two profiles are of different devices: /device:TPU:80 before, /device:TPU:192 now
where the time goes in v2:
time: 93.1 us; the launch traced here: 92.9 us
  starting transfers between devices  35.9 us (39%)
  Pallas kernels  27.4 us (29%)
  blocking collectives  13.7 us (15%)
  waiting for transfers between devices  12.4 us (13%)
  local copies, waits for them, and re-layouts  2.6 us (3%)
    pallas_call x11, Pallas kernels, call(): pl.pallas_call(kernel, out_shape=tuple((jax.ShapeDtypeStruct(shape, dtype...  25.4 us
    ppermute x10, starting transfers between devices, flip(): return lax.ppermute(x, axis, [(0, 1), (1, 0)])  15.8 us
    all_to_all x1, blocking collectives, local(): got = lax.all_to_all(whole, 'tp', split_axis=0, concat_axis=0, tiled=True)  13.7 us
    ppermute x6, starting transfers between devices, shift(): return lax.ppermute(x, 'z', pairs)  12.3 us
    ppermute x6, waiting for transfers between devices, shift(): return lax.ppermute(x, 'z', pairs)  10.3 us
    ppermute x2, starting transfers between devices, wrapped(): return lax.ppermute(x, 'z', [(i, (i + by) % slabs) for i in sources])  5.19 us
    unnamed x6, local copies, waits for them, and re-layouts  2.6 us
    pallas_call x1, Pallas kernels, local(): pl.pallas_call(pack_kernel, out_shape=(jax.ShapeDtypeStruct((ROWS, 2 * GR...  1.97 us
  transfers between devices with their start and end apart: 21, of which 7 were waited for; matrix products, arithmetic and copies ran while one was open for 0% of the time, Pallas kernels for 22%

profile of v2, /device:TPU:192, one launch (start us, length us, event | category | flops | bytes accessed | tf_op | source)
XLA Modules:
  0.0 92.9 jit_solution(147835951322237178)
XLA Ops:
  0.6 2.0 %pack.1 = (bf16[256,1024]{1,0:T(8,128)(2,1)}, bf16[256,256]{1,0:T(8,128)(2,1)}) custom-call(bf16[256,512]{1,0:T(8,128)(2,1)} %q_ref.1, bf16[256,512]{1,0:T(8,128)(2,1)} %g_ref.1, bf16[256,128]{1,0:T(8,128)(2,1)} %k_ref.1, bf16[256,128]{1,0:T(8,128)(2,1)} %v_ref.1), custom_call_target="tpu_custom_call" | custom-call | flops 1 | bytes 1 | tf_op jit(solution)/shard_map/pack/pallas_call | solution.py:445
  2.6 0.1 collective-permute-start
  2.7 3.3 %collective-permute-start.1 = (bf16[256,1024]{1,0:T(8,128)(2,1)}, bf16[256,1024]{1,0:T(8,128)(2,1)S(1)}, u32[]{:S(2)}, u32[]{:S(2)}) collective-permute-start(bf16[256,1024]{1,0:T(8,128)(2,1)} %get-tuple-element.50.qg0), channel_id=1, source_target_pairs={{0,16},{16,0},{1,17},{17,1},{2,18},{18,2},{3,19},{19,3},{4,20},{20... | collective-permute-start | bytes 1572872 | tf_op jit(solution)/shard_map/ppermute | solution.py:409
  6.0 1.3 %collective-permute-start.5 = (bf16[256,256]{1,0:T(8,128)(2,1)}, bf16[256,256]{1,0:T(8,128)(2,1)S(1)}, u32[]{:S(2)}, u32[]{:S(2)}) collective-permute-start(bf16[256,256]{1,0:T(8,128)(2,1)} %get-tuple-element.51.kv0), channel_id=1, source_target_pairs={{0,64},{32,96},{64,128},{96,160},{128,192},{160,224},{1,65},{33,97... | collective-permute-start | bytes 393224 | tf_op jit(solution)/shard_map/ppermute | solution.py:414
  7.3 2.9 %collective-permute-start.4 = (bf16[256,256]{1,0:T(8,128)(2,1)}, bf16[256,256]{1,0:T(8,128)(2,1)S(1)}, u32[]{:S(2)}, u32[]{:S(2)}) collective-permute-start(bf16[256,256]{1,0:T(8,128)(2,1)} %get-tuple-element.51.kv0), channel_id=1, source_target_pairs={{0,32},{32,64},{64,96},{96,128},{128,160},{160,192},{192,224},{1,3... | collective-permute-start | bytes 393224 | tf_op jit(solution)/shard_map/ppermute | solution.py:414
  10.2 0.7 collective-permute-start.3
  10.9 0.0 collective-permute-done.qg1
  10.9 1.3 %collective-permute-start.2 = (bf16[256,256]{1,0:T(8,128)(2,1)}, bf16[256,256]{1,0:T(8,128)(2,1)S(1)}, u32[]{:S(2)}, u32[]{:S(2)}) collective-permute-start(bf16[256,256]{1,0:T(8,128)(2,1)} %get-tuple-element.51.kv0), channel_id=1, source_target_pairs={{0,192},{32,224},{64,0},{96,32},{1,193},{33,225},{65,1},{97,33},{2... | collective-permute-start | bytes 393224 | tf_op jit(solution)/shard_map/ppermute | solution.py:418
  12.2 0.1 pad_add_fusion.place_ref
  12.3 0.0 copy-start
  12.3 1.0 %copy-done = bf16[256,1024]{1,0:T(8,128)(2,1)S(1)} copy-done((bf16[256,1024]{1,0:T(8,128)(2,1)S(1)}, bf16[256,1024]{1,0:T(8,128)(2,1)}, u32[]{:S(2)}) %copy-start) | copy-done | bytes 524312
  13.3 0.0 copy-start.1
  13.3 0.9 copy-done.1
  14.2 0.0 copy-start.2
  14.2 0.7 copy-done.2
  14.9 2.6 %first_statistics.1 = (s32[8]{0:T(128)S(1)}, s32[8,256]{1,0:T(8,128)S(1)}, f32[3,16,256]{2,1,0:T(8,128)S(1)}, f32[6,16,256]{2,1,0:T(8,128)S(1)}, bf16[24,4,256,2...) custom-call(s32[2]{0:T(128)S(1)} %pad_add_fusion.place_ref, ...), custom_call_target="tpu_custom_call" | custom-call | flops 1 | bytes 1 | tf_op jit(solution)/shard_map/first_statistics/pallas_call | solution.py:381
  17.5 0.6 collective-permute-done.5.kv2
  18.0 1.7 %collective-permute-done.4.kv1 = bf16[256,256]{1,0:T(8,128)(2,1)S(1)} collective-permute-done((bf16[256,256]{1,0:T(8,128)(2,1)}, bf16[256,256]{1,0:T(8,128)(2,1)S(1)}, u32[]{:S(2)}, u32[]{:S(2)}) %collective-permute-start.4) | collective-permute-done | bytes 131104 | tf_op jit(solution)/shard_map/ppermute | solution.py:414
  19.7 0.0 collective-permute-done.3.kv5
  19.7 0.8 collective-permute-done.2
  20.5 0.0 collective-permute-done.1.qg2
  20.5 0.0 collective-permute-start.6
  20.5 3.9 %collective-permute-start.8 = (bf16[256,256]{1,0:T(8,128)(2,1)S(1)}, bf16[256,256]{1,0:T(8,128)(2,1)S(1)}, u32[]{:S(2)}, u32[]{:S(2)}) collective-permute-start(bf16[256,256]{1,0:T(8,128)(2,1)S(1)} %collective-permute-done.2), channel_id=1, source_target_pairs={{192,128},{224,160},{0,192},{32,224},{193,129},{225,161},{1,193},{... | collective-permute-start | bytes 393224 | tf_op jit(solution)/shard_map/ppermute | solution.py:418
  24.4 3.6 %collective-permute-start.7 = (bf16[256,256]{1,0:T(8,128)(2,1)S(1)}, bf16[256,256]{1,0:T(8,128)(2,1)S(1)}, u32[]{:S(2)}, u32[]{:S(2)}) collective-permute-start(bf16[256,256]{1,0:T(8,128)(2,1)S(1)} %collective-permute-done.5.kv2), channel_id=1, source_target_pairs={{0,32},{32,64},{64,96},{96,128},{128,160},{160,192},{192,224},{1,3... | collective-permute-start | bytes 393224 | tf_op jit(solution)/shard_map/ppermute | solution.py:414
  28.0 3.1 %here_statistics.1 = (f32[3,16,256]{2,1,0:T(8,128)S(1)}, f32[6,16,256]{2,1,0:T(8,128)S(1)}, bf16[24,4,256,256]{3,2,1,0:T(8,128)(2,1)S(1)}, bf16[6,256,256]{2,1,0:T(8,128)(2,1)S(1)}) custom-call(s32[2]{0:T(128)S(1)} %pad_add_fusion.place_ref, s32[8]{0:T(128)S(1)} %get-tuple-element.52.ranges, ...), custom_call_target="tpu_custom_call", output_to_operand_aliasing={{0}: (2, {}), {1}: (3, {}), {2}: (4, {}), {3}: (5, {})} | custom-call | flops 1 | bytes 1 | tf_op jit(solution)/shard_map/here_statistics/pallas_call | solution.py:381
  31.1 0.0 collective-permute-done.6.qg3
  31.1 4.4 %there_statistics.1 = (f32[3,16,256]{2,1,0:T(8,128)S(1)}, f32[6,16,256]{2,1,0:T(8,128)S(1)}, bf16[24,4,256,256]{3,2,1,0:T(8,128)(2,1)S(1)}, bf16[4,256,1024]{2,1,0:T(8,128)(2,1)S(1)}) custom-call(s32[2]{0:T(128)S(1)} %pad_add_fusion.place_ref, ...), custom_call_target="tpu_custom_call", output_to_operand_aliasing={{0}: (2, {}), {1}: (3, {}), {2}: (4, {}), {3}: (5, {})} | custom-call | flops 1 | bytes 1 | tf_op jit(solution)/shard_map/there_statistics/pallas_call | solution.py:381
  35.4 0.0 collective-permute-done.8.kv4
  35.4 0.0 collective-permute-done.7.kv3
  35.4 0.7 far_statistics.1
  36.1 3.8 %collective-permute-start.10 = (f32[3,16,256]{2,1,0:T(8,128)S(1)}, f32[3,16,256]{2,1,0:T(8,128)S(1)}, u32[]{:S(2)}, u32[]{:S(2)}) collective-permute-start(f32[3,16,256]{2,1,0:T(8,128)S(1)} %get-tuple-element.73.st0), channel_id=1, source_target_pairs={{0,16},{16,0},{1,17},{17,1},{2,18},{18,2},{3,19},{19,3},{4,20},{20... | collective-permute-start | bytes 147464 | tf_op jit(solution)/shard_map/ppermute | solution.py:409
  40.0 1.7 %collective-permute-start.9 = (f32[3,16,256]{2,1,0:T(8,128)S(1)}, f32[3,16,256]{2,1,0:T(8,128)S(1)}, u32[]{:S(2)}, u32[]{:S(2)}) collective-permute-start(f32[3,16,256]{2,1,0:T(8,128)S(1)} %get-tuple-element.73.st0), channel_id=1, source_target_pairs={{0,8},{8,0},{1,9},{9,1},{2,10},{10,2},{3,11},{11,3},{4,12},{12,4},... | collective-permute-start | bytes 147464 | tf_op jit(solution)/shard_map/ppermute | solution.py:409
  41.7 0.4 collective-permute-done.10.st2
  42.0 1.1 %collective-permute-start.11 = (f32[3,16,256]{2,1,0:T(8,128)S(1)}, f32[3,16,256]{2,1,0:T(8,128)S(1)}, u32[]{:S(2)}, u32[]{:S(2)}) collective-permute-start(f32[3,16,256]{2,1,0:T(8,128)S(1)} %collective-permute-done.10.st2), channel_id=1, source_target_pairs={{0,8},{8,0},{1,9},{9,1},{2,10},{10,2},{3,11},{11,3},{4,12},{12,4},... | collective-permute-start | bytes 147464 | tf_op jit(solution)/shard_map/ppermute | solution.py:409
  43.1 0.0 collective-permute-done.9.st1
  43.1 0.9 collective-permute-done.11.st3
  44.0 2.9 %far_gradients.1 = (f32[16,128,256]{2,1,0:T(8,128)S(1)}, bf16[256,256]{1,0:T(8,128)(2,1)S(1)}, bf16[256,256]{1,0:T(8,128)(2,1)S(1)}, bf16[256,256]{1,0:T(8,128)(...) custom-call(s32[2]{0:T(128)S(1)} %pad_add_fusion.place_ref, ...), custom_call_target="tpu_custom_call" | custom-call | flops 1 | bytes 1 | tf_op jit(solution)/shard_map/far_gradients/pallas_call | solution.py:381
  47.0 1.3 %collective-permute-start.14 = (bf16[256,256]{1,0:T(8,128)(2,1)S(1)}, bf16[256,256]{1,0:T(8,128)(2,1)S(1)}, u32[]{:S(2)}, u32[]{:S(2)}) collective-permute-start(bf16[256,256]{1,0:T(8,128)(2,1)S(1)} %get-tuple-element.90), channel_id=1, source_target_pairs={{64,0},{96,32},{128,64},{160,96},{192,128},{224,160},{65,1},{97,33... | collective-permute-start | bytes 393224 | tf_op jit(solution)/shard_map/ppermute | solution.py:414
  48.3 4.2 %there_gradients.1 = (f32[16,128,256]{2,1,0:T(8,128)S(1)}, bf16[256,512]{1,0:T(8,128)(2,1)S(1)}, bf16[256,512]{1,0:T(8,128)(2,1)S(1)}, f32[2,256,256]{2,1,0:T(8,128)S(1)}) custom-call(s32[2]{0:T(128)S(1)} %pad_add_fusion.place_ref, s32[8]{0:T(128)S(1)} %get-tuple-element.52.ranges, ...), custom_call_target="tpu_custom_call", output_to_operand_aliasing={{0}: (2, {})} | custom-call | flops 1 | bytes 1 | tf_op jit(solution)/shard_map/there_gradients/pallas_call | solution.py:381
  52.4 0.5 collective-permute-start.13
  52.9 1.3 %collective-permute-start.18 = (bf16[256,256]{1,0:T(8,128)(2,1)S(1)}, bf16[256,256]{1,0:T(8,128)(2,1)S(1)}, u32[]{:S(2)}, u32[]{:S(2)}) collective-permute-start(bf16[256,256]{1,0:T(8,128)(2,1)S(1)} %get-tuple-element.95), channel_id=1, source_target_pairs={{128,8},{136,0},{144,24},{152,16},{160,40},{168,32},{176,56},{184,... | collective-permute-start | bytes 393224 | tf_op jit(solution)/shard_map/ppermute | solution.py:428
  54.2 0.7 collective-permute-start.20
  54.8 5.1 %here_gradients.1 = (f32[16,128,256]{2,1,0:T(8,128)S(1)}, bf16[256,512]{1,0:T(8,128)(2,1)S(1)}, f32[256,256]{1,0:T(8,128)S(1)}, bf16[256,256]{1,0:T(8,128)(2,1)S(1)}, f32[256,256]{1,0:T(8,128)S(1)}) custom-call(s32[2]{0:T(128)S(1)} %pad_add_fusion.place_ref, s32[8]{0:T(128)S(1)} %get-tuple-element.52.ranges, ...), custom_call_target="tpu_custom_call", output_to_operand_aliasing={{0}: (2, {})} | custom-call | flops 1 | bytes 1 | tf_op jit(solution)/shard_map/here_gradients/pallas_call | solution.py:381
  59.9 0.1 collective-permute-start.12
  60.0 0.0 collective-permute-done.14
  60.1 0.0 collective-permute-done.13.got
  60.1 0.1 pair.1
  60.2 4.9 %collective-permute-start.15 = (bf16[256,512]{1,0:T(8,128)(2,1)S(1)}, bf16[256,512]{1,0:T(8,128)(2,1)S(1)}, u32[]{:S(2)}, u32[]{:S(2)}) collective-permute-start(bf16[256,512]{1,0:T(8,128)(2,1)S(1)} %pair.1), channel_id=1, source_target_pairs={{0,16},{16,0},{1,17},{17,1},{2,18},{18,2},{3,19},{19,3},{4,20},{20... | collective-permute-start | bytes 786440 | tf_op jit(solution)/shard_map/ppermute | solution.py:409
  65.1 1.3 %collective-permute-start.17 = (bf16[256,256]{1,0:T(8,128)(2,1)S(1)}, bf16[256,256]{1,0:T(8,128)(2,1)S(1)}, u32[]{:S(2)}, u32[]{:S(2)}) collective-permute-start(bf16[256,256]{1,0:T(8,128)(2,1)S(1)} %get-tuple-element.94), channel_id=1, source_target_pairs={{64,0},{96,32},{128,64},{160,96},{192,128},{224,160},{65,1},{97,33... | collective-permute-start | bytes 393224 | tf_op jit(solution)/shard_map/ppermute | solution.py:414
  66.4 0.0 collective-permute-done.18
  66.4 0.3 collective-permute-start.19
  66.7 0.0 collective-permute-done.20.got5
  66.7 1.9 %collective-permute-start.16 = (bf16[256,256]{1,0:T(8,128)(2,1)S(1)}, bf16[256,256]{1,0:T(8,128)(2,1)S(1)}, u32[]{:S(2)}, u32[]{:S(2)}) collective-permute-start(bf16[256,256]{1,0:T(8,128)(2,1)S(1)} %add_convert_fusion), channel_id=1, source_target_pairs={{32,0},{64,32},{96,64},{128,96},{160,128},{192,160},{224,192},{33,... | collective-permute-start | bytes 393224 | tf_op jit(solution)/shard_map/ppermute | solution.py:414
  68.6 1.5 %own_gradients.1 = (f32[16,128,256]{2,1,0:T(8,128)S(1)}, bf16[256,512]{1,0:T(8,128)(2,1)S(1)}, f32[256,256]{1,0:T(8,128)S(1)}) custom-call(s32[2]{0:T(128)S(1)} %pad_add_fusion.place_ref, s32[8]{0:T(128)S(1)} %get-tuple-element.52.ranges, f32[16,128,256]{2,1,0:T(8,128)S(1)} %get-tuple-element.83.dqt_in, ...), custom_call_target="tpu_custom_call", output_to_operand_aliasing={{0}: (2, {})} | custom-call | flops 1 | bytes 1 | tf_op jit(solution)/shard_map/own_gradients/pallas_call | solution.py:381
  70.2 0.1 collective-permute-done.17.got2
  70.2 0.0 collective-permute-done.19.got4
  70.2 0.0 collective-permute-done.12.beside
  70.2 8.1 %collective-permute-done.16.got1 = bf16[256,256]{1,0:T(8,128)(2,1)S(1)} collective-permute-done((bf16[256,256]{1,0:T(8,128)(2,1)S(1)}, bf16[256,256]{1,0:T(8,128)(2,1)S(1)}, u32[]{:S(2)}, u32[]{:S(2)}) %collective-permute-start.16) | collective-permute-done | bytes 131104 | tf_op jit(solution)/shard_map/ppermute | solution.py:414
  78.3 0.0 collective-permute-done.15.across
  78.3 0.2 merge.1
  78.5 13.7 %all_to_all.5.got = bf16[8,32,768]{2,1,0:T(8,128)(2,1)S(1)} all-to-all(bf16[8,32,768]{2,1,0:T(8,128)(2,1)S(1)} %merge.1), channel_id=1, replica_groups=mesh['z'=8,'y'=2,'core'=2,'tp'=8] {'tp'}, dimensions={0} | all-to-all | bytes 786432 | tf_op jit(solution)/shard_map/all_to_all | solution.py:534
  92.1 0.8 finish.1
  (1 shorter events, 0.0 us)
Async XLA Ops:
  2.6 8.3 %collective-permute-start = (bf16[256,1024]{1,0:T(8,128)(2,1)}, bf16[256,1024]{1,0:T(8,128)(2,1)S(1)}, u32[]{:S(2)}, u32[]{:S(2)}) collective-permute-start(bf16[256,1024]{1,0:T(8,128)(2,1)} %get-tuple-element.50.qg0), channel_id=1, source_target_pairs={{0,8},{8,0},{1,9},{9,1},{2,10},{10,2},{3,11},{11,3},{4,12},{12,4},... | collective-permute-start | bytes 1572872 | tf_op jit(solution)/shard_map/ppermute | solution.py:409
  2.7 17.8 %collective-permute-start.1 = (bf16[256,1024]{1,0:T(8,128)(2,1)}, bf16[256,1024]{1,0:T(8,128)(2,1)S(1)}, u32[]{:S(2)}, u32[]{:S(2)}) collective-permute-start(bf16[256,1024]{1,0:T(8,128)(2,1)} %get-tuple-element.50.qg0), channel_id=1, source_target_pairs={{0,16},{16,0},{1,17},{17,1},{2,18},{18,2},{3,19},{19,3},{4,20},{20... | collective-permute-start | bytes 1572872 | tf_op jit(solution)/shard_map/ppermute | solution.py:409
  6.0 12.1 %collective-permute-start.5 = (bf16[256,256]{1,0:T(8,128)(2,1)}, bf16[256,256]{1,0:T(8,128)(2,1)S(1)}, u32[]{:S(2)}, u32[]{:S(2)}) collective-permute-start(bf16[256,256]{1,0:T(8,128)(2,1)} %get-tuple-element.51.kv0), channel_id=1, source_target_pairs={{0,64},{32,96},{64,128},{96,160},{128,192},{160,224},{1,65},{33,97... | collective-permute-start | bytes 393224 | tf_op jit(solution)/shard_map/ppermute | solution.py:414
  7.3 12.4 %collective-permute-start.4 = (bf16[256,256]{1,0:T(8,128)(2,1)}, bf16[256,256]{1,0:T(8,128)(2,1)S(1)}, u32[]{:S(2)}, u32[]{:S(2)}) collective-permute-start(bf16[256,256]{1,0:T(8,128)(2,1)} %get-tuple-element.51.kv0), channel_id=1, source_target_pairs={{0,32},{32,64},{64,96},{96,128},{128,160},{160,192},{192,224},{1,3... | collective-permute-start | bytes 393224 | tf_op jit(solution)/shard_map/ppermute | solution.py:414
  10.2 9.5 %collective-permute-start.3 = (bf16[256,256]{1,0:T(8,128)(2,1)}, bf16[256,256]{1,0:T(8,128)(2,1)S(1)}, u32[]{:S(2)}, u32[]{:S(2)}) collective-permute-start(bf16[256,256]{1,0:T(8,128)(2,1)} %get-tuple-element.51.kv0), channel_id=1, source_target_pairs={{24,184},{56,216},{88,248},{25,185},{57,217},{89,249},{26,186},{58... | collective-permute-start | bytes 393224 | tf_op jit(solution)/shard_map/ppermute | solution.py:436
  10.9 9.6 %collective-permute-start.2 = (bf16[256,256]{1,0:T(8,128)(2,1)}, bf16[256,256]{1,0:T(8,128)(2,1)S(1)}, u32[]{:S(2)}, u32[]{:S(2)}) collective-permute-start(bf16[256,256]{1,0:T(8,128)(2,1)} %get-tuple-element.51.kv0), channel_id=1, source_target_pairs={{0,192},{32,224},{64,0},{96,32},{1,193},{33,225},{65,1},{97,33},{2... | collective-permute-start | bytes 393224 | tf_op jit(solution)/shard_map/ppermute | solution.py:418
  12.3 1.0 %copy-start = (bf16[256,1024]{1,0:T(8,128)(2,1)S(1)}, bf16[256,1024]{1,0:T(8,128)(2,1)}, u32[]{:S(2)}) copy-start(bf16[256,1024]{1,0:T(8,128)(2,1)} %get-tuple-element.50.qg0) | copy-start | bytes 1572868
  13.3 0.9 copy-start.1
  14.2 0.7 copy-start.2
  20.5 10.6 %collective-permute-start.6 = (bf16[256,1024]{1,0:T(8,128)(2,1)S(1)}, bf16[256,1024]{1,0:T(8,128)(2,1)S(1)}, u32[]{:S(2)}, u32[]{:S(2)}) collective-permute-start(bf16[256,1024]{1,0:T(8,128)(2,1)S(1)} %collective-permute-done.1.qg2), channel_id=1, source_target_pairs={{0,8},{8,0},{1,9},{9,1},{2,10},{10,2},{3,11},{11,3},{4,12},{12,4},... | collective-permute-start | bytes 1572872 | tf_op jit(solution)/shard_map/ppermute | solution.py:409
  20.5 14.9 %collective-permute-start.8 = (bf16[256,256]{1,0:T(8,128)(2,1)S(1)}, bf16[256,256]{1,0:T(8,128)(2,1)S(1)}, u32[]{:S(2)}, u32[]{:S(2)}) collective-permute-start(bf16[256,256]{1,0:T(8,128)(2,1)S(1)} %collective-permute-done.2), channel_id=1, source_target_pairs={{192,128},{224,160},{0,192},{32,224},{193,129},{225,161},{1,193},{... | collective-permute-start | bytes 393224 | tf_op jit(solution)/shard_map/ppermute | solution.py:418
  24.4 11.0 %collective-permute-start.7 = (bf16[256,256]{1,0:T(8,128)(2,1)S(1)}, bf16[256,256]{1,0:T(8,128)(2,1)S(1)}, u32[]{:S(2)}, u32[]{:S(2)}) collective-permute-start(bf16[256,256]{1,0:T(8,128)(2,1)S(1)} %collective-permute-done.5.kv2), channel_id=1, source_target_pairs={{0,32},{32,64},{64,96},{96,128},{128,160},{160,192},{192,224},{1,3... | collective-permute-start | bytes 393224 | tf_op jit(solution)/shard_map/ppermute | solution.py:414
  36.1 5.9 %collective-permute-start.10 = (f32[3,16,256]{2,1,0:T(8,128)S(1)}, f32[3,16,256]{2,1,0:T(8,128)S(1)}, u32[]{:S(2)}, u32[]{:S(2)}) collective-permute-start(f32[3,16,256]{2,1,0:T(8,128)S(1)} %get-tuple-element.73.st0), channel_id=1, source_target_pairs={{0,16},{16,0},{1,17},{17,1},{2,18},{18,2},{3,19},{19,3},{4,20},{20... | collective-permute-start | bytes 147464 | tf_op jit(solution)/shard_map/ppermute | solution.py:409
  40.0 3.2 %collective-permute-start.9 = (f32[3,16,256]{2,1,0:T(8,128)S(1)}, f32[3,16,256]{2,1,0:T(8,128)S(1)}, u32[]{:S(2)}, u32[]{:S(2)}) collective-permute-start(f32[3,16,256]{2,1,0:T(8,128)S(1)} %get-tuple-element.73.st0), channel_id=1, source_target_pairs={{0,8},{8,0},{1,9},{9,1},{2,10},{10,2},{3,11},{11,3},{4,12},{12,4},... | collective-permute-start | bytes 147464 | tf_op jit(solution)/shard_map/ppermute | solution.py:409
  42.0 2.0 %collective-permute-start.11 = (f32[3,16,256]{2,1,0:T(8,128)S(1)}, f32[3,16,256]{2,1,0:T(8,128)S(1)}, u32[]{:S(2)}, u32[]{:S(2)}) collective-permute-start(f32[3,16,256]{2,1,0:T(8,128)S(1)} %collective-permute-done.10.st2), channel_id=1, source_target_pairs={{0,8},{8,0},{1,9},{9,1},{2,10},{10,2},{3,11},{11,3},{4,12},{12,4},... | collective-permute-start | bytes 147464 | tf_op jit(solution)/shard_map/ppermute | solution.py:409
  47.0 13.1 %collective-permute-start.14 = (bf16[256,256]{1,0:T(8,128)(2,1)S(1)}, bf16[256,256]{1,0:T(8,128)(2,1)S(1)}, u32[]{:S(2)}, u32[]{:S(2)}) collective-permute-start(bf16[256,256]{1,0:T(8,128)(2,1)S(1)} %get-tuple-element.90), channel_id=1, source_target_pairs={{64,0},{96,32},{128,64},{160,96},{192,128},{224,160},{65,1},{97,33... | collective-permute-start | bytes 393224 | tf_op jit(solution)/shard_map/ppermute | solution.py:414
  52.4 7.7 %collective-permute-start.13 = (bf16[256,512]{1,0:T(8,128)(2,1)S(1)}, bf16[256,512]{1,0:T(8,128)(2,1)S(1)}, u32[]{:S(2)}, u32[]{:S(2)}) collective-permute-start(bf16[256,512]{1,0:T(8,128)(2,1)S(1)} %get-tuple-element.88), channel_id=1, source_target_pairs={{0,8},{8,0},{1,9},{9,1},{2,10},{10,2},{3,11},{11,3},{4,12},{12,4},... | collective-permute-start | bytes 786440 | tf_op jit(solution)/shard_map/ppermute | solution.py:409
  52.9 13.5 %collective-permute-start.18 = (bf16[256,256]{1,0:T(8,128)(2,1)S(1)}, bf16[256,256]{1,0:T(8,128)(2,1)S(1)}, u32[]{:S(2)}, u32[]{:S(2)}) collective-permute-start(bf16[256,256]{1,0:T(8,128)(2,1)S(1)} %get-tuple-element.95), channel_id=1, source_target_pairs={{128,8},{136,0},{144,24},{152,16},{160,40},{168,32},{176,56},{184,... | collective-permute-start | bytes 393224 | tf_op jit(solution)/shard_map/ppermute | solution.py:428
  54.2 12.5 %collective-permute-start.20 = (bf16[256,256]{1,0:T(8,128)(2,1)S(1)}, bf16[256,256]{1,0:T(8,128)(2,1)S(1)}, u32[]{:S(2)}, u32[]{:S(2)}) collective-permute-start(bf16[256,256]{1,0:T(8,128)(2,1)S(1)} %get-tuple-element.96), channel_id=1, source_target_pairs={{184,24},{216,56},{248,88},{185,25},{217,57},{249,89},{186,26},{21... | collective-permute-start | bytes 393224 | tf_op jit(solution)/shard_map/ppermute | solution.py:436
  59.9 10.3 %collective-permute-start.12 = (bf16[256,512]{1,0:T(8,128)(2,1)S(1)}, bf16[256,512]{1,0:T(8,128)(2,1)S(1)}, u32[]{:S(2)}, u32[]{:S(2)}) collective-permute-start(bf16[256,512]{1,0:T(8,128)(2,1)S(1)} %get-tuple-element.86), channel_id=1, source_target_pairs={{0,8},{8,0},{1,9},{9,1},{2,10},{10,2},{3,11},{11,3},{4,12},{12,4},... | collective-permute-start | bytes 786440 | tf_op jit(solution)/shard_map/ppermute | solution.py:409
  60.2 18.1 %collective-permute-start.15 = (bf16[256,512]{1,0:T(8,128)(2,1)S(1)}, bf16[256,512]{1,0:T(8,128)(2,1)S(1)}, u32[]{:S(2)}, u32[]{:S(2)}) collective-permute-start(bf16[256,512]{1,0:T(8,128)(2,1)S(1)} %pair.1), channel_id=1, source_target_pairs={{0,16},{16,0},{1,17},{17,1},{2,18},{18,2},{3,19},{19,3},{4,20},{20... | collective-permute-start | bytes 786440 | tf_op jit(solution)/shard_map/ppermute | solution.py:409
  65.1 5.1 %collective-permute-start.17 = (bf16[256,256]{1,0:T(8,128)(2,1)S(1)}, bf16[256,256]{1,0:T(8,128)(2,1)S(1)}, u32[]{:S(2)}, u32[]{:S(2)}) collective-permute-start(bf16[256,256]{1,0:T(8,128)(2,1)S(1)} %get-tuple-element.94), channel_id=1, source_target_pairs={{64,0},{96,32},{128,64},{160,96},{192,128},{224,160},{65,1},{97,33... | collective-permute-start | bytes 393224 | tf_op jit(solution)/shard_map/ppermute | solution.py:414
  66.4 3.8 %collective-permute-start.19 = (bf16[256,256]{1,0:T(8,128)(2,1)S(1)}, bf16[256,256]{1,0:T(8,128)(2,1)S(1)}, u32[]{:S(2)}, u32[]{:S(2)}) collective-permute-start(bf16[256,256]{1,0:T(8,128)(2,1)S(1)} %collective-permute-done.18), channel_id=1, source_target_pairs={{0,8},{8,0},{1,9},{9,1},{2,10},{10,2},{3,11},{11,3},{4,12},{12,4},... | collective-permute-start | bytes 393224 | tf_op jit(solution)/shard_map/ppermute | solution.py:409
  66.7 11.6 %collective-permute-start.16 = (bf16[256,256]{1,0:T(8,128)(2,1)S(1)}, bf16[256,256]{1,0:T(8,128)(2,1)S(1)}, u32[]{:S(2)}, u32[]{:S(2)}) collective-permute-start(bf16[256,256]{1,0:T(8,128)(2,1)S(1)} %add_convert_fusion), channel_id=1, source_target_pairs={{32,0},{64,32},{96,64},{128,96},{160,128},{192,160},{224,192},{33,... | collective-permute-start | bytes 393224 | tf_op jit(solution)/shard_map/ppermute | solution.py:414

commit v3 on v2

--- a/solution.py
+++ b/solution.py
@@ -418,16 +418,6 @@
     return lax.ppermute(x, "z", [(i, (i + by) % slabs) for i in sources])
 
 
-def crossed(x, by, slabs):
-    pairs = [
-        (i * SLAB + at, (i + by) * SLAB + (at ^ 1))
-        for i in range(slabs)
-        if 0 <= i + by < slabs
-        for at in range(SLAB)
-    ]
-    return flip(lax.ppermute(x, ("z", "y", "core"), pairs), "core")
-
-
 def shift_last(x, by, slabs):
     last = SLAB - 1
     pairs = [
@@ -499,7 +489,8 @@
         place, ranges, stats, stats_c, stats_y, stats_yc, *data,
     )
     got3 = shift(dkv3, -2, slabs)
-    got4 = crossed(dkv4, -4, slabs)
+    far_slabs = [i for i in range(slabs) if i >= 4]
+    got4 = wrapped(dkv4, 2, far_slabs, slabs)
     got5 = shift_last(dkv5, -5, slabs)
     dqt, there_keep, there_send, acc_near = call(
         there_kernel, "there_gradients", [DQT, DQ, DQ, ((2,) + ACC[0], F32)], [ACC],
@@ -517,6 +508,7 @@
     )
     dq_across = flip(dq_pair, "y")
     dq_beside = flip(dq_beside, "core")
+    got4 = wrapped(got4, 2, [(i + 2) % slabs for i in far_slabs], slabs)
     got2 = shift(dkv2, -2, slabs)
     got1 = shift(dkv1, -1, slabs)
     _, dq_keep, dkv0 = call(

time: 93.1 us -> 100 us (1.074)
  the two profiles are of different devices: /device:TPU:192 before, /device:TPU:32 now
where the time goes in v3:
time: 100 us; the launch traced here: 102 us
  starting transfers between devices  39.1 us (39%)
  waiting for transfers between devices  30.8 us (31%)
  Pallas kernels  14.7 us (15%)
  blocking collectives  13.3 us (13%)
  local copies, waits for them, and re-layouts  2.6 us (3%)
    ppermute x4, waiting for transfers between devices, wrapped(): return lax.ppermute(x, 'z', [(i, (i + by) % slabs) for i in sources])  16.9 us
    ppermute x6, starting transfers between devices, shift(): return lax.ppermute(x, 'z', pairs)  16.6 us
    ppermute x4, starting transfers between devices, wrapped(): return lax.ppermute(x, 'z', [(i, (i + by) % slabs) for i in sources])  14.5 us
    all_to_all x1, blocking collectives, local(): got = lax.all_to_all(whole, 'tp', split_axis=0, concat_axis=0, tiled=True)  13.3 us
    pallas_call x11, Pallas kernels, call(): pl.pallas_call(kernel, out_shape=tuple((jax.ShapeDtypeStruct(shape, dtype...  12.7 us
    ppermute x6, waiting for transfers between devices, shift(): return lax.ppermute(x, 'z', pairs)  9.81 us
    ppermute x9, starting transfers between devices, flip(): return lax.ppermute(x, axis, [(0, 1), (1, 0)])  6.7 us
    ppermute x9, waiting for transfers between devices, flip(): return lax.ppermute(x, axis, [(0, 1), (1, 0)])  4.05 us
  transfers between devices with their start and end apart: 21, of which 8 were waited for; matrix products, arithmetic and copies ran while one was open for 0% of the time, Pallas kernels for 9%

profile of v3, /device:TPU:32, one launch (start us, length us, event | category | flops | bytes accessed | tf_op | source)
XLA Modules:
  0.0 101.6 jit_solution(2296423336263158511)
XLA Ops:
  0.6 2.0 %pack.1 = (bf16[256,1024]{1,0:T(8,128)(2,1)}, bf16[256,256]{1,0:T(8,128)(2,1)}) custom-call(bf16[256,512]{1,0:T(8,128)(2,1)} %q_ref.1, bf16[256,512]{1,0:T(8,128)(2,1)} %g_ref.1, bf16[256,128]{1,0:T(8,128)(2,1)} %k_ref.1, bf16[256,128]{1,0:T(8,128)(2,1)} %v_ref.1), custom_call_target="tpu_custom_call" | custom-call | flops 1 | bytes 1 | tf_op jit(solution)/shard_map/pack/pallas_call | solution.py:435
  2.6 0.1 collective-permute-start
  2.7 3.3 %collective-permute-start.1 = (bf16[256,1024]{1,0:T(8,128)(2,1)}, bf16[256,1024]{1,0:T(8,128)(2,1)S(1)}, u32[]{:S(2)}, u32[]{:S(2)}) collective-permute-start(bf16[256,1024]{1,0:T(8,128)(2,1)} %get-tuple-element.50.qg0), channel_id=1, source_target_pairs={{0,16},{16,0},{1,17},{17,1},{2,18},{18,2},{3,19},{19,3},{4,20},{20... | collective-permute-start | bytes 1572872 | tf_op jit(solution)/shard_map/ppermute | solution.py:409
  6.0 5.2 %collective-permute-start.5 = (bf16[256,256]{1,0:T(8,128)(2,1)}, bf16[256,256]{1,0:T(8,128)(2,1)S(1)}, u32[]{:S(2)}, u32[]{:S(2)}) collective-permute-start(bf16[256,256]{1,0:T(8,128)(2,1)} %get-tuple-element.51.kv0), channel_id=1, source_target_pairs={{0,64},{32,96},{64,128},{96,160},{128,192},{160,224},{1,65},{33,97... | collective-permute-start | bytes 393224 | tf_op jit(solution)/shard_map/ppermute | solution.py:414
  11.2 5.0 %collective-permute-start.4 = (bf16[256,256]{1,0:T(8,128)(2,1)}, bf16[256,256]{1,0:T(8,128)(2,1)S(1)}, u32[]{:S(2)}, u32[]{:S(2)}) collective-permute-start(bf16[256,256]{1,0:T(8,128)(2,1)} %get-tuple-element.51.kv0), channel_id=1, source_target_pairs={{0,32},{32,64},{64,96},{96,128},{128,160},{160,192},{192,224},{1,3... | collective-permute-start | bytes 393224 | tf_op jit(solution)/shard_map/ppermute | solution.py:414
  16.2 0.7 collective-permute-start.3
  16.9 0.0 collective-permute-done.qg1
  16.9 1.9 %collective-permute-start.2 = (bf16[256,256]{1,0:T(8,128)(2,1)}, bf16[256,256]{1,0:T(8,128)(2,1)S(1)}, u32[]{:S(2)}, u32[]{:S(2)}) collective-permute-start(bf16[256,256]{1,0:T(8,128)(2,1)} %get-tuple-element.51.kv0), channel_id=1, source_target_pairs={{0,192},{32,224},{64,0},{96,32},{1,193},{33,225},{65,1},{97,33},{2... | collective-permute-start | bytes 393224 | tf_op jit(solution)/shard_map/ppermute | solution.py:418
  18.8 0.1 pad_add_fusion.place_ref
  18.9 0.0 copy-start
  18.9 1.0 %copy-done = bf16[256,1024]{1,0:T(8,128)(2,1)S(1)} copy-done((bf16[256,1024]{1,0:T(8,128)(2,1)S(1)}, bf16[256,1024]{1,0:T(8,128)(2,1)}, u32[]{:S(2)}) %copy-start) | copy-done | bytes 524312
  19.9 0.0 copy-start.1
  20.0 0.9 copy-done.1
  20.9 0.0 copy-start.2
  20.9 0.7 copy-done.2
  21.5 2.6 %first_statistics.1 = (s32[8]{0:T(128)S(1)}, s32[8,256]{1,0:T(8,128)S(1)}, f32[3,16,256]{2,1,0:T(8,128)S(1)}, f32[6,16,256]{2,1,0:T(8,128)S(1)}, bf16[24,4,256,2...) custom-call(s32[2]{0:T(128)S(1)} %pad_add_fusion.place_ref, ...), custom_call_target="tpu_custom_call" | custom-call | flops 1 | bytes 1 | tf_op jit(solution)/shard_map/first_statistics/pallas_call | solution.py:381
  24.1 0.0 collective-permute-done.5.kv2
  24.1 0.0 collective-permute-done.4.kv1
  24.1 0.0 collective-permute-done.3.kv5
  24.1 0.9 collective-permute-done.2
  25.0 0.0 collective-permute-done.1.qg2
  25.0 0.0 collective-permute-start.6
  25.0 5.4 %collective-permute-start.8 = (bf16[256,256]{1,0:T(8,128)(2,1)S(1)}, bf16[256,256]{1,0:T(8,128)(2,1)S(1)}, u32[]{:S(2)}, u32[]{:S(2)}) collective-permute-start(bf16[256,256]{1,0:T(8,128)(2,1)S(1)} %collective-permute-done.2), channel_id=1, source_target_pairs={{192,128},{224,160},{0,192},{32,224},{193,129},{225,161},{1,193},{... | collective-permute-start | bytes 393224 | tf_op jit(solution)/shard_map/ppermute | solution.py:418
  30.4 1.9 %collective-permute-start.7 = (bf16[256,256]{1,0:T(8,128)(2,1)S(1)}, bf16[256,256]{1,0:T(8,128)(2,1)S(1)}, u32[]{:S(2)}, u32[]{:S(2)}) collective-permute-start(bf16[256,256]{1,0:T(8,128)(2,1)S(1)} %collective-permute-done.5.kv2), channel_id=1, source_target_pairs={{0,32},{32,64},{64,96},{96,128},{128,160},{160,192},{192,224},{1,3... | collective-permute-start | bytes 393224 | tf_op jit(solution)/shard_map/ppermute | solution.py:414
  32.4 0.6 here_statistics.1
  33.0 0.0 collective-permute-done.6.qg3
  33.0 1.3 %there_statistics.1 = (f32[3,16,256]{2,1,0:T(8,128)S(1)}, f32[6,16,256]{2,1,0:T(8,128)S(1)}, bf16[24,4,256,256]{3,2,1,0:T(8,128)(2,1)S(1)}, bf16[4,256,1024]{2,1,0:T(8,128)(2,1)S(1)}) custom-call(s32[2]{0:T(128)S(1)} %pad_add_fusion.place_ref, ...), custom_call_target="tpu_custom_call", output_to_operand_aliasing={{0}: (2, {}), {1}: (3, {}), {2}: (4, {}), {3}: (5, {})} | custom-call | flops 1 | bytes 1 | tf_op jit(solution)/shard_map/there_statistics/pallas_call | solution.py:381
  34.3 0.0 collective-permute-done.8.kv4
  34.3 3.7 %collective-permute-done.7.kv3 = bf16[256,256]{1,0:T(8,128)(2,1)S(1)} collective-permute-done((bf16[256,256]{1,0:T(8,128)(2,1)S(1)}, bf16[256,256]{1,0:T(8,128)(2,1)S(1)}, u32[]{:S(2)}, u32[]{:S(2)}) %collective-permute-start.7) | collective-permute-done | bytes 131104 | tf_op jit(solution)/shard_map/ppermute | solution.py:414
  38.0 0.7 far_statistics.1
  38.6 2.9 %collective-permute-start.10 = (f32[3,16,256]{2,1,0:T(8,128)S(1)}, f32[3,16,256]{2,1,0:T(8,128)S(1)}, u32[]{:S(2)}, u32[]{:S(2)}) collective-permute-start(f32[3,16,256]{2,1,0:T(8,128)S(1)} %get-tuple-element.73.st0), channel_id=1, source_target_pairs={{0,16},{16,0},{1,17},{17,1},{2,18},{18,2},{3,19},{19,3},{4,20},{20... | collective-permute-start | bytes 147464 | tf_op jit(solution)/shard_map/ppermute | solution.py:409
  41.5 0.0 collective-permute-start.9
  41.5 2.8 %collective-permute-done.10.st2 = f32[3,16,256]{2,1,0:T(8,128)S(1)} collective-permute-done((f32[3,16,256]{2,1,0:T(8,128)S(1)}, f32[3,16,256]{2,1,0:T(8,128)S(1)}, u32[]{:S(2)}, u32[]{:S(2)}) %collective-permute-start.10) | collective-permute-done | bytes 49184 | tf_op jit(solution)/shard_map/ppermute | solution.py:409
  44.3 0.0 collective-permute-start.11
  44.3 0.0 collective-permute-done.9.st1
  44.3 1.2 %collective-permute-done.11.st3 = f32[3,16,256]{2,1,0:T(8,128)S(1)} collective-permute-done((f32[3,16,256]{2,1,0:T(8,128)S(1)}, f32[3,16,256]{2,1,0:T(8,128)S(1)}, u32[]{:S(2)}, u32[]{:S(2)}) %collective-permute-start.11) | collective-permute-done | bytes 49184 | tf_op jit(solution)/shard_map/ppermute | solution.py:409
  45.5 2.1 %far_gradients.1 = (f32[16,128,256]{2,1,0:T(8,128)S(1)}, bf16[256,256]{1,0:T(8,128)(2,1)S(1)}, bf16[256,256]{1,0:T(8,128)(2,1)S(1)}, bf16[256,256]{1,0:T(8,128)(...) custom-call(s32[2]{0:T(128)S(1)} %pad_add_fusion.place_ref, ...), custom_call_target="tpu_custom_call" | custom-call | flops 1 | bytes 1 | tf_op jit(solution)/shard_map/far_gradients/pallas_call | solution.py:381
  47.7 1.3 %collective-permute-start.14 = (bf16[256,256]{1,0:T(8,128)(2,1)S(1)}, bf16[256,256]{1,0:T(8,128)(2,1)S(1)}, u32[]{:S(2)}, u32[]{:S(2)}) collective-permute-start(bf16[256,256]{1,0:T(8,128)(2,1)S(1)} %get-tuple-element.90), channel_id=1, source_target_pairs={{64,0},{96,32},{128,64},{160,96},{192,128},{224,160},{65,1},{97,33... | collective-permute-start | bytes 393224 | tf_op jit(solution)/shard_map/ppermute | solution.py:414
  49.0 1.0 there_gradients.1
  50.0 0.3 collective-permute-start.13
  50.2 1.3 %collective-permute-start.18 = (bf16[256,256]{1,0:T(8,128)(2,1)S(1)}, bf16[256,256]{1,0:T(8,128)(2,1)S(1)}, u32[]{:S(2)}, u32[]{:S(2)}) collective-permute-start(bf16[256,256]{1,0:T(8,128)(2,1)S(1)} %get-tuple-element.95), channel_id=1, source_target_pairs={{128,192},{160,224},{192,0},{224,32},{129,193},{161,225},{193,1},{... | collective-permute-start | bytes 393224 | tf_op jit(solution)/shard_map/ppermute | solution.py:418
  51.5 0.7 collective-permute-start.20
  52.2 1.9 %here_gradients.1 = (f32[16,128,256]{2,1,0:T(8,128)S(1)}, bf16[256,512]{1,0:T(8,128)(2,1)S(1)}, f32[256,256]{1,0:T(8,128)S(1)}, bf16[256,256]{1,0:T(8,128)(2,1)S(1)}, f32[256,256]{1,0:T(8,128)S(1)}) custom-call(s32[2]{0:T(128)S(1)} %pad_add_fusion.place_ref, s32[8]{0:T(128)S(1)} %get-tuple-element.52.ranges, ...), custom_call_target="tpu_custom_call", output_to_operand_aliasing={{0}: (2, {})} | custom-call | flops 1 | bytes 1 | tf_op jit(solution)/shard_map/here_gradients/pallas_call | solution.py:381
  54.1 0.1 collective-permute-start.12
  54.2 4.7 %collective-permute-done.14 = bf16[256,256]{1,0:T(8,128)(2,1)S(1)} collective-permute-done((bf16[256,256]{1,0:T(8,128)(2,1)S(1)}, bf16[256,256]{1,0:T(8,128)(2,1)S(1)}, u32[]{:S(2)}, u32[]{:S(2)}) %collective-permute-start.14) | collective-permute-done | bytes 131104 | tf_op jit(solution)/shard_map/ppermute | solution.py:414
  58.9 0.0 collective-permute-done.13.got
  58.9 0.1 pair.1
  59.0 0.1 collective-permute-start.15
  59.1 1.3 %collective-permute-start.17 = (bf16[256,256]{1,0:T(8,128)(2,1)S(1)}, bf16[256,256]{1,0:T(8,128)(2,1)S(1)}, u32[]{:S(2)}, u32[]{:S(2)}) collective-permute-start(bf16[256,256]{1,0:T(8,128)(2,1)S(1)} %get-tuple-element.94), channel_id=1, source_target_pairs={{64,0},{96,32},{128,64},{160,96},{192,128},{224,160},{65,1},{97,33... | collective-permute-start | bytes 393224 | tf_op jit(solution)/shard_map/ppermute | solution.py:414
  60.4 9.4 %collective-permute-done.18 = bf16[256,256]{1,0:T(8,128)(2,1)S(1)} collective-permute-done((bf16[256,256]{1,0:T(8,128)(2,1)S(1)}, bf16[256,256]{1,0:T(8,128)(2,1)S(1)}, u32[]{:S(2)}, u32[]{:S(2)}) %collective-permute-start.18) | collective-permute-done | bytes 131104 | tf_op jit(solution)/shard_map/ppermute | solution.py:418
  69.8 5.8 %collective-permute-start.19 = (bf16[256,256]{1,0:T(8,128)(2,1)S(1)}, bf16[256,256]{1,0:T(8,128)(2,1)S(1)}, u32[]{:S(2)}, u32[]{:S(2)}) collective-permute-start(bf16[256,256]{1,0:T(8,128)(2,1)S(1)} %collective-permute-done.18), channel_id=1, source_target_pairs={{192,0},{224,32},{0,64},{32,96},{193,1},{225,33},{1,65},{33,97},{1... | collective-permute-start | bytes 393224 | tf_op jit(solution)/shard_map/ppermute | solution.py:418
  75.7 0.0 collective-permute-done.20.got5
  75.7 1.9 %collective-permute-start.16 = (bf16[256,256]{1,0:T(8,128)(2,1)S(1)}, bf16[256,256]{1,0:T(8,128)(2,1)S(1)}, u32[]{:S(2)}, u32[]{:S(2)}) collective-permute-start(bf16[256,256]{1,0:T(8,128)(2,1)S(1)} %add_convert_fusion), channel_id=1, source_target_pairs={{32,0},{64,32},{96,64},{128,96},{160,128},{192,160},{224,192},{33,... | collective-permute-start | bytes 393224 | tf_op jit(solution)/shard_map/ppermute | solution.py:414
  77.6 1.5 %own_gradients.1 = (f32[16,128,256]{2,1,0:T(8,128)S(1)}, bf16[256,512]{1,0:T(8,128)(2,1)S(1)}, f32[256,256]{1,0:T(8,128)S(1)}) custom-call(s32[2]{0:T(128)S(1)} %pad_add_fusion.place_ref, s32[8]{0:T(128)S(1)} %get-tuple-element.52.ranges, f32[16,128,256]{2,1,0:T(8,128)S(1)} %get-tuple-element.83.dqt_in, ...), custom_call_target="tpu_custom_call", output_to_operand_aliasing={{0}: (2, {})} | custom-call | flops 1 | bytes 1 | tf_op jit(solution)/shard_map/own_gradients/pallas_call | solution.py:381
  79.2 1.4 %collective-permute-done.17.got2 = bf16[256,256]{1,0:T(8,128)(2,1)S(1)} collective-permute-done((bf16[256,256]{1,0:T(8,128)(2,1)S(1)}, bf16[256,256]{1,0:T(8,128)(2,1)S(1)}, u32[]{:S(2)}, u32[]{:S(2)}) %collective-permute-start.17) | collective-permute-done | bytes 131104 | tf_op jit(solution)/shard_map/ppermute | solution.py:414
  80.6 6.7 %collective-permute-done.19.got4 = bf16[256,256]{1,0:T(8,128)(2,1)S(1)} collective-permute-done((bf16[256,256]{1,0:T(8,128)(2,1)S(1)}, bf16[256,256]{1,0:T(8,128)(2,1)S(1)}, u32[]{:S(2)}, u32[]{:S(2)}) %collective-permute-start.19) | collective-permute-done | bytes 131104 | tf_op jit(solution)/shard_map/ppermute | solution.py:418
  87.3 0.0 collective-permute-done.12.beside
  87.3 0.0 collective-permute-done.16.got1
  87.3 0.0 collective-permute-done.15.across
  87.3 0.2 merge.1
  87.5 13.3 %all_to_all.5.got = bf16[8,32,768]{2,1,0:T(8,128)(2,1)S(1)} all-to-all(bf16[8,32,768]{2,1,0:T(8,128)(2,1)S(1)} %merge.1), channel_id=1, replica_groups=mesh['z'=8,'y'=2,'core'=2,'tp'=8] {'tp'}, dimensions={0} | all-to-all | bytes 786432 | tf_op jit(solution)/shard_map/all_to_all | solution.py:526
  100.8 0.8 finish.1
  (1 shorter events, 0.0 us)
Async XLA Ops:
  2.6 14.3 %collective-permute-start = (bf16[256,1024]{1,0:T(8,128)(2,1)}, bf16[256,1024]{1,0:T(8,128)(2,1)S(1)}, u32[]{:S(2)}, u32[]{:S(2)}) collective-permute-start(bf16[256,1024]{1,0:T(8,128)(2,1)} %get-tuple-element.50.qg0), channel_id=1, source_target_pairs={{0,8},{8,0},{1,9},{9,1},{2,10},{10,2},{3,11},{11,3},{4,12},{12,4},... | collective-permute-start | bytes 1572872 | tf_op jit(solution)/shard_map/ppermute | solution.py:409
  2.7 22.3 %collective-permute-start.1 = (bf16[256,1024]{1,0:T(8,128)(2,1)}, bf16[256,1024]{1,0:T(8,128)(2,1)S(1)}, u32[]{:S(2)}, u32[]{:S(2)}) collective-permute-start(bf16[256,1024]{1,0:T(8,128)(2,1)} %get-tuple-element.50.qg0), channel_id=1, source_target_pairs={{0,16},{16,0},{1,17},{17,1},{2,18},{18,2},{3,19},{19,3},{4,20},{20... | collective-permute-start | bytes 1572872 | tf_op jit(solution)/shard_map/ppermute | solution.py:409
  6.0 18.1 %collective-permute-start.5 = (bf16[256,256]{1,0:T(8,128)(2,1)}, bf16[256,256]{1,0:T(8,128)(2,1)S(1)}, u32[]{:S(2)}, u32[]{:S(2)}) collective-permute-start(bf16[256,256]{1,0:T(8,128)(2,1)} %get-tuple-element.51.kv0), channel_id=1, source_target_pairs={{0,64},{32,96},{64,128},{96,160},{128,192},{160,224},{1,65},{33,97... | collective-permute-start | bytes 393224 | tf_op jit(solution)/shard_map/ppermute | solution.py:414
  11.2 12.9 %collective-permute-start.4 = (bf16[256,256]{1,0:T(8,128)(2,1)}, bf16[256,256]{1,0:T(8,128)(2,1)S(1)}, u32[]{:S(2)}, u32[]{:S(2)}) collective-permute-start(bf16[256,256]{1,0:T(8,128)(2,1)} %get-tuple-element.51.kv0), channel_id=1, source_target_pairs={{0,32},{32,64},{64,96},{96,128},{128,160},{160,192},{192,224},{1,3... | collective-permute-start | bytes 393224 | tf_op jit(solution)/shard_map/ppermute | solution.py:414
  16.2 7.9 %collective-permute-start.3 = (bf16[256,256]{1,0:T(8,128)(2,1)}, bf16[256,256]{1,0:T(8,128)(2,1)S(1)}, u32[]{:S(2)}, u32[]{:S(2)}) collective-permute-start(bf16[256,256]{1,0:T(8,128)(2,1)} %get-tuple-element.51.kv0), channel_id=1, source_target_pairs={{24,184},{56,216},{88,248},{25,185},{57,217},{89,249},{26,186},{58... | collective-permute-start | bytes 393224 | tf_op jit(solution)/shard_map/ppermute | solution.py:426
  16.9 8.1 %collective-permute-start.2 = (bf16[256,256]{1,0:T(8,128)(2,1)}, bf16[256,256]{1,0:T(8,128)(2,1)S(1)}, u32[]{:S(2)}, u32[]{:S(2)}) collective-permute-start(bf16[256,256]{1,0:T(8,128)(2,1)} %get-tuple-element.51.kv0), channel_id=1, source_target_pairs={{0,192},{32,224},{64,0},{96,32},{1,193},{33,225},{65,1},{97,33},{2... | collective-permute-start | bytes 393224 | tf_op jit(solution)/shard_map/ppermute | solution.py:418
  18.9 1.0 %copy-start = (bf16[256,1024]{1,0:T(8,128)(2,1)S(1)}, bf16[256,1024]{1,0:T(8,128)(2,1)}, u32[]{:S(2)}) copy-start(bf16[256,1024]{1,0:T(8,128)(2,1)} %get-tuple-element.50.qg0) | copy-start | bytes 1572868
  19.9 0.9 copy-start.1
  20.9 0.7 copy-start.2
  25.0 8.0 %collective-permute-start.6 = (bf16[256,1024]{1,0:T(8,128)(2,1)S(1)}, bf16[256,1024]{1,0:T(8,128)(2,1)S(1)}, u32[]{:S(2)}, u32[]{:S(2)}) collective-permute-start(bf16[256,1024]{1,0:T(8,128)(2,1)S(1)} %collective-permute-done.1.qg2), channel_id=1, source_target_pairs={{0,8},{8,0},{1,9},{9,1},{2,10},{10,2},{3,11},{11,3},{4,12},{12,4},... | collective-permute-start | bytes 1572872 | tf_op jit(solution)/shard_map/ppermute | solution.py:409
  25.0 9.3 %collective-permute-start.8 = (bf16[256,256]{1,0:T(8,128)(2,1)S(1)}, bf16[256,256]{1,0:T(8,128)(2,1)S(1)}, u32[]{:S(2)}, u32[]{:S(2)}) collective-permute-start(bf16[256,256]{1,0:T(8,128)(2,1)S(1)} %collective-permute-done.2), channel_id=1, source_target_pairs={{192,128},{224,160},{0,192},{32,224},{193,129},{225,161},{1,193},{... | collective-permute-start | bytes 393224 | tf_op jit(solution)/shard_map/ppermute | solution.py:418
  30.4 7.5 %collective-permute-start.7 = (bf16[256,256]{1,0:T(8,128)(2,1)S(1)}, bf16[256,256]{1,0:T(8,128)(2,1)S(1)}, u32[]{:S(2)}, u32[]{:S(2)}) collective-permute-start(bf16[256,256]{1,0:T(8,128)(2,1)S(1)} %collective-permute-done.5.kv2), channel_id=1, source_target_pairs={{0,32},{32,64},{64,96},{96,128},{128,160},{160,192},{192,224},{1,3... | collective-permute-start | bytes 393224 | tf_op jit(solution)/shard_map/ppermute | solution.py:414
  38.6 5.7 %collective-permute-start.10 = (f32[3,16,256]{2,1,0:T(8,128)S(1)}, f32[3,16,256]{2,1,0:T(8,128)S(1)}, u32[]{:S(2)}, u32[]{:S(2)}) collective-permute-start(f32[3,16,256]{2,1,0:T(8,128)S(1)} %get-tuple-element.73.st0), channel_id=1, source_target_pairs={{0,16},{16,0},{1,17},{17,1},{2,18},{18,2},{3,19},{19,3},{4,20},{20... | collective-permute-start | bytes 147464 | tf_op jit(solution)/shard_map/ppermute | solution.py:409
  41.5 2.8 %collective-permute-start.9 = (f32[3,16,256]{2,1,0:T(8,128)S(1)}, f32[3,16,256]{2,1,0:T(8,128)S(1)}, u32[]{:S(2)}, u32[]{:S(2)}) collective-permute-start(f32[3,16,256]{2,1,0:T(8,128)S(1)} %get-tuple-element.73.st0), channel_id=1, source_target_pairs={{0,8},{8,0},{1,9},{9,1},{2,10},{10,2},{3,11},{11,3},{4,12},{12,4},... | collective-permute-start | bytes 147464 | tf_op jit(solution)/shard_map/ppermute | solution.py:409
  44.3 1.2 %collective-permute-start.11 = (f32[3,16,256]{2,1,0:T(8,128)S(1)}, f32[3,16,256]{2,1,0:T(8,128)S(1)}, u32[]{:S(2)}, u32[]{:S(2)}) collective-permute-start(f32[3,16,256]{2,1,0:T(8,128)S(1)} %collective-permute-done.10.st2), channel_id=1, source_target_pairs={{0,8},{8,0},{1,9},{9,1},{2,10},{10,2},{3,11},{11,3},{4,12},{12,4},... | collective-permute-start | bytes 147464 | tf_op jit(solution)/shard_map/ppermute | solution.py:409
  47.7 11.2 %collective-permute-start.14 = (bf16[256,256]{1,0:T(8,128)(2,1)S(1)}, bf16[256,256]{1,0:T(8,128)(2,1)S(1)}, u32[]{:S(2)}, u32[]{:S(2)}) collective-permute-start(bf16[256,256]{1,0:T(8,128)(2,1)S(1)} %get-tuple-element.90), channel_id=1, source_target_pairs={{64,0},{96,32},{128,64},{160,96},{192,128},{224,160},{65,1},{97,33... | collective-permute-start | bytes 393224 | tf_op jit(solution)/shard_map/ppermute | solution.py:414
  50.0 9.0 %collective-permute-start.13 = (bf16[256,512]{1,0:T(8,128)(2,1)S(1)}, bf16[256,512]{1,0:T(8,128)(2,1)S(1)}, u32[]{:S(2)}, u32[]{:S(2)}) collective-permute-start(bf16[256,512]{1,0:T(8,128)(2,1)S(1)} %get-tuple-element.88), channel_id=1, source_target_pairs={{0,8},{8,0},{1,9},{9,1},{2,10},{10,2},{3,11},{11,3},{4,12},{12,4},... | collective-permute-start | bytes 786440 | tf_op jit(solution)/shard_map/ppermute | solution.py:409
  50.2 19.6 %collective-permute-start.18 = (bf16[256,256]{1,0:T(8,128)(2,1)S(1)}, bf16[256,256]{1,0:T(8,128)(2,1)S(1)}, u32[]{:S(2)}, u32[]{:S(2)}) collective-permute-start(bf16[256,256]{1,0:T(8,128)(2,1)S(1)} %get-tuple-element.95), channel_id=1, source_target_pairs={{128,192},{160,224},{192,0},{224,32},{129,193},{161,225},{193,1},{... | collective-permute-start | bytes 393224 | tf_op jit(solution)/shard_map/ppermute | solution.py:418
  51.5 24.2 %collective-permute-start.20 = (bf16[256,256]{1,0:T(8,128)(2,1)S(1)}, bf16[256,256]{1,0:T(8,128)(2,1)S(1)}, u32[]{:S(2)}, u32[]{:S(2)}) collective-permute-start(bf16[256,256]{1,0:T(8,128)(2,1)S(1)} %get-tuple-element.96), channel_id=1, source_target_pairs={{184,24},{216,56},{248,88},{185,25},{217,57},{249,89},{186,26},{21... | collective-permute-start | bytes 393224 | tf_op jit(solution)/shard_map/ppermute | solution.py:426
  54.1 33.2 %collective-permute-start.12 = (bf16[256,512]{1,0:T(8,128)(2,1)S(1)}, bf16[256,512]{1,0:T(8,128)(2,1)S(1)}, u32[]{:S(2)}, u32[]{:S(2)}) collective-permute-start(bf16[256,512]{1,0:T(8,128)(2,1)S(1)} %get-tuple-element.86), channel_id=1, source_target_pairs={{0,8},{8,0},{1,9},{9,1},{2,10},{10,2},{3,11},{11,3},{4,12},{12,4},... | collective-permute-start | bytes 786440 | tf_op jit(solution)/shard_map/ppermute | solution.py:409
  59.0 28.3 %collective-permute-start.15 = (bf16[256,512]{1,0:T(8,128)(2,1)S(1)}, bf16[256,512]{1,0:T(8,128)(2,1)S(1)}, u32[]{:S(2)}, u32[]{:S(2)}) collective-permute-start(bf16[256,512]{1,0:T(8,128)(2,1)S(1)} %pair.1), channel_id=1, source_target_pairs={{0,16},{16,0},{1,17},{17,1},{2,18},{18,2},{3,19},{19,3},{4,20},{20... | collective-permute-start | bytes 786440 | tf_op jit(solution)/shard_map/ppermute | solution.py:409
  59.1 21.5 %collective-permute-start.17 = (bf16[256,256]{1,0:T(8,128)(2,1)S(1)}, bf16[256,256]{1,0:T(8,128)(2,1)S(1)}, u32[]{:S(2)}, u32[]{:S(2)}) collective-permute-start(bf16[256,256]{1,0:T(8,128)(2,1)S(1)} %get-tuple-element.94), channel_id=1, source_target_pairs={{64,0},{96,32},{128,64},{160,96},{192,128},{224,160},{65,1},{97,33... | collective-permute-start | bytes 393224 | tf_op jit(solution)/shard_map/ppermute | solution.py:414
  69.8 17.4 %collective-permute-start.19 = (bf16[256,256]{1,0:T(8,128)(2,1)S(1)}, bf16[256,256]{1,0:T(8,128)(2,1)S(1)}, u32[]{:S(2)}, u32[]{:S(2)}) collective-permute-start(bf16[256,256]{1,0:T(8,128)(2,1)S(1)} %collective-permute-done.18), channel_id=1, source_target_pairs={{192,0},{224,32},{0,64},{32,96},{193,1},{225,33},{1,65},{33,97},{1... | collective-permute-start | bytes 393224 | tf_op jit(solution)/shard_map/ppermute | solution.py:418
  75.7 11.6 %collective-permute-start.16 = (bf16[256,256]{1,0:T(8,128)(2,1)S(1)}, bf16[256,256]{1,0:T(8,128)(2,1)S(1)}, u32[]{:S(2)}, u32[]{:S(2)}) collective-permute-start(bf16[256,256]{1,0:T(8,128)(2,1)S(1)} %add_convert_fusion), channel_id=1, source_target_pairs={{32,0},{64,32},{96,64},{128,96},{160,128},{192,160},{224,192},{33,... | collective-permute-start | bytes 393224 | tf_op jit(solution)/shard_map/ppermute | solution.py:414

commit v4 on v3

--- a/solution.py
+++ b/solution.py
@@ -251,7 +251,7 @@
 
 def far_kernel(
     place_ref, ranges, st0, st1, st2, st3, tops, weights, qg_all, kv_all,
-    dqt, dkv3, dkv4, dkv5, acc0_ref, lse_ref, delta_ref, acc,
+    dqt, dkv34, dkv5, acc0_ref, lse_ref, delta_ref, acc,
 ):
     combine_stats((st0, st1, st2, st3), lse_ref, delta_ref)
     dqt[...] = jnp.zeros_like(dqt)
@@ -268,7 +268,7 @@
         def _():
             acc0_ref[...] = acc[...]
 
-        for slot, ref in enumerate((dkv5, dkv4, dkv3)):
+        for slot, ref in enumerate((dkv5, dkv34.at[1], dkv34.at[0])):
 
             @pl.when(step == slot + 1)
             def _():
@@ -355,11 +355,11 @@
     out_ref[...] = (keep[...].astype(F32) + got[...].astype(F32)).astype(BF16)
 
 
-def merge_kernel(keep, beside, across, dkv0, got1, got2, got4, got5, out_ref):
+def merge_kernel(keep, beside, across, dkv0, got1, got2, got5, out_ref):
     parts, part = out_ref.shape[:2]
     width = GROUP * HD
     dkv = dkv0[...] + got1[...].astype(F32) + got2[...].astype(F32)
-    dkv = dkv + got4[...].astype(F32) + got5[...].astype(F32)
+    dkv = dkv + got5[...].astype(F32)
     dq = keep[...].astype(F32) + beside[...].astype(F32) + across[...].astype(F32)
     out_ref[:, :, :width] = dq.astype(BF16).reshape(parts, part, width)
     out_ref[:, :, width:] = dkv.astype(BF16).reshape(parts, part, 2 * HD)
@@ -484,13 +484,12 @@
     stats_yc = flip(stats_y, "core")
 
     data = (tops, weights, qg_all, kv_all)
-    dqt, dkv3, dkv4, dkv5, acc0, lse, delta = call(
-        far_kernel, "far_gradients", [DQT, DKV, DKV, DKV, ACC, ROW_STATS, ROW_STATS], [ACC],
+    dqt, dkv34, dkv5, acc0, lse, delta = call(
+        far_kernel, "far_gradients",
+        [DQT, ((2,) + DKV[0], BF16), DKV, ACC, ROW_STATS, ROW_STATS], [ACC],
         place, ranges, stats, stats_c, stats_y, stats_yc, *data,
     )
-    got3 = shift(dkv3, -2, slabs)
-    far_slabs = [i for i in range(slabs) if i >= 4]
-    got4 = wrapped(dkv4, 2, far_slabs, slabs)
+    got_far = shift(dkv34, -2, slabs)
     got5 = shift_last(dkv5, -5, slabs)
     dqt, there_keep, there_send, acc_near = call(
         there_kernel, "there_gradients", [DQT, DQ, DQ, ((2,) + ACC[0], F32)], [ACC],
@@ -498,19 +497,19 @@
     )
     there_got = flip(there_send, "core")
     dqt, dq_beside, dkv1, dkv2, acc0 = call(
-        here_kernel, "here_gradients", [DQT, DQ, ACC, DKV, ACC], [ACC],
+        here_kernel, "here_gradients", [DQT, DQ, ACC, ACC, ACC], [ACC],
         place, ranges, dqt, lse, delta, *data, acc0, acc_near, aliases={2: 0},
     )
-    dkv1 = (dkv1 + got3.astype(F32)).astype(BF16)
-    there_got, dkv1 = lax.optimization_barrier((there_got, dkv1))
+    dkv1 = (dkv1 + got_far[0].astype(F32)).astype(BF16)
+    dkv2 = (dkv2 + got_far[1].astype(F32)).astype(BF16)
+    there_got, dkv1, dkv2 = lax.optimization_barrier((there_got, dkv1, dkv2))
     dq_pair, = call(
         pair_kernel, "pair", [DQ], [], there_keep, there_got, scalars=0
     )
     dq_across = flip(dq_pair, "y")
     dq_beside = flip(dq_beside, "core")
-    got4 = wrapped(got4, 2, [(i + 2) % slabs for i in far_slabs], slabs)
+    got1 = shift(dkv1, -1, slabs)
     got2 = shift(dkv2, -2, slabs)
-    got1 = shift(dkv1, -1, slabs)
     _, dq_keep, dkv0 = call(
         own_kernel, "own_gradients", [DQT, DQ, ACC], [ACC],
         place, ranges, dqt, lse, delta, *data, acc0, aliases={2: 0},
@@ -521,7 +520,7 @@
     width = GROUP * HD
     whole, = call(
         merge_kernel, "merge", [((tp, part, width + 2 * HD), BF16)], [],
-        dq_keep, dq_beside, dq_across, dkv0, got1, got2, got4, got5, scalars=0,
+        dq_keep, dq_beside, dq_across, dkv0, got1, got2, got5, scalars=0,
     )
     got = lax.all_to_all(whole, "tp", split_axis=0, concat_axis=0, tiled=True)
     return call(

time: 100 us -> 98.7 us (0.987)
  the two profiles are of different devices: /device:TPU:32 before, /device:TPU:64 now
where the time goes in v4:
time: 98.7 us; the launch traced here: 97 us
  waiting for transfers between devices  34.7 us (35%)
  starting transfers between devices  32 us (32%)
  blocking collectives  13.5 us (14%)
  Pallas kernels  13.2 us (13%)
  local copies, waits for them, and re-layouts  2.6 us (3%)
    ppermute x6, waiting for transfers between devices, shift(): return lax.ppermute(x, 'z', pairs)  29.6 us
    ppermute x6, starting transfers between devices, shift(): return lax.ppermute(x, 'z', pairs)  20.2 us
    all_to_all x1, blocking collectives, local(): got = lax.all_to_all(whole, 'tp', split_axis=0, concat_axis=0, tiled=True)  13.5 us
    pallas_call x11, Pallas kernels, call(): pl.pallas_call(kernel, out_shape=tuple((jax.ShapeDtypeStruct(shape, dtype...  11.3 us
    ppermute x9, starting transfers between devices, flip(): return lax.ppermute(x, axis, [(0, 1), (1, 0)])  8.5 us
    ppermute x9, waiting for transfers between devices, flip(): return lax.ppermute(x, axis, [(0, 1), (1, 0)])  4.41 us
    unnamed x6, local copies, waits for them, and re-layouts  2.6 us
  transfers between devices with their start and end apart: 19, of which 7 were waited for; matrix products, arithmetic and copies ran while one was open for 0% of the time, Pallas kernels for 9%

profile of v4, /device:TPU:64, one launch (start us, length us, event | category | flops | bytes accessed | tf_op | source)
XLA Modules:
  0.0 97.0 jit_solution(7760987563969089227)
XLA Ops:
  0.6 2.0 %pack.1 = (bf16[256,1024]{1,0:T(8,128)(2,1)}, bf16[256,256]{1,0:T(8,128)(2,1)}) custom-call(bf16[256,512]{1,0:T(8,128)(2,1)} %q_ref.1, bf16[256,512]{1,0:T(8,128)(2,1)} %g_ref.1, bf16[256,128]{1,0:T(8,128)(2,1)} %k_ref.1, bf16[256,128]{1,0:T(8,128)(2,1)} %v_ref.1), custom_call_target="tpu_custom_call" | custom-call | flops 1 | bytes 1 | tf_op jit(solution)/shard_map/pack/pallas_call | solution.py:435
  2.6 0.1 collective-permute-start
  2.7 3.3 %collective-permute-start.1 = (bf16[256,1024]{1,0:T(8,128)(2,1)}, bf16[256,1024]{1,0:T(8,128)(2,1)S(1)}, u32[]{:S(2)}, u32[]{:S(2)}) collective-permute-start(bf16[256,1024]{1,0:T(8,128)(2,1)} %get-tuple-element.50.qg0), channel_id=1, source_target_pairs={{0,16},{16,0},{1,17},{17,1},{2,18},{18,2},{3,19},{19,3},{4,20},{20... | collective-permute-start | bytes 1572872 | tf_op jit(solution)/shard_map/ppermute | solution.py:409
  6.0 6.4 %collective-permute-start.5 = (bf16[256,256]{1,0:T(8,128)(2,1)}, bf16[256,256]{1,0:T(8,128)(2,1)S(1)}, u32[]{:S(2)}, u32[]{:S(2)}) collective-permute-start(bf16[256,256]{1,0:T(8,128)(2,1)} %get-tuple-element.51.kv0), channel_id=1, source_target_pairs={{0,64},{32,96},{64,128},{96,160},{128,192},{160,224},{1,65},{33,97... | collective-permute-start | bytes 393224 | tf_op jit(solution)/shard_map/ppermute | solution.py:414
  12.4 2.9 %collective-permute-start.4 = (bf16[256,256]{1,0:T(8,128)(2,1)}, bf16[256,256]{1,0:T(8,128)(2,1)S(1)}, u32[]{:S(2)}, u32[]{:S(2)}) collective-permute-start(bf16[256,256]{1,0:T(8,128)(2,1)} %get-tuple-element.51.kv0), channel_id=1, source_target_pairs={{0,32},{32,64},{64,96},{96,128},{128,160},{160,192},{192,224},{1,3... | collective-permute-start | bytes 393224 | tf_op jit(solution)/shard_map/ppermute | solution.py:414
  15.3 0.7 collective-permute-start.3
  16.0 0.0 collective-permute-done.qg1
  16.0 1.3 %collective-permute-start.2 = (bf16[256,256]{1,0:T(8,128)(2,1)}, bf16[256,256]{1,0:T(8,128)(2,1)S(1)}, u32[]{:S(2)}, u32[]{:S(2)}) collective-permute-start(bf16[256,256]{1,0:T(8,128)(2,1)} %get-tuple-element.51.kv0), channel_id=1, source_target_pairs={{0,192},{32,224},{64,0},{96,32},{1,193},{33,225},{65,1},{97,33},{2... | collective-permute-start | bytes 393224 | tf_op jit(solution)/shard_map/ppermute | solution.py:418
  17.3 0.1 pad_add_fusion.place_ref
  17.4 0.0 copy-start
  17.4 1.0 %copy-done = bf16[256,1024]{1,0:T(8,128)(2,1)S(1)} copy-done((bf16[256,1024]{1,0:T(8,128)(2,1)S(1)}, bf16[256,1024]{1,0:T(8,128)(2,1)}, u32[]{:S(2)}) %copy-start) | copy-done | bytes 524312
  18.4 0.0 copy-start.1
  18.4 0.9 copy-done.1
  19.3 0.0 copy-start.2
  19.3 0.7 copy-done.2
  20.0 2.6 %first_statistics.1 = (s32[8]{0:T(128)S(1)}, s32[8,256]{1,0:T(8,128)S(1)}, f32[3,16,256]{2,1,0:T(8,128)S(1)}, f32[6,16,256]{2,1,0:T(8,128)S(1)}, bf16[24,4,256,2...) custom-call(s32[2]{0:T(128)S(1)} %pad_add_fusion.place_ref, ...), custom_call_target="tpu_custom_call" | custom-call | flops 1 | bytes 1 | tf_op jit(solution)/shard_map/first_statistics/pallas_call | solution.py:381
  22.6 0.0 collective-permute-done.5.kv2
  22.6 0.0 collective-permute-done.4.kv1
  22.6 0.0 collective-permute-done.3.kv5
  22.6 0.7 collective-permute-done.2
  23.3 0.0 collective-permute-done.1.qg2
  23.3 0.0 collective-permute-start.6
  23.3 0.7 collective-permute-start.8
  23.9 4.5 %collective-permute-start.7 = (bf16[256,256]{1,0:T(8,128)(2,1)S(1)}, bf16[256,256]{1,0:T(8,128)(2,1)S(1)}, u32[]{:S(2)}, u32[]{:S(2)}) collective-permute-start(bf16[256,256]{1,0:T(8,128)(2,1)S(1)} %collective-permute-done.5.kv2), channel_id=1, source_target_pairs={{0,32},{32,64},{64,96},{96,128},{128,160},{160,192},{192,224},{1,3... | collective-permute-start | bytes 393224 | tf_op jit(solution)/shard_map/ppermute | solution.py:414
  28.4 0.6 here_statistics.1
  29.0 0.0 collective-permute-done.6.qg3
  29.0 0.7 there_statistics.1
  29.7 0.0 collective-permute-done.8.kv4
  29.7 6.6 %collective-permute-done.7.kv3 = bf16[256,256]{1,0:T(8,128)(2,1)S(1)} collective-permute-done((bf16[256,256]{1,0:T(8,128)(2,1)S(1)}, bf16[256,256]{1,0:T(8,128)(2,1)S(1)}, u32[]{:S(2)}, u32[]{:S(2)}) %collective-permute-start.7) | collective-permute-done | bytes 131104 | tf_op jit(solution)/shard_map/ppermute | solution.py:414
  36.3 0.7 far_statistics.1
  37.0 2.5 %collective-permute-start.10 = (f32[3,16,256]{2,1,0:T(8,128)S(1)}, f32[3,16,256]{2,1,0:T(8,128)S(1)}, u32[]{:S(2)}, u32[]{:S(2)}) collective-permute-start(f32[3,16,256]{2,1,0:T(8,128)S(1)} %get-tuple-element.73.st0), channel_id=1, source_target_pairs={{0,16},{16,0},{1,17},{17,1},{2,18},{18,2},{3,19},{19,3},{4,20},{20... | collective-permute-start | bytes 147464 | tf_op jit(solution)/shard_map/ppermute | solution.py:409
  39.5 0.0 collective-permute-start.9
  39.5 3.2 %collective-permute-done.10.st2 = f32[3,16,256]{2,1,0:T(8,128)S(1)} collective-permute-done((f32[3,16,256]{2,1,0:T(8,128)S(1)}, f32[3,16,256]{2,1,0:T(8,128)S(1)}, u32[]{:S(2)}, u32[]{:S(2)}) %collective-permute-start.10) | collective-permute-done | bytes 49184 | tf_op jit(solution)/shard_map/ppermute | solution.py:409
  42.7 0.0 collective-permute-start.11
  42.7 0.0 collective-permute-done.9.st1
  42.7 1.2 %collective-permute-done.11.st3 = f32[3,16,256]{2,1,0:T(8,128)S(1)} collective-permute-done((f32[3,16,256]{2,1,0:T(8,128)S(1)}, f32[3,16,256]{2,1,0:T(8,128)S(1)}, u32[]{:S(2)}, u32[]{:S(2)}) %collective-permute-start.11) | collective-permute-done | bytes 49184 | tf_op jit(solution)/shard_map/ppermute | solution.py:409
  43.9 1.3 %far_gradients.1 = (f32[16,128,256]{2,1,0:T(8,128)S(1)}, bf16[2,256,256]{2,1,0:T(8,128)(2,1)S(1)}, bf16[256,256]{1,0:T(8,128)(2,1)S(1)}, f32[256,256]{1,0:T(8,12...) custom-call(s32[2]{0:T(128)S(1)} %pad_add_fusion.place_ref, s32[8]{0:T(128)S(1)} %get-tuple-element.52.ranges, ...), custom_call_target="tpu_custom_call" | custom-call | flops 1 | bytes 1 | tf_op jit(solution)/shard_map/far_gradients/pallas_call | solution.py:381
  45.3 2.6 %collective-permute-start.14 = (bf16[2,256,256]{2,1,0:T(8,128)(2,1)S(1)}, bf16[2,256,256]{2,1,0:T(8,128)(2,1)S(1)}, u32[]{:S(2)}, u32[]{:S(2)}) collective-permute-start(bf16[2,256,256]{2,1,0:T(8,128)(2,1)S(1)} %get-tuple-element.90), channel_id=1, source_target_pairs={{64,0},{96,32},{128,64},{160,96},{192,128},{224,160},{65,1},{97,33... | collective-permute-start | bytes 786440 | tf_op jit(solution)/shard_map/ppermute | solution.py:414
  47.9 1.0 there_gradients.1
  48.9 0.8 collective-permute-start.13
  49.6 1.9 %here_gradients.1 = (f32[16,128,256]{2,1,0:T(8,128)S(1)}, bf16[256,512]{1,0:T(8,128)(2,1)S(1)}, f32[256,256]{1,0:T(8,128)S(1)}, f32[256,256]{1,0:T(8,128)S(1)}, f32[256,256]{1,0:T(8,128)S(1)}) custom-call(s32[2]{0:T(128)S(1)} %pad_add_fusion.place_ref, s32[8]{0:T(128)S(1)} %get-tuple-element.52.ranges, ...), custom_call_target="tpu_custom_call", output_to_operand_aliasing={{0}: (2, {})} | custom-call | flops 1 | bytes 1 | tf_op jit(solution)/shard_map/here_gradients/pallas_call | solution.py:381
  51.5 0.1 collective-permute-start.12
  51.6 12.4 %collective-permute-done.14 = bf16[2,256,256]{2,1,0:T(8,128)(2,1)S(1)} collective-permute-done((bf16[2,256,256]{2,1,0:T(8,128)(2,1)S(1)}, bf16[2,256,256]{2,1,0:T(8,128)(2,1)S(1)}, u32[]{:S(2)}, u32[]{:S(2)}) %collective-permute-start.14) | collective-permute-done | bytes 262176 | tf_op jit(solution)/shard_map/ppermute | solution.py:414
  64.1 0.1 fusion
  64.1 0.0 collective-permute-done.13.got
  64.1 0.1 pair.1
  64.2 1.8 %collective-permute-start.15 = (bf16[256,512]{1,0:T(8,128)(2,1)S(1)}, bf16[256,512]{1,0:T(8,128)(2,1)S(1)}, u32[]{:S(2)}, u32[]{:S(2)}) collective-permute-start(bf16[256,512]{1,0:T(8,128)(2,1)S(1)} %pair.1), channel_id=1, source_target_pairs={{0,16},{16,0},{1,17},{17,1},{2,18},{18,2},{3,19},{19,3},{4,20},{20... | collective-permute-start | bytes 786440 | tf_op jit(solution)/shard_map/ppermute | solution.py:409
  66.0 0.7 collective-permute-start.18
  66.6 1.9 %collective-permute-start.16 = (bf16[256,256]{1,0:T(8,128)(2,1)S(1)}, bf16[256,256]{1,0:T(8,128)(2,1)S(1)}, u32[]{:S(2)}, u32[]{:S(2)}) collective-permute-start(bf16[256,256]{1,0:T(8,128)(2,1)S(1)} %get-tuple-element.94), channel_id=1, source_target_pairs={{32,0},{64,32},{96,64},{128,96},{160,128},{192,160},{224,192},{33,... | collective-permute-start | bytes 393224 | tf_op jit(solution)/shard_map/ppermute | solution.py:414
  68.6 1.9 %collective-permute-start.17 = (bf16[256,256]{1,0:T(8,128)(2,1)S(1)}, bf16[256,256]{1,0:T(8,128)(2,1)S(1)}, u32[]{:S(2)}, u32[]{:S(2)}) collective-permute-start(bf16[256,256]{1,0:T(8,128)(2,1)S(1)} %get-tuple-element.95), channel_id=1, source_target_pairs={{64,0},{96,32},{128,64},{160,96},{192,128},{224,160},{65,1},{97,33... | collective-permute-start | bytes 393224 | tf_op jit(solution)/shard_map/ppermute | solution.py:414
  70.5 1.5 %own_gradients.1 = (f32[16,128,256]{2,1,0:T(8,128)S(1)}, bf16[256,512]{1,0:T(8,128)(2,1)S(1)}, f32[256,256]{1,0:T(8,128)S(1)}) custom-call(s32[2]{0:T(128)S(1)} %pad_add_fusion.place_ref, s32[8]{0:T(128)S(1)} %get-tuple-element.52.ranges, f32[16,128,256]{2,1,0:T(8,128)S(1)} %get-tuple-element.83.dqt_in, ...), custom_call_target="tpu_custom_call", output_to_operand_aliasing={{0}: (2, {})} | custom-call | flops 1 | bytes 1 | tf_op jit(solution)/shard_map/own_gradients/pallas_call | solution.py:381
  72.0 0.0 collective-permute-done.18.got5
  72.0 0.0 collective-permute-done.12.beside
  72.1 2.8 %collective-permute-done.16.got1 = bf16[256,256]{1,0:T(8,128)(2,1)S(1)} collective-permute-done((bf16[256,256]{1,0:T(8,128)(2,1)S(1)}, bf16[256,256]{1,0:T(8,128)(2,1)S(1)}, u32[]{:S(2)}, u32[]{:S(2)}) %collective-permute-start.16) | collective-permute-done | bytes 131104 | tf_op jit(solution)/shard_map/ppermute | solution.py:414
  74.9 7.7 %collective-permute-done.17.got2 = bf16[256,256]{1,0:T(8,128)(2,1)S(1)} collective-permute-done((bf16[256,256]{1,0:T(8,128)(2,1)S(1)}, bf16[256,256]{1,0:T(8,128)(2,1)S(1)}, u32[]{:S(2)}, u32[]{:S(2)}) %collective-permute-start.17) | collective-permute-done | bytes 131104 | tf_op jit(solution)/shard_map/ppermute | solution.py:414
  82.6 0.0 collective-permute-done.15.across
  82.6 0.2 merge.1
  82.8 13.5 %all_to_all.5.got = bf16[8,32,768]{2,1,0:T(8,128)(2,1)S(1)} all-to-all(bf16[8,32,768]{2,1,0:T(8,128)(2,1)S(1)} %merge.1), channel_id=1, replica_groups=mesh['z'=8,'y'=2,'core'=2,'tp'=8] {'tp'}, dimensions={0} | all-to-all | bytes 786432 | tf_op jit(solution)/shard_map/all_to_all | solution.py:525
  96.3 0.8 finish.1
Async XLA Ops:
  2.6 13.4 %collective-permute-start = (bf16[256,1024]{1,0:T(8,128)(2,1)}, bf16[256,1024]{1,0:T(8,128)(2,1)S(1)}, u32[]{:S(2)}, u32[]{:S(2)}) collective-permute-start(bf16[256,1024]{1,0:T(8,128)(2,1)} %get-tuple-element.50.qg0), channel_id=1, source_target_pairs={{0,8},{8,0},{1,9},{9,1},{2,10},{10,2},{3,11},{11,3},{4,12},{12,4},... | collective-permute-start | bytes 1572872 | tf_op jit(solution)/shard_map/ppermute | solution.py:409
  2.7 20.6 %collective-permute-start.1 = (bf16[256,1024]{1,0:T(8,128)(2,1)}, bf16[256,1024]{1,0:T(8,128)(2,1)S(1)}, u32[]{:S(2)}, u32[]{:S(2)}) collective-permute-start(bf16[256,1024]{1,0:T(8,128)(2,1)} %get-tuple-element.50.qg0), channel_id=1, source_target_pairs={{0,16},{16,0},{1,17},{17,1},{2,18},{18,2},{3,19},{19,3},{4,20},{20... | collective-permute-start | bytes 1572872 | tf_op jit(solution)/shard_map/ppermute | solution.py:409
  6.0 16.6 %collective-permute-start.5 = (bf16[256,256]{1,0:T(8,128)(2,1)}, bf16[256,256]{1,0:T(8,128)(2,1)S(1)}, u32[]{:S(2)}, u32[]{:S(2)}) collective-permute-start(bf16[256,256]{1,0:T(8,128)(2,1)} %get-tuple-element.51.kv0), channel_id=1, source_target_pairs={{0,64},{32,96},{64,128},{96,160},{128,192},{160,224},{1,65},{33,97... | collective-permute-start | bytes 393224 | tf_op jit(solution)/shard_map/ppermute | solution.py:414
  12.4 10.2 %collective-permute-start.4 = (bf16[256,256]{1,0:T(8,128)(2,1)}, bf16[256,256]{1,0:T(8,128)(2,1)S(1)}, u32[]{:S(2)}, u32[]{:S(2)}) collective-permute-start(bf16[256,256]{1,0:T(8,128)(2,1)} %get-tuple-element.51.kv0), channel_id=1, source_target_pairs={{0,32},{32,64},{64,96},{96,128},{128,160},{160,192},{192,224},{1,3... | collective-permute-start | bytes 393224 | tf_op jit(solution)/shard_map/ppermute | solution.py:414
  15.3 7.3 %collective-permute-start.3 = (bf16[256,256]{1,0:T(8,128)(2,1)}, bf16[256,256]{1,0:T(8,128)(2,1)S(1)}, u32[]{:S(2)}, u32[]{:S(2)}) collective-permute-start(bf16[256,256]{1,0:T(8,128)(2,1)} %get-tuple-element.51.kv0), channel_id=1, source_target_pairs={{24,184},{56,216},{88,248},{25,185},{57,217},{89,249},{26,186},{58... | collective-permute-start | bytes 393224 | tf_op jit(solution)/shard_map/ppermute | solution.py:426
  16.0 7.3 %collective-permute-start.2 = (bf16[256,256]{1,0:T(8,128)(2,1)}, bf16[256,256]{1,0:T(8,128)(2,1)S(1)}, u32[]{:S(2)}, u32[]{:S(2)}) collective-permute-start(bf16[256,256]{1,0:T(8,128)(2,1)} %get-tuple-element.51.kv0), channel_id=1, source_target_pairs={{0,192},{32,224},{64,0},{96,32},{1,193},{33,225},{65,1},{97,33},{2... | collective-permute-start | bytes 393224 | tf_op jit(solution)/shard_map/ppermute | solution.py:418
  17.4 1.0 %copy-start = (bf16[256,1024]{1,0:T(8,128)(2,1)S(1)}, bf16[256,1024]{1,0:T(8,128)(2,1)}, u32[]{:S(2)}) copy-start(bf16[256,1024]{1,0:T(8,128)(2,1)} %get-tuple-element.50.qg0) | copy-start | bytes 1572868
  18.4 0.9 copy-start.1
  19.3 0.7 copy-start.2
  23.3 5.8 %collective-permute-start.6 = (bf16[256,1024]{1,0:T(8,128)(2,1)S(1)}, bf16[256,1024]{1,0:T(8,128)(2,1)S(1)}, u32[]{:S(2)}, u32[]{:S(2)}) collective-permute-start(bf16[256,1024]{1,0:T(8,128)(2,1)S(1)} %collective-permute-done.1.qg2), channel_id=1, source_target_pairs={{0,8},{8,0},{1,9},{9,1},{2,10},{10,2},{3,11},{11,3},{4,12},{12,4},... | collective-permute-start | bytes 1572872 | tf_op jit(solution)/shard_map/ppermute | solution.py:409
  23.3 6.4 %collective-permute-start.8 = (bf16[256,256]{1,0:T(8,128)(2,1)S(1)}, bf16[256,256]{1,0:T(8,128)(2,1)S(1)}, u32[]{:S(2)}, u32[]{:S(2)}) collective-permute-start(bf16[256,256]{1,0:T(8,128)(2,1)S(1)} %collective-permute-done.2), channel_id=1, source_target_pairs={{192,128},{224,160},{0,192},{32,224},{193,129},{225,161},{1,193},{... | collective-permute-start | bytes 393224 | tf_op jit(solution)/shard_map/ppermute | solution.py:418
  23.9 12.4 %collective-permute-start.7 = (bf16[256,256]{1,0:T(8,128)(2,1)S(1)}, bf16[256,256]{1,0:T(8,128)(2,1)S(1)}, u32[]{:S(2)}, u32[]{:S(2)}) collective-permute-start(bf16[256,256]{1,0:T(8,128)(2,1)S(1)} %collective-permute-done.5.kv2), channel_id=1, source_target_pairs={{0,32},{32,64},{64,96},{96,128},{128,160},{160,192},{192,224},{1,3... | collective-permute-start | bytes 393224 | tf_op jit(solution)/shard_map/ppermute | solution.py:414
  37.0 5.7 %collective-permute-start.10 = (f32[3,16,256]{2,1,0:T(8,128)S(1)}, f32[3,16,256]{2,1,0:T(8,128)S(1)}, u32[]{:S(2)}, u32[]{:S(2)}) collective-permute-start(f32[3,16,256]{2,1,0:T(8,128)S(1)} %get-tuple-element.73.st0), channel_id=1, source_target_pairs={{0,16},{16,0},{1,17},{17,1},{2,18},{18,2},{3,19},{19,3},{4,20},{20... | collective-permute-start | bytes 147464 | tf_op jit(solution)/shard_map/ppermute | solution.py:409
  39.5 3.2 %collective-permute-start.9 = (f32[3,16,256]{2,1,0:T(8,128)S(1)}, f32[3,16,256]{2,1,0:T(8,128)S(1)}, u32[]{:S(2)}, u32[]{:S(2)}) collective-permute-start(f32[3,16,256]{2,1,0:T(8,128)S(1)} %get-tuple-element.73.st0), channel_id=1, source_target_pairs={{0,8},{8,0},{1,9},{9,1},{2,10},{10,2},{3,11},{11,3},{4,12},{12,4},... | collective-permute-start | bytes 147464 | tf_op jit(solution)/shard_map/ppermute | solution.py:409
  42.7 1.2 %collective-permute-start.11 = (f32[3,16,256]{2,1,0:T(8,128)S(1)}, f32[3,16,256]{2,1,0:T(8,128)S(1)}, u32[]{:S(2)}, u32[]{:S(2)}) collective-permute-start(f32[3,16,256]{2,1,0:T(8,128)S(1)} %collective-permute-done.10.st2), channel_id=1, source_target_pairs={{0,8},{8,0},{1,9},{9,1},{2,10},{10,2},{3,11},{11,3},{4,12},{12,4},... | collective-permute-start | bytes 147464 | tf_op jit(solution)/shard_map/ppermute | solution.py:409
  45.3 18.8 %collective-permute-start.14 = (bf16[2,256,256]{2,1,0:T(8,128)(2,1)S(1)}, bf16[2,256,256]{2,1,0:T(8,128)(2,1)S(1)}, u32[]{:S(2)}, u32[]{:S(2)}) collective-permute-start(bf16[2,256,256]{2,1,0:T(8,128)(2,1)S(1)} %get-tuple-element.90), channel_id=1, source_target_pairs={{64,0},{96,32},{128,64},{160,96},{192,128},{224,160},{65,1},{97,33... | collective-permute-start | bytes 786440 | tf_op jit(solution)/shard_map/ppermute | solution.py:414
  48.9 15.3 %collective-permute-start.13 = (bf16[256,512]{1,0:T(8,128)(2,1)S(1)}, bf16[256,512]{1,0:T(8,128)(2,1)S(1)}, u32[]{:S(2)}, u32[]{:S(2)}) collective-permute-start(bf16[256,512]{1,0:T(8,128)(2,1)S(1)} %get-tuple-element.88), channel_id=1, source_target_pairs={{0,8},{8,0},{1,9},{9,1},{2,10},{10,2},{3,11},{11,3},{4,12},{12,4},... | collective-permute-start | bytes 786440 | tf_op jit(solution)/shard_map/ppermute | solution.py:409
  51.5 20.5 %collective-permute-start.12 = (bf16[256,512]{1,0:T(8,128)(2,1)S(1)}, bf16[256,512]{1,0:T(8,128)(2,1)S(1)}, u32[]{:S(2)}, u32[]{:S(2)}) collective-permute-start(bf16[256,512]{1,0:T(8,128)(2,1)S(1)} %get-tuple-element.86), channel_id=1, source_target_pairs={{0,8},{8,0},{1,9},{9,1},{2,10},{10,2},{3,11},{11,3},{4,12},{12,4},... | collective-permute-start | bytes 786440 | tf_op jit(solution)/shard_map/ppermute | solution.py:409
  64.2 18.4 %collective-permute-start.15 = (bf16[256,512]{1,0:T(8,128)(2,1)S(1)}, bf16[256,512]{1,0:T(8,128)(2,1)S(1)}, u32[]{:S(2)}, u32[]{:S(2)}) collective-permute-start(bf16[256,512]{1,0:T(8,128)(2,1)S(1)} %pair.1), channel_id=1, source_target_pairs={{0,16},{16,0},{1,17},{17,1},{2,18},{18,2},{3,19},{19,3},{4,20},{20... | collective-permute-start | bytes 786440 | tf_op jit(solution)/shard_map/ppermute | solution.py:409
  66.0 6.1 %collective-permute-start.18 = (bf16[256,256]{1,0:T(8,128)(2,1)S(1)}, bf16[256,256]{1,0:T(8,128)(2,1)S(1)}, u32[]{:S(2)}, u32[]{:S(2)}) collective-permute-start(bf16[256,256]{1,0:T(8,128)(2,1)S(1)} %get-tuple-element.96), channel_id=1, source_target_pairs={{184,24},{216,56},{248,88},{185,25},{217,57},{249,89},{186,26},{21... | collective-permute-start | bytes 393224 | tf_op jit(solution)/shard_map/ppermute | solution.py:426
  66.6 8.3 %collective-permute-start.16 = (bf16[256,256]{1,0:T(8,128)(2,1)S(1)}, bf16[256,256]{1,0:T(8,128)(2,1)S(1)}, u32[]{:S(2)}, u32[]{:S(2)}) collective-permute-start(bf16[256,256]{1,0:T(8,128)(2,1)S(1)} %get-tuple-element.94), channel_id=1, source_target_pairs={{32,0},{64,32},{96,64},{128,96},{160,128},{192,160},{224,192},{33,... | collective-permute-start | bytes 393224 | tf_op jit(solution)/shard_map/ppermute | solution.py:414
  68.6 14.0 %collective-permute-start.17 = (bf16[256,256]{1,0:T(8,128)(2,1)S(1)}, bf16[256,256]{1,0:T(8,128)(2,1)S(1)}, u32[]{:S(2)}, u32[]{:S(2)}) collective-permute-start(bf16[256,256]{1,0:T(8,128)(2,1)S(1)} %get-tuple-element.95), channel_id=1, source_target_pairs={{64,0},{96,32},{128,64},{160,96},{192,128},{224,160},{65,1},{97,33... | collective-permute-start | bytes 393224 | tf_op jit(solution)/shard_map/ppermute | solution.py:414

commit v5 on v4

--- a/solution.py
+++ b/solution.py
@@ -251,32 +251,28 @@
 
 def far_kernel(
     place_ref, ranges, st0, st1, st2, st3, tops, weights, qg_all, kv_all,
-    dqt, dkv34, dkv5, acc0_ref, lse_ref, delta_ref, acc,
+    dqt, dkv34, dkv5, lse_ref, delta_ref, acc,
 ):
     combine_stats((st0, st1, st2, st3), lse_ref, delta_ref)
     dqt[...] = jnp.zeros_like(dqt)
 
     def per_step(step, _):
-        k = jnp.where(step == 0, 0, REACH + 1 - step)
+        k = REACH - step
         acc[...] = jnp.zeros_like(acc)
         visit_step(
-            place_ref[1], k, (jnp.where(step == 0, THERE[0], 0), SLAB), ranges,
+            place_ref[1], k, (0, SLAB), ranges,
             (lse_ref, delta_ref, tops, weights, qg_all, kv_all), dqt, acc,
         )
 
-        @pl.when(step == 0)
-        def _():
-            acc0_ref[...] = acc[...]
-
         for slot, ref in enumerate((dkv5, dkv34.at[1], dkv34.at[0])):
 
-            @pl.when(step == slot + 1)
+            @pl.when(step == slot)
             def _():
                 write_dkv(ref, acc)
 
         return 0
 
-    lax.fori_loop(0, HALF + 1, per_step, 0)
+    lax.fori_loop(0, HALF, per_step, 0)
 
 
 def there_kernel(
@@ -292,31 +288,23 @@
             place_ref[1], k, THERE, ranges,
             (lse_ref, delta_ref, tops, weights, qg_all, kv_all), dqt, acc,
         )
-        acc_ref[k - 1] = acc[...]
+        acc_ref[k] = acc[...]
         return 0
 
-    lax.fori_loop(0, 2, per_step, 0)
+    lax.fori_loop(0, HALF, per_step, 0)
     write_dq(dqt, 2, keep_ref)
     write_dq(dqt, 3, send_ref)
 
 
 def here_kernel(
-    place_ref, ranges, dqt_in, lse_ref, delta_ref, tops, weights, qg_all, kv_all, acc0, acc_near,
+    place_ref, ranges, dqt_in, lse_ref, delta_ref, tops, weights, qg_all, kv_all, acc_near,
     dqt, beside_ref, dkv1, dkv2, acc0_out, acc,
 ):
     del dqt_in
 
     def per_step(step, _):
         k = 2 - step
-
-        @pl.when(k > 0)
-        def _():
-            acc[...] = acc_near[jnp.maximum(k - 1, 0)]
-
-        @pl.when(k == 0)
-        def _():
-            acc[...] = acc0[...]
-
+        acc[...] = acc_near[k]
         visit_step(
             place_ref[1], k, (jnp.where(k == 0, 1, 0), HERE[1]), ranges,
             (lse_ref, delta_ref, tops, weights, qg_all, kv_all), dqt, acc,
@@ -332,7 +320,7 @@
 
         return 0
 
-    lax.fori_loop(0, 3, per_step, 0)
+    lax.fori_loop(0, HALF, per_step, 0)
     acc0_out[...] = acc[...]
     write_dq(dqt, 1, beside_ref)
 
@@ -484,21 +472,21 @@
     stats_yc = flip(stats_y, "core")
 
     data = (tops, weights, qg_all, kv_all)
-    dqt, dkv34, dkv5, acc0, lse, delta = call(
+    dqt, dkv34, dkv5, lse, delta = call(
         far_kernel, "far_gradients",
-        [DQT, ((2,) + DKV[0], BF16), DKV, ACC, ROW_STATS, ROW_STATS], [ACC],
+        [DQT, ((2,) + DKV[0], BF16), DKV, ROW_STATS, ROW_STATS], [ACC],
         place, ranges, stats, stats_c, stats_y, stats_yc, *data,
     )
     got_far = shift(dkv34, -2, slabs)
     got5 = shift_last(dkv5, -5, slabs)
     dqt, there_keep, there_send, acc_near = call(
-        there_kernel, "there_gradients", [DQT, DQ, DQ, ((2,) + ACC[0], F32)], [ACC],
+        there_kernel, "there_gradients", [DQT, DQ, DQ, ((HALF,) + ACC[0], F32)], [ACC],
         place, ranges, dqt, lse, delta, *data, aliases={2: 0},
     )
     there_got = flip(there_send, "core")
     dqt, dq_beside, dkv1, dkv2, acc0 = call(
         here_kernel, "here_gradients", [DQT, DQ, ACC, ACC, ACC], [ACC],
-        place, ranges, dqt, lse, delta, *data, acc0, acc_near, aliases={2: 0},
+        place, ranges, dqt, lse, delta, *data, acc_near, aliases={2: 0},
     )
     dkv1 = (dkv1 + got_far[0].astype(F32)).astype(BF16)
     dkv2 = (dkv2 + got_far[1].astype(F32)).astype(BF16)
@@ -508,8 +496,8 @@
     )
     dq_across = flip(dq_pair, "y")
     dq_beside = flip(dq_beside, "core")
+    got2 = shift(dkv2, -2, slabs)
     got1 = shift(dkv1, -1, slabs)
-    got2 = shift(dkv2, -2, slabs)
     _, dq_keep, dkv0 = call(
         own_kernel, "own_gradients", [DQT, DQ, ACC], [ACC],
         place, ranges, dqt, lse, delta, *data, acc0, aliases={2: 0},

time: 98.7 us -> 98.3 us (level)
  the two profiles are of different devices: /device:TPU:64 before, /device:TPU:96 now
where the time goes in v5:
time: 98.3 us; the launch traced here: 98.6 us
  starting transfers between devices  36.5 us (37%)
  waiting for transfers between devices  30.7 us (31%)
  Pallas kernels  14.5 us (15%)
  blocking collectives  13.1 us (13%)
  local copies, waits for them, and re-layouts  2.6 us (3%)
    ppermute x6, starting transfers between devices, shift(): return lax.ppermute(x, 'z', pairs)  27 us
    ppermute x6, waiting for transfers between devices, shift(): return lax.ppermute(x, 'z', pairs)  24.2 us
    all_to_all x1, blocking collectives, local(): got = lax.all_to_all(whole, 'tp', split_axis=0, concat_axis=0, tiled=True)  13.1 us
    pallas_call x11, Pallas kernels, call(): pl.pallas_call(kernel, out_shape=tuple((jax.ShapeDtypeStruct(shape, dtype...  12.5 us
    ppermute x9, waiting for transfers between devices, flip(): return lax.ppermute(x, axis, [(0, 1), (1, 0)])  6.5 us
    ppermute x9, starting transfers between devices, flip(): return lax.ppermute(x, axis, [(0, 1), (1, 0)])  4.17 us
    ppermute x2, starting transfers between devices, wrapped(): return lax.ppermute(x, 'z', [(i, (i + by) % slabs) for i in sources])  4.03 us
    unnamed x6, local copies, waits for them, and re-layouts  2.6 us
  transfers between devices with their start and end apart: 19, of which 6 were waited for; matrix products, arithmetic and copies ran while one was open for 0% of the time, Pallas kernels for 10%

profile of v5, /device:TPU:96, one launch (start us, length us, event | category | flops | bytes accessed | tf_op | source)
XLA Modules:
  0.0 98.6 jit_solution(3027530868220237666)
XLA Ops:
  0.6 2.0 %pack.1 = (bf16[256,1024]{1,0:T(8,128)(2,1)}, bf16[256,256]{1,0:T(8,128)(2,1)}) custom-call(bf16[256,512]{1,0:T(8,128)(2,1)} %q_ref.1, bf16[256,512]{1,0:T(8,128)(2,1)} %g_ref.1, bf16[256,128]{1,0:T(8,128)(2,1)} %k_ref.1, bf16[256,128]{1,0:T(8,128)(2,1)} %v_ref.1), custom_call_target="tpu_custom_call" | custom-call | flops 1 | bytes 1 | tf_op jit(solution)/shard_map/pack/pallas_call | solution.py:423
  2.6 0.1 collective-permute-start
  2.7 3.3 %collective-permute-start.1 = (bf16[256,1024]{1,0:T(8,128)(2,1)}, bf16[256,1024]{1,0:T(8,128)(2,1)S(1)}, u32[]{:S(2)}, u32[]{:S(2)}) collective-permute-start(bf16[256,1024]{1,0:T(8,128)(2,1)} %get-tuple-element.49.qg0), channel_id=1, source_target_pairs={{0,16},{16,0},{1,17},{17,1},{2,18},{18,2},{3,19},{19,3},{4,20},{20... | collective-permute-start | bytes 1572872 | tf_op jit(solution)/shard_map/ppermute | solution.py:397
  6.0 5.5 %collective-permute-start.5 = (bf16[256,256]{1,0:T(8,128)(2,1)}, bf16[256,256]{1,0:T(8,128)(2,1)S(1)}, u32[]{:S(2)}, u32[]{:S(2)}) collective-permute-start(bf16[256,256]{1,0:T(8,128)(2,1)} %get-tuple-element.50.kv0), channel_id=1, source_target_pairs={{0,64},{32,96},{64,128},{96,160},{128,192},{160,224},{1,65},{33,97... | collective-permute-start | bytes 393224 | tf_op jit(solution)/shard_map/ppermute | solution.py:402
  11.5 2.9 %collective-permute-start.4 = (bf16[256,256]{1,0:T(8,128)(2,1)}, bf16[256,256]{1,0:T(8,128)(2,1)S(1)}, u32[]{:S(2)}, u32[]{:S(2)}) collective-permute-start(bf16[256,256]{1,0:T(8,128)(2,1)} %get-tuple-element.50.kv0), channel_id=1, source_target_pairs={{0,32},{32,64},{64,96},{96,128},{128,160},{160,192},{192,224},{1,3... | collective-permute-start | bytes 393224 | tf_op jit(solution)/shard_map/ppermute | solution.py:402
  14.4 0.7 collective-permute-start.3
  15.1 0.0 collective-permute-done.qg1
  15.1 3.4 %collective-permute-start.2 = (bf16[256,256]{1,0:T(8,128)(2,1)}, bf16[256,256]{1,0:T(8,128)(2,1)S(1)}, u32[]{:S(2)}, u32[]{:S(2)}) collective-permute-start(bf16[256,256]{1,0:T(8,128)(2,1)} %get-tuple-element.50.kv0), channel_id=1, source_target_pairs={{0,192},{32,224},{64,0},{96,32},{1,193},{33,225},{65,1},{97,33},{2... | collective-permute-start | bytes 393224 | tf_op jit(solution)/shard_map/ppermute | solution.py:406
  18.5 0.1 pad_add_fusion.place_ref
  18.6 0.0 copy-start
  18.6 1.0 %copy-done = bf16[256,1024]{1,0:T(8,128)(2,1)S(1)} copy-done((bf16[256,1024]{1,0:T(8,128)(2,1)S(1)}, bf16[256,1024]{1,0:T(8,128)(2,1)}, u32[]{:S(2)}) %copy-start) | copy-done | bytes 524312
  19.6 0.0 copy-start.1
  19.6 0.9 copy-done.1
  20.5 0.0 copy-start.2
  20.5 0.7 copy-done.2
  21.2 2.6 %first_statistics.1 = (s32[8]{0:T(128)S(1)}, s32[8,256]{1,0:T(8,128)S(1)}, f32[3,16,256]{2,1,0:T(8,128)S(1)}, f32[6,16,256]{2,1,0:T(8,128)S(1)}, bf16[24,4,256,2...) custom-call(s32[2]{0:T(128)S(1)} %pad_add_fusion.place_ref, ...), custom_call_target="tpu_custom_call" | custom-call | flops 1 | bytes 1 | tf_op jit(solution)/shard_map/first_statistics/pallas_call | solution.py:369
  23.7 0.0 collective-permute-done.5.kv2
  23.8 0.0 collective-permute-done.4.kv1
  23.8 0.0 collective-permute-done.3.kv5
  23.8 0.0 collective-permute-done.2
  23.8 0.0 collective-permute-done.1.qg2
  23.8 0.1 collective-permute-start.6
  23.9 0.7 collective-permute-start.8
  24.6 2.8 %collective-permute-start.7 = (bf16[256,256]{1,0:T(8,128)(2,1)S(1)}, bf16[256,256]{1,0:T(8,128)(2,1)S(1)}, u32[]{:S(2)}, u32[]{:S(2)}) collective-permute-start(bf16[256,256]{1,0:T(8,128)(2,1)S(1)} %collective-permute-done.5.kv2), channel_id=1, source_target_pairs={{0,32},{32,64},{64,96},{96,128},{128,160},{160,192},{192,224},{1,3... | collective-permute-start | bytes 393224 | tf_op jit(solution)/shard_map/ppermute | solution.py:402
  27.4 0.6 here_statistics.1
  28.0 0.0 collective-permute-done.6.qg3
  28.0 1.3 %there_statistics.1 = (f32[3,16,256]{2,1,0:T(8,128)S(1)}, f32[6,16,256]{2,1,0:T(8,128)S(1)}, bf16[24,4,256,256]{3,2,1,0:T(8,128)(2,1)S(1)}, bf16[4,256,1024]{2,1,0:T(8,128)(2,1)S(1)}) custom-call(s32[2]{0:T(128)S(1)} %pad_add_fusion.place_ref, ...), custom_call_target="tpu_custom_call", output_to_operand_aliasing={{0}: (2, {}), {1}: (3, {}), {2}: (4, {}), {3}: (5, {})} | custom-call | flops 1 | bytes 1 | tf_op jit(solution)/shard_map/there_statistics/pallas_call | solution.py:369
  29.3 0.0 collective-permute-done.8.kv4
  29.3 3.1 %collective-permute-done.7.kv3 = bf16[256,256]{1,0:T(8,128)(2,1)S(1)} collective-permute-done((bf16[256,256]{1,0:T(8,128)(2,1)S(1)}, bf16[256,256]{1,0:T(8,128)(2,1)S(1)}, u32[]{:S(2)}, u32[]{:S(2)}) %collective-permute-start.7) | collective-permute-done | bytes 131104 | tf_op jit(solution)/shard_map/ppermute | solution.py:402
  32.4 0.7 far_statistics.1
  33.0 0.4 collective-permute-start.10
  33.5 0.0 collective-permute-start.9
  33.5 5.3 %collective-permute-done.10.st2 = f32[3,16,256]{2,1,0:T(8,128)S(1)} collective-permute-done((f32[3,16,256]{2,1,0:T(8,128)S(1)}, f32[3,16,256]{2,1,0:T(8,128)S(1)}, u32[]{:S(2)}, u32[]{:S(2)}) %collective-permute-start.10) | collective-permute-done | bytes 49184 | tf_op jit(solution)/shard_map/ppermute | solution.py:397
  38.7 0.0 collective-permute-start.11
  38.7 0.0 collective-permute-done.9.st1
  38.7 1.2 %collective-permute-done.11.st3 = f32[3,16,256]{2,1,0:T(8,128)S(1)} collective-permute-done((f32[3,16,256]{2,1,0:T(8,128)S(1)}, f32[3,16,256]{2,1,0:T(8,128)S(1)}, u32[]{:S(2)}, u32[]{:S(2)}) %collective-permute-start.11) | collective-permute-done | bytes 49184 | tf_op jit(solution)/shard_map/ppermute | solution.py:397
  39.9 1.2 %far_gradients.1 = (f32[16,128,256]{2,1,0:T(8,128)S(1)}, bf16[2,256,256]{2,1,0:T(8,128)(2,1)S(1)}, bf16[256,256]{1,0:T(8,128)(2,1)S(1)}, f32[16,256]{1,0:T(8,128)S(1)}, f32[16,256]{1,0:T(8,128)S(1)}) custom-call(s32[2]{0:T(128)S(1)} %pad_add_fusion.place_ref, s32[8]{0:T(128)S(1)} %get-tuple-element.51.ranges, f32[3,16,256]{2,1,0:T(8,128)S(1)} %get-tuple-element.72.st0, ...), custom_call_target="tpu_custom_call" | custom-call | flops 1 | bytes 1 | tf_op jit(solution)/shard_map/far_gradients/pallas_call | solution.py:369
  41.1 7.2 %collective-permute-start.14 = (bf16[2,256,256]{2,1,0:T(8,128)(2,1)S(1)}, bf16[2,256,256]{2,1,0:T(8,128)(2,1)S(1)}, u32[]{:S(2)}, u32[]{:S(2)}) collective-permute-start(bf16[2,256,256]{2,1,0:T(8,128)(2,1)S(1)} %get-tuple-element.88), channel_id=1, source_target_pairs={{64,0},{96,32},{128,64},{160,96},{192,128},{224,160},{65,1},{97,33... | collective-permute-start | bytes 786440 | tf_op jit(solution)/shard_map/ppermute | solution.py:402
  48.3 1.9 %there_gradients.1 = (f32[16,128,256]{2,1,0:T(8,128)S(1)}, bf16[256,512]{1,0:T(8,128)(2,1)S(1)}, bf16[256,512]{1,0:T(8,128)(2,1)S(1)}, f32[3,256,256]{2,1,0:T(8,128)S(1)}) custom-call(s32[2]{0:T(128)S(1)} %pad_add_fusion.place_ref, s32[8]{0:T(128)S(1)} %get-tuple-element.51.ranges, ...), custom_call_target="tpu_custom_call", output_to_operand_aliasing={{0}: (2, {})} | custom-call | flops 1 | bytes 1 | tf_op jit(solution)/shard_map/there_gradients/pallas_call | solution.py:369
  50.2 0.1 collective-permute-start.13
  50.3 1.8 %here_gradients.1 = (f32[16,128,256]{2,1,0:T(8,128)S(1)}, bf16[256,512]{1,0:T(8,128)(2,1)S(1)}, f32[256,256]{1,0:T(8,128)S(1)}, f32[256,256]{1,0:T(8,128)S(1)}, f32[256,256]{1,0:T(8,128)S(1)}) custom-call(s32[2]{0:T(128)S(1)} %pad_add_fusion.place_ref, s32[8]{0:T(128)S(1)} %get-tuple-element.51.ranges, ...), custom_call_target="tpu_custom_call", output_to_operand_aliasing={{0}: (2, {})} | custom-call | flops 1 | bytes 1 | tf_op jit(solution)/shard_map/here_gradients/pallas_call | solution.py:369
  52.1 0.1 collective-permute-start.12
  52.2 8.7 %collective-permute-done.14 = bf16[2,256,256]{2,1,0:T(8,128)(2,1)S(1)} collective-permute-done((bf16[2,256,256]{2,1,0:T(8,128)(2,1)S(1)}, bf16[2,256,256]{2,1,0:T(8,128)(2,1)S(1)}, u32[]{:S(2)}, u32[]{:S(2)}) %collective-permute-start.14) | collective-permute-done | bytes 262176 | tf_op jit(solution)/shard_map/ppermute | solution.py:402
  60.9 0.1 fusion
  61.0 0.0 collective-permute-done.13.got
  61.0 0.1 pair.1
  61.1 0.1 collective-permute-start.15
  61.2 0.7 collective-permute-start.18
  61.8 6.6 %collective-permute-start.16 = (bf16[256,256]{1,0:T(8,128)(2,1)S(1)}, bf16[256,256]{1,0:T(8,128)(2,1)S(1)}, u32[]{:S(2)}, u32[]{:S(2)}) collective-permute-start(bf16[256,256]{1,0:T(8,128)(2,1)S(1)} %get-tuple-element.92), channel_id=1, source_target_pairs={{32,0},{64,32},{96,64},{128,96},{160,128},{192,160},{224,192},{33,... | collective-permute-start | bytes 393224 | tf_op jit(solution)/shard_map/ppermute | solution.py:402
  68.5 2.0 %collective-permute-start.17 = (bf16[256,256]{1,0:T(8,128)(2,1)S(1)}, bf16[256,256]{1,0:T(8,128)(2,1)S(1)}, u32[]{:S(2)}, u32[]{:S(2)}) collective-permute-start(bf16[256,256]{1,0:T(8,128)(2,1)S(1)} %get-tuple-element.93), channel_id=1, source_target_pairs={{64,0},{96,32},{128,64},{160,96},{192,128},{224,160},{65,1},{97,33... | collective-permute-start | bytes 393224 | tf_op jit(solution)/shard_map/ppermute | solution.py:402
  70.5 1.5 %own_gradients.1 = (f32[16,128,256]{2,1,0:T(8,128)S(1)}, bf16[256,512]{1,0:T(8,128)(2,1)S(1)}, f32[256,256]{1,0:T(8,128)S(1)}) custom-call(s32[2]{0:T(128)S(1)} %pad_add_fusion.place_ref, s32[8]{0:T(128)S(1)} %get-tuple-element.51.ranges, f32[16,128,256]{2,1,0:T(8,128)S(1)} %get-tuple-element.81.dqt_in, ...), custom_call_target="tpu_custom_call", output_to_operand_aliasing={{0}: (2, {})} | custom-call | flops 1 | bytes 1 | tf_op jit(solution)/shard_map/own_gradients/pallas_call | solution.py:369
  72.0 0.0 collective-permute-done.18.got5
  72.0 0.0 collective-permute-done.12.beside
  72.1 6.9 %collective-permute-done.16.got1 = bf16[256,256]{1,0:T(8,128)(2,1)S(1)} collective-permute-done((bf16[256,256]{1,0:T(8,128)(2,1)S(1)}, bf16[256,256]{1,0:T(8,128)(2,1)S(1)}, u32[]{:S(2)}, u32[]{:S(2)}) %collective-permute-start.16) | collective-permute-done | bytes 131104 | tf_op jit(solution)/shard_map/ppermute | solution.py:402
  79.0 5.6 %collective-permute-done.17.got2 = bf16[256,256]{1,0:T(8,128)(2,1)S(1)} collective-permute-done((bf16[256,256]{1,0:T(8,128)(2,1)S(1)}, bf16[256,256]{1,0:T(8,128)(2,1)S(1)}, u32[]{:S(2)}, u32[]{:S(2)}) %collective-permute-start.17) | collective-permute-done | bytes 131104 | tf_op jit(solution)/shard_map/ppermute | solution.py:402
  84.5 0.0 collective-permute-done.15.across
  84.5 0.2 merge.1
  84.7 13.1 %all_to_all.5.got = bf16[8,32,768]{2,1,0:T(8,128)(2,1)S(1)} all-to-all(bf16[8,32,768]{2,1,0:T(8,128)(2,1)S(1)} %merge.1), channel_id=1, replica_groups=mesh['z'=8,'y'=2,'core'=2,'tp'=8] {'tp'}, dimensions={0} | all-to-all | bytes 786432 | tf_op jit(solution)/shard_map/all_to_all | solution.py:513
  97.8 0.8 finish.1
Async XLA Ops:
  2.6 12.5 %collective-permute-start = (bf16[256,1024]{1,0:T(8,128)(2,1)}, bf16[256,1024]{1,0:T(8,128)(2,1)S(1)}, u32[]{:S(2)}, u32[]{:S(2)}) collective-permute-start(bf16[256,1024]{1,0:T(8,128)(2,1)} %get-tuple-element.49.qg0), channel_id=1, source_target_pairs={{0,8},{8,0},{1,9},{9,1},{2,10},{10,2},{3,11},{11,3},{4,12},{12,4},... | collective-permute-start | bytes 1572872 | tf_op jit(solution)/shard_map/ppermute | solution.py:397
  2.7 21.1 %collective-permute-start.1 = (bf16[256,1024]{1,0:T(8,128)(2,1)}, bf16[256,1024]{1,0:T(8,128)(2,1)S(1)}, u32[]{:S(2)}, u32[]{:S(2)}) collective-permute-start(bf16[256,1024]{1,0:T(8,128)(2,1)} %get-tuple-element.49.qg0), channel_id=1, source_target_pairs={{0,16},{16,0},{1,17},{17,1},{2,18},{18,2},{3,19},{19,3},{4,20},{20... | collective-permute-start | bytes 1572872 | tf_op jit(solution)/shard_map/ppermute | solution.py:397
  6.0 17.8 %collective-permute-start.5 = (bf16[256,256]{1,0:T(8,128)(2,1)}, bf16[256,256]{1,0:T(8,128)(2,1)S(1)}, u32[]{:S(2)}, u32[]{:S(2)}) collective-permute-start(bf16[256,256]{1,0:T(8,128)(2,1)} %get-tuple-element.50.kv0), channel_id=1, source_target_pairs={{0,64},{32,96},{64,128},{96,160},{128,192},{160,224},{1,65},{33,97... | collective-permute-start | bytes 393224 | tf_op jit(solution)/shard_map/ppermute | solution.py:402
  11.5 12.3 %collective-permute-start.4 = (bf16[256,256]{1,0:T(8,128)(2,1)}, bf16[256,256]{1,0:T(8,128)(2,1)S(1)}, u32[]{:S(2)}, u32[]{:S(2)}) collective-permute-start(bf16[256,256]{1,0:T(8,128)(2,1)} %get-tuple-element.50.kv0), channel_id=1, source_target_pairs={{0,32},{32,64},{64,96},{96,128},{128,160},{160,192},{192,224},{1,3... | collective-permute-start | bytes 393224 | tf_op jit(solution)/shard_map/ppermute | solution.py:402
  14.4 9.4 %collective-permute-start.3 = (bf16[256,256]{1,0:T(8,128)(2,1)}, bf16[256,256]{1,0:T(8,128)(2,1)S(1)}, u32[]{:S(2)}, u32[]{:S(2)}) collective-permute-start(bf16[256,256]{1,0:T(8,128)(2,1)} %get-tuple-element.50.kv0), channel_id=1, source_target_pairs={{24,184},{56,216},{88,248},{25,185},{57,217},{89,249},{26,186},{58... | collective-permute-start | bytes 393224 | tf_op jit(solution)/shard_map/ppermute | solution.py:414
  15.1 8.7 %collective-permute-start.2 = (bf16[256,256]{1,0:T(8,128)(2,1)}, bf16[256,256]{1,0:T(8,128)(2,1)S(1)}, u32[]{:S(2)}, u32[]{:S(2)}) collective-permute-start(bf16[256,256]{1,0:T(8,128)(2,1)} %get-tuple-element.50.kv0), channel_id=1, source_target_pairs={{0,192},{32,224},{64,0},{96,32},{1,193},{33,225},{65,1},{97,33},{2... | collective-permute-start | bytes 393224 | tf_op jit(solution)/shard_map/ppermute | solution.py:406
  18.6 1.0 %copy-start = (bf16[256,1024]{1,0:T(8,128)(2,1)S(1)}, bf16[256,1024]{1,0:T(8,128)(2,1)}, u32[]{:S(2)}) copy-start(bf16[256,1024]{1,0:T(8,128)(2,1)} %get-tuple-element.49.qg0) | copy-start | bytes 1572868
  19.6 0.9 copy-start.1
  20.5 0.7 copy-start.2
  23.8 4.2 %collective-permute-start.6 = (bf16[256,1024]{1,0:T(8,128)(2,1)S(1)}, bf16[256,1024]{1,0:T(8,128)(2,1)S(1)}, u32[]{:S(2)}, u32[]{:S(2)}) collective-permute-start(bf16[256,1024]{1,0:T(8,128)(2,1)S(1)} %collective-permute-done.1.qg2), channel_id=1, source_target_pairs={{0,8},{8,0},{1,9},{9,1},{2,10},{10,2},{3,11},{11,3},{4,12},{12,4},... | collective-permute-start | bytes 1572872 | tf_op jit(solution)/shard_map/ppermute | solution.py:397
  23.9 5.4 %collective-permute-start.8 = (bf16[256,256]{1,0:T(8,128)(2,1)S(1)}, bf16[256,256]{1,0:T(8,128)(2,1)S(1)}, u32[]{:S(2)}, u32[]{:S(2)}) collective-permute-start(bf16[256,256]{1,0:T(8,128)(2,1)S(1)} %collective-permute-done.2), channel_id=1, source_target_pairs={{192,128},{224,160},{0,192},{32,224},{193,129},{225,161},{1,193},{... | collective-permute-start | bytes 393224 | tf_op jit(solution)/shard_map/ppermute | solution.py:406
  24.6 7.8 %collective-permute-start.7 = (bf16[256,256]{1,0:T(8,128)(2,1)S(1)}, bf16[256,256]{1,0:T(8,128)(2,1)S(1)}, u32[]{:S(2)}, u32[]{:S(2)}) collective-permute-start(bf16[256,256]{1,0:T(8,128)(2,1)S(1)} %collective-permute-done.5.kv2), channel_id=1, source_target_pairs={{0,32},{32,64},{64,96},{96,128},{128,160},{160,192},{192,224},{1,3... | collective-permute-start | bytes 393224 | tf_op jit(solution)/shard_map/ppermute | solution.py:402
  33.0 5.7 %collective-permute-start.10 = (f32[3,16,256]{2,1,0:T(8,128)S(1)}, f32[3,16,256]{2,1,0:T(8,128)S(1)}, u32[]{:S(2)}, u32[]{:S(2)}) collective-permute-start(f32[3,16,256]{2,1,0:T(8,128)S(1)} %get-tuple-element.72.st0), channel_id=1, source_target_pairs={{0,16},{16,0},{1,17},{17,1},{2,18},{18,2},{3,19},{19,3},{4,20},{20... | collective-permute-start | bytes 147464 | tf_op jit(solution)/shard_map/ppermute | solution.py:397
  33.5 5.3 %collective-permute-start.9 = (f32[3,16,256]{2,1,0:T(8,128)S(1)}, f32[3,16,256]{2,1,0:T(8,128)S(1)}, u32[]{:S(2)}, u32[]{:S(2)}) collective-permute-start(f32[3,16,256]{2,1,0:T(8,128)S(1)} %get-tuple-element.72.st0), channel_id=1, source_target_pairs={{0,8},{8,0},{1,9},{9,1},{2,10},{10,2},{3,11},{11,3},{4,12},{12,4},... | collective-permute-start | bytes 147464 | tf_op jit(solution)/shard_map/ppermute | solution.py:397
  38.7 1.2 %collective-permute-start.11 = (f32[3,16,256]{2,1,0:T(8,128)S(1)}, f32[3,16,256]{2,1,0:T(8,128)S(1)}, u32[]{:S(2)}, u32[]{:S(2)}) collective-permute-start(f32[3,16,256]{2,1,0:T(8,128)S(1)} %collective-permute-done.10.st2), channel_id=1, source_target_pairs={{0,8},{8,0},{1,9},{9,1},{2,10},{10,2},{3,11},{11,3},{4,12},{12,4},... | collective-permute-start | bytes 147464 | tf_op jit(solution)/shard_map/ppermute | solution.py:397
  41.1 19.8 %collective-permute-start.14 = (bf16[2,256,256]{2,1,0:T(8,128)(2,1)S(1)}, bf16[2,256,256]{2,1,0:T(8,128)(2,1)S(1)}, u32[]{:S(2)}, u32[]{:S(2)}) collective-permute-start(bf16[2,256,256]{2,1,0:T(8,128)(2,1)S(1)} %get-tuple-element.88), channel_id=1, source_target_pairs={{64,0},{96,32},{128,64},{160,96},{192,128},{224,160},{65,1},{97,33... | collective-permute-start | bytes 786440 | tf_op jit(solution)/shard_map/ppermute | solution.py:402
  50.2 10.8 %collective-permute-start.13 = (bf16[256,512]{1,0:T(8,128)(2,1)S(1)}, bf16[256,512]{1,0:T(8,128)(2,1)S(1)}, u32[]{:S(2)}, u32[]{:S(2)}) collective-permute-start(bf16[256,512]{1,0:T(8,128)(2,1)S(1)} %get-tuple-element.86), channel_id=1, source_target_pairs={{0,8},{8,0},{1,9},{9,1},{2,10},{10,2},{3,11},{11,3},{4,12},{12,4},... | collective-permute-start | bytes 786440 | tf_op jit(solution)/shard_map/ppermute | solution.py:397
  52.1 19.9 %collective-permute-start.12 = (bf16[256,512]{1,0:T(8,128)(2,1)S(1)}, bf16[256,512]{1,0:T(8,128)(2,1)S(1)}, u32[]{:S(2)}, u32[]{:S(2)}) collective-permute-start(bf16[256,512]{1,0:T(8,128)(2,1)S(1)} %get-tuple-element.84), channel_id=1, source_target_pairs={{0,8},{8,0},{1,9},{9,1},{2,10},{10,2},{3,11},{11,3},{4,12},{12,4},... | collective-permute-start | bytes 786440 | tf_op jit(solution)/shard_map/ppermute | solution.py:397
  61.1 23.5 %collective-permute-start.15 = (bf16[256,512]{1,0:T(8,128)(2,1)S(1)}, bf16[256,512]{1,0:T(8,128)(2,1)S(1)}, u32[]{:S(2)}, u32[]{:S(2)}) collective-permute-start(bf16[256,512]{1,0:T(8,128)(2,1)S(1)} %pair.1), channel_id=1, source_target_pairs={{0,16},{16,0},{1,17},{17,1},{2,18},{18,2},{3,19},{19,3},{4,20},{20... | collective-permute-start | bytes 786440 | tf_op jit(solution)/shard_map/ppermute | solution.py:397
  61.2 10.9 %collective-permute-start.18 = (bf16[256,256]{1,0:T(8,128)(2,1)S(1)}, bf16[256,256]{1,0:T(8,128)(2,1)S(1)}, u32[]{:S(2)}, u32[]{:S(2)}) collective-permute-start(bf16[256,256]{1,0:T(8,128)(2,1)S(1)} %get-tuple-element.94), channel_id=1, source_target_pairs={{184,24},{216,56},{248,88},{185,25},{217,57},{249,89},{186,26},{21... | collective-permute-start | bytes 393224 | tf_op jit(solution)/shard_map/ppermute | solution.py:414
  61.8 17.1 %collective-permute-start.16 = (bf16[256,256]{1,0:T(8,128)(2,1)S(1)}, bf16[256,256]{1,0:T(8,128)(2,1)S(1)}, u32[]{:S(2)}, u32[]{:S(2)}) collective-permute-start(bf16[256,256]{1,0:T(8,128)(2,1)S(1)} %get-tuple-element.92), channel_id=1, source_target_pairs={{32,0},{64,32},{96,64},{128,96},{160,128},{192,160},{224,192},{33,... | collective-permute-start | bytes 393224 | tf_op jit(solution)/shard_map/ppermute | solution.py:402
  68.5 16.1 %collective-permute-start.17 = (bf16[256,256]{1,0:T(8,128)(2,1)S(1)}, bf16[256,256]{1,0:T(8,128)(2,1)S(1)}, u32[]{:S(2)}, u32[]{:S(2)}) collective-permute-start(bf16[256,256]{1,0:T(8,128)(2,1)S(1)} %get-tuple-element.93), channel_id=1, source_target_pairs={{64,0},{96,32},{128,64},{160,96},{192,128},{224,160},{65,1},{97,33... | collective-permute-start | bytes 393224 | tf_op jit(solution)/shard_map/ppermute | solution.py:402
